TPU v7x, 32 devices: a whole 2x2x4 slice. The times are simulated.
32 devices in a mesh: parts: 2 (over x), seq: 8 (over z, y), dp: 2 (over core).
Axes of the slice: x: 2, y: 2, z: 4, core: 2. Of those that a mesh axis runs over, the one named last changes fastest.
Arguments:
- queries: bfloat16 [4, 2048, 1024], P(('parts', 'dp'), 'seq'), parts along dimension 0, may hold values from -8 to 8
- key_states: bfloat16 [4, 2048, 1024], P(('parts', 'dp'), 'seq'), parts along dimension 0, may hold values from -8 to 8
- value_states: bfloat16 [4, 2048, 1024], P(('parts', 'dp'), 'seq'), parts along dimension 0, may hold values from -6 to 6
- out_grad: bfloat16 [4, 2048, 1024], P(('parts', 'dp'), 'seq'), parts along dimension 0, may hold values from -1.5 to 1.5
- layer_input: bfloat16 [4, 2048, 2048], P(('parts', 'dp'), 'seq'), parts along dimension 0, may hold values from -6 to 6
Outputs:
- weight_grad: float32 [4096, 1024], P(('parts', 'seq', 'dp')), parts along dimension 0
There are 2 independent parts, one for each index of `parts`. A program takes and returns all parts, laid end to end along the dimension named above; each array names one. Nothing has to cross between parts.
All inputs are finite; a program needn't handle non-finite values.
Results may differ from a plain program's by a relative error of at most 0.0041.
Values may be sent and summed in bfloat16 or wider, within the bound.
No kernel may reach another device: no remote copies, remote signals or barrier semaphores. Data moves between devices by JAX's collectives and lax.ppermute only.
A program may use at most 192 MiB of HBM per device.

v0:
```python
import functools
import math

import jax
import jax.numpy as jnp
from jax import lax
from jax.experimental import pallas as pl
from jax.experimental.pallas import tpu as pltpu
from jax.sharding import PartitionSpec as P

HEADS = 8
HEAD_DIM = 128
HALF = 1024
NEG = -1e30
CHUNK = 2
NT = (((1,), (1,)), ((), ()))


def exchange(value, axis, distance):
    count = lax.axis_size(axis)
    return lax.ppermute(value, axis, [(source, source ^ distance) for source in range(count)])


def fold_rows(value, op):
    rows = value.shape[0]
    total = value[0:8]
    for start in range(8, rows, 8):
        total = op(total, value[start : start + 8])
    return total


def columns(array, block):
    return array[:, pl.ds(pl.multiple_of(block * HEAD_DIM, HEAD_DIM), HEAD_DIM)]


def split_kernel(distances, place, left, right, *outs):
    for distance, out in zip(distances, outs):
        for index, array in enumerate((left, right)):
            out[index] = columns(array, place[0] ^ distance)


def split_heads(place, left, right, distances):
    vmem = pl.BlockSpec(memory_space=pltpu.VMEM)
    tok = left.shape[0]
    shape = jax.ShapeDtypeStruct((2, tok, HEAD_DIM), left.dtype)
    pieces = pl.pallas_call(
        functools.partial(split_kernel, distances),
        out_shape=[shape] * len(distances),
        in_specs=[pl.BlockSpec(memory_space=pltpu.SMEM), vmem, vmem],
        out_specs=[vmem] * len(distances),
        compiler_params=pltpu.CompilerParams(vmem_limit_bytes=4 * 2**20),
        name="split_heads",
    )(place, left, right)
    return dict(zip(distances, pieces))


def core_kernel(place, inputs, out):
    for device in range(HEADS):
        out[device] = columns(inputs, 2 * device + 1 - place[2])


def neighbour_kernel(place, inputs, other, out):
    count = HEADS // 2
    for column in range(count):
        device = 2 * column + 1 - place[0] % 2
        out[column] = columns(inputs, 2 * device + place[2])
        out[count + column] = other[device]


def turned_kernel(place, inputs, other, received, out):
    count = HEADS // 2
    tok = inputs.shape[0]
    parity, core = place[0] % 2, place[2]

    def put(distance, document, side, block):
        start = pl.multiple_of((2 * document + side) * tok, tok)
        out[distance, :, pl.ds(start, tok)] = block.T

    for distance in range(count):
        column = (place[0] // 2) ^ distance
        device = 2 * column + parity
        put(distance, core, parity, columns(inputs, 2 * device + core))
        put(distance, 1 - core, parity, other[device])
        put(distance, core, 1 - parity, received[column])
        put(distance, 1 - core, 1 - parity, received[count + column])


def moved(kernel, shape, dtype, *operands):
    vmem = pl.BlockSpec(memory_space=pltpu.VMEM)
    return pl.pallas_call(
        kernel,
        out_shape=jax.ShapeDtypeStruct(shape, dtype),
        in_specs=[pl.BlockSpec(memory_space=pltpu.SMEM)] + [vmem] * (len(operands) - 1),
        out_specs=vmem,
        compiler_params=pltpu.CompilerParams(vmem_limit_bytes=6 * 2**20),
        name="moved",
    )(*operands)


def head_block(dims, place, b, query, grad, key_ref, value_ref, score_ref, dprob_ref, total_ref):
    tok, halo, groups = dims
    shift = halo // tok
    reach = HALF // tok
    scale = math.log2(math.e) / math.sqrt(HEAD_DIM)
    ahead = lax.broadcasted_iota(jnp.int32, (tok, tok), 0)
    ahead = ahead - lax.broadcasted_iota(jnp.int32, (tok, tok), 1)
    first, count = (b + shift - reach, 2 * reach + 1) if halo else (0, HEADS)
    chunks = [range(start, min(start + CHUNK, count)) for start in range(0, count, CHUNK)]

    def rows_of(chunk):
        start = (first + chunk[0]) * tok
        return pl.ds(pl.multiple_of(start, tok) if halo else start, len(chunk) * tok)

    def held(at):
        return slice(at * tok, (at + 1) * tok)

    top = None
    for chunk in chunks:
        scores = lax.dot_general(
            key_ref[rows_of(chunk)], query, NT, preferred_element_type=jnp.float32
        )
        for at in chunk:
            score = scores[held(at - chunk[0])]
            distance = first + at - shift - b
            if at == 0 if halo else at < HEADS - reach:
                score = jnp.where(ahead >= -HALF - distance * tok, score, NEG)
            if at == 2 * reach if halo else at >= reach:
                score = jnp.where(ahead <= HALF - distance * tok, score, NEG)
            if halo:
                inside = (first + at >= shift) | (place[1] > 0)
                inside &= (first + at < shift + HEADS) | (place[1] < groups - 1)
                score = jnp.where(inside, score, NEG)
            score_ref[held(at)] = score
            part = fold_rows(score, jnp.maximum)
            top = part if top is None else jnp.maximum(top, part)
    top = jnp.max(top, axis=0, keepdims=True) * scale
    weight_sum = jnp.zeros((8, tok), jnp.float32)
    delta_sum = jnp.zeros((8, tok), jnp.float32)
    for chunk in chunks:
        dprobs = lax.dot_general(
            value_ref[rows_of(chunk)], grad, NT, preferred_element_type=jnp.float32
        )
        for at in chunk:
            dprob = dprobs[held(at - chunk[0])]
            weight = jnp.exp2(score_ref[held(at)] * scale - top)
            score_ref[held(at)] = weight
            dprob_ref[held(at)] = dprob
            weight_sum = weight_sum + fold_rows(weight, jnp.add)
            delta_sum = delta_sum + fold_rows(weight * dprob, jnp.add)
    inverse = 1.0 / jnp.sum(weight_sum, axis=0, keepdims=True)
    delta = jnp.sum(delta_sum, axis=0, keepdims=True) * inverse
    for chunk in chunks:
        held_rows = slice(chunk[0] * tok, (chunk[-1] + 1) * tok)
        prob = score_ref[held_rows] * inverse
        dscore = prob * (dprob_ref[held_rows] - delta)
        total_ref[rows_of(chunk)] += jnp.dot(
            dscore.astype(jnp.bfloat16), query, preferred_element_type=jnp.float32
        )


def query_blocks(dims, place, distances, sources, refs):
    tok = dims[0]
    me = place[0]
    key_ref, value_ref, query_ref, grad_ref, score_ref, dprob_ref, total_ref, sem = refs
    copies = []
    for slot, source in enumerate(sources):
        rows = slice(slot * tok, (slot + 1) * tok)
        for target, piece in zip((query_ref, grad_ref), source):
            copies.append(pltpu.make_async_copy(piece, target.at[rows], sem))
    for copy in copies:
        copy.start()
    yield
    for copy in copies:
        copy.wait()

    def block(slot, distance):
        rows = pl.ds(pl.multiple_of(slot * tok, tok), tok)
        head_block(
            dims, place, me ^ distance, query_ref[rows], grad_ref[rows], key_ref, value_ref,
            score_ref, dprob_ref, total_ref,
        )

    @pl.loop(0, 2 * len(distances))
    def _(slot):
        block(slot, 2 * distances[0] + slot)

    yield


def first_kernel(dims, distances, place, *refs):
    tok, halo, _ = dims
    me = place[0]
    query, key, value, grad = refs[:4]
    key_values, refs = refs[4 : 3 + HEADS], refs[3 + HEADS :]
    count = 2 * len(distances) - 1
    others, refs = refs[:count], refs[count:]
    if halo:
        halves, refs = refs[:2], refs[2:]
    total_ref, key_ref, value_ref, query_ref, grad_ref, score_ref, dprob_ref, sem = refs
    mine = pl.ds(pl.multiple_of(me * HEAD_DIM, HEAD_DIM), HEAD_DIM)
    copies = []
    for distance in range(HEADS):
        rows = pl.ds(pl.multiple_of((me ^ distance) * tok + halo, tok), tok)
        pair = (key, value)
        if distance:
            pair = [key_values[distance - 1].at[index] for index in range(2)]
        else:
            pair = (key.at[:, mine], value.at[:, mine])
        for source, target in zip(pair, (key_ref, value_ref)):
            copies.append(pltpu.make_async_copy(source, target.at[rows], sem))
    if halo:
        for side, start in ((0, 0), (1, halo + HEADS * tok)):
            for index, target in enumerate((key_ref, value_ref)):
                copies.append(
                    pltpu.make_async_copy(
                        halves[side].at[index], target.at[pl.ds(start, halo)], sem
                    )
                )
    for copy in copies:
        copy.start()
    sources = [(query.at[:, mine], grad.at[:, mine])]
    sources += [(other.at[0], other.at[1]) for other in others]
    steps = query_blocks(
        dims, place, distances, sources,
        (key_ref, value_ref, query_ref, grad_ref, score_ref, dprob_ref, total_ref, sem),
    )
    next(steps)
    total_ref[...] = jnp.zeros_like(total_ref)
    for copy in copies:
        copy.wait()
    next(steps)


def later_kernel(dims, distances, last, place, before_ref, key_ref, value_ref, *refs):
    tok, halo, _ = dims
    count = 2 * len(distances)
    others, refs = refs[:count], refs[count:]
    split = last and not halo
    if split:
        outs, refs = refs[: HEADS // 2], refs[HEADS // 2 :]
        total_ref, refs = refs[0], refs[1:]
    else:
        total_ref, refs = refs[0], refs[1:]
    sources = [(other.at[0], other.at[1]) for other in others]
    query_ref, grad_ref, score_ref, dprob_ref, sem = refs
    steps = query_blocks(
        dims, place, distances, sources,
        (key_ref, value_ref, query_ref, grad_ref, score_ref, dprob_ref, total_ref, sem),
    )
    next(steps)
    total_ref[...] = before_ref[...]
    next(steps)
    inverse_root = 1.0 / math.sqrt(HEAD_DIM)
    if split:
        pair = 2 * tok
        for distance, out in enumerate(outs):
            start = pl.multiple_of(((place[0] // 2) ^ distance) * pair, pair)
            out[...] = (total_ref[pl.ds(start, pair)] * inverse_root).astype(jnp.bfloat16)
    elif last:
        total_ref[...] = total_ref[...] * inverse_root


def head_grads(place, arrays, key_values, query_grads, halves, groups):
    tok = arrays[0].shape[0]
    halo = HALF if halves else 0
    dims = (tok, halo, groups)
    span = HEADS * tok + 2 * halo
    window = min(span, tok + 2 * HALF)
    any_spec = pl.BlockSpec(memory_space=pltpu.HBM)
    vmem = pl.BlockSpec(memory_space=pltpu.VMEM)
    smem = pl.BlockSpec(memory_space=pltpu.SMEM)
    total = jax.ShapeDtypeStruct((span, HEAD_DIM), jnp.float32)
    low = jax.ShapeDtypeStruct((span, HEAD_DIM), jnp.bfloat16)
    piece = jax.ShapeDtypeStruct((2 * tok, HEAD_DIM), jnp.bfloat16)
    params = pltpu.CompilerParams(vmem_limit_bytes=(14 if halo else 10) * 2**20)

    def scratch(pairs):
        return [
            pltpu.VMEM((2 * pairs * tok, HEAD_DIM), jnp.bfloat16),
            pltpu.VMEM((2 * pairs * tok, HEAD_DIM), jnp.bfloat16),
            pltpu.VMEM((window, tok), jnp.float32),
            pltpu.VMEM((window, tok), jnp.float32),
        ]

    def cost(pairs):
        return pl.CostEstimate(
            flops=100 * pairs * tok * window * HEAD_DIM,
            bytes_accessed=8 * span * HEAD_DIM,
            transcendentals=2 * pairs * tok * window,
        )

    sem = [pltpu.SemaphoreType.DMA]
    state = pl.pallas_call(
        functools.partial(first_kernel, dims, (0, 1)),
        out_shape=[total, low, low],
        in_specs=[smem] + [any_spec] * (4 + HEADS - 1 + 3 + len(halves)),
        out_specs=[vmem] * 3,
        scratch_shapes=scratch(2) + sem,
        compiler_params=params,
        cost_estimate=cost(2),
        name="head_first",
    )(place, *arrays, *key_values, *query_grads[:3], *halves)
    for distance in (2, 3):
        last = distance == 3
        split = last and not halo
        others = query_grads[2 * distance - 1 : 2 * distance + 1]
        out = pl.pallas_call(
            functools.partial(later_kernel, dims, (distance,), last),
            out_shape=[piece] * (HEADS // 2) if split else [total],
            in_specs=[smem] + [vmem] * 3 + [any_spec] * 2,
            out_specs=[vmem] * (HEADS // 2 if split else 1),
            scratch_shapes=([pltpu.VMEM(total.shape, total.dtype)] if split else [])
            + scratch(1)
            + sem,
            compiler_params=params,
            cost_estimate=cost(1),
            name="head_later",
        )(place, *state, *others)
        state = [out[0], *state[1:]]
    return out if split else out[0]


def weight_kernel(place, input_ref, *refs):
    count = HEADS // 2
    own, other = refs[0:count], refs[count : 2 * count]
    near_ref, grad_ref = refs[-2:]
    out_refs = refs[2 * count : -2]
    column = place[0] // 2
    core = place[2]
    tokens = own[0].shape[0]
    for distance in range(count):
        start = pl.multiple_of((column ^ distance) * HEAD_DIM, HEAD_DIM)
        at = pl.multiple_of(core * tokens, tokens)
        grad_ref[pl.ds(at, tokens), pl.ds(start, HEAD_DIM)] = own[distance][...]
        at = pl.multiple_of((1 - core) * tokens, tokens)
        grad_ref[pl.ds(at, tokens), pl.ds(start, HEAD_DIM)] = other[distance][...]
    for target in range(input_ref.shape[0]):
        product = jnp.dot(
            input_ref[target], grad_ref[...], preferred_element_type=jnp.float32
        )
        out_refs[target][...] = product.astype(out_refs[target].dtype)
        if target == 0:
            near_ref[...] = product


def weight_parts(place, inputs, own, other, dtype):
    targets, share, depth = inputs.shape
    width = len(own) * HEAD_DIM
    vmem = pl.BlockSpec(memory_space=pltpu.VMEM)
    return pl.pallas_call(
        weight_kernel,
        out_shape=[jax.ShapeDtypeStruct((share, width), dtype)] * targets
        + [jax.ShapeDtypeStruct((share, width), jnp.float32)],
        in_specs=[pl.BlockSpec(memory_space=pltpu.SMEM)] + [vmem] * (1 + len(own) + len(other)),
        out_specs=[vmem] * (targets + 1),
        scratch_shapes=[pltpu.VMEM((depth, width), jnp.bfloat16)],
        compiler_params=pltpu.CompilerParams(vmem_limit_bytes=8 * 2**20),
        cost_estimate=pl.CostEstimate(
            flops=2 * targets * share * depth * width,
            bytes_accessed=2 * depth * (width + targets * share),
            transcendentals=0,
        ),
        name="weight_parts",
    )(place, inputs, *own, *other)


def sum_kernel(place, *refs):
    out_ref = refs[-1]
    count = HEADS // 2
    for side in range(2):
        total = refs[side * count][...]
        for index in range(1, count):
            total = total + refs[side * count + index][...].astype(jnp.float32)
        parity = (place[0] % 2) ^ side
        for column in range(count):
            start = pl.multiple_of((2 * column + parity) * HEAD_DIM, HEAD_DIM)
            out_ref[:, pl.ds(start, HEAD_DIM)] = total[
                :, column * HEAD_DIM : (column + 1) * HEAD_DIM
            ]


def summed(place, near, far):
    share, width = near[0].shape
    vmem = pl.BlockSpec(memory_space=pltpu.VMEM)
    return pl.pallas_call(
        sum_kernel,
        out_shape=jax.ShapeDtypeStruct((share, 2 * width), jnp.float32),
        in_specs=[pl.BlockSpec(memory_space=pltpu.SMEM)] + [vmem] * (len(near) + len(far)),
        out_specs=vmem,
        compiler_params=pltpu.CompilerParams(vmem_limit_bytes=4 * 2**20),
        name="summed",
    )(place, *near, *far)


def ordered(first, own, other, axis):
    return jnp.where(first == 0, jnp.stack([own, other], axis), jnp.stack([other, own], axis))


def gathered_inputs(layer_input, me, parity, core, groups):
    tok, width = layer_input.shape
    columns = lax.axis_size("seq") // 2
    share = width // (columns * 4)
    shaped = layer_input.reshape(tok, columns, 2, 2, share)
    keep = lax.dynamic_index_in_dim(shaped, parity, 2, keepdims=False)
    give = lax.dynamic_index_in_dim(shaped, 1 - parity, 2, keepdims=False)
    both = ordered(parity, keep, exchange(give, "seq", 1), 0)
    both = both.reshape(2 * tok, columns, 2, share)
    keep = lax.dynamic_index_in_dim(both, core, 2, keepdims=False)
    give = lax.dynamic_index_in_dim(both, 1 - core, 2, keepdims=False)
    full = ordered(core, keep, exchange(give, "dp", 1), 0)
    full = full.reshape(4 * tok, columns, share).transpose(1, 2, 0)
    if groups == 1:
        here = me // 2
        full = jnp.stack(
            [
                lax.dynamic_index_in_dim(full, here ^ distance, 0, keepdims=False)
                for distance in range(columns)
            ]
        )
    return full


def after(*values):
    return lax.optimization_barrier(values)


def local(queries, key_states, value_states, out_grad, layer_input):
    seq_count = lax.axis_size("seq")
    groups = seq_count // HEADS
    tok = queries.shape[1]
    index = lax.axis_index("seq")
    core = lax.axis_index("dp")
    me = index % HEADS
    group = index // HEADS
    parity = index % 2
    place = jnp.stack([me, group, core]).astype(jnp.int32)
    arrays = [array[0] for array in (queries, key_states, value_states, out_grad)]

    def sent(pieces, distances):
        return {d: exchange(pieces[d], "seq", d) for d in distances}

    keys, values = arrays[1:3]
    source = layer_input[0]
    width = source.shape[1]
    every = (6, 7, 4, 5, 2, 3, 1)
    direct = groups == 1 and width == HEADS * 2 * HEAD_DIM
    if direct:
        pieces = split_heads(place, keys, values, every)
        key_values = sent(pieces, (6, 7, 1, 2, 3))
        for first, second in ((6, 4), (7, 5)):
            key_values[first], pieces[second] = after(key_values[first], pieces[second])
        key_values |= sent(pieces, (4, 5))
        key_values[1], source = after(key_values[1], source)
        block = (HEADS, tok, HEAD_DIM)
        other = exchange(moved(core_kernel, block, source.dtype, place, source), "dp", 1)
        near_piece = moved(neighbour_kernel, block, source.dtype, place, source, other)
        received = exchange(near_piece, "seq", 1)
        shape = (HEADS // 2, HEAD_DIM, 4 * tok)
        inputs = moved(turned_kernel, shape, source.dtype, place, source, other, received)
    else:
        key_values = sent(split_heads(place, keys, values, every), every)
        inputs = gathered_inputs(source, me, parity, core, groups)
    pieces = split_heads(place, arrays[0], arrays[3], every)
    for first, second in ((1, 1), (2, 2), (3, 3), (4, 4), (5, 5), (5, 6)):
        key_values[first], pieces[second] = after(key_values[first], pieces[second])
    query_grads = sent(pieces, (1, 2, 3, 4, 5, 6))
    query_grads[4], pieces[7] = after(query_grads[4], pieces[7])
    query_grads[7] = exchange(pieces[7], "seq", 7)
    key_values = [key_values[d] for d in range(1, HEADS)]
    query_grads = [query_grads[d] for d in range(1, HEADS)]
    halves = []
    if groups > 1:
        mine = [lax.dynamic_slice_in_dim(a, me * HEAD_DIM, HEAD_DIM, 1) for a in arrays[1:3]]
        by_distance = jnp.stack([jnp.stack(mine), *key_values])
        rows = jnp.stack(
            [
                lax.dynamic_index_in_dim(by_distance, me ^ block, 0, keepdims=False)
                for block in range(HEADS)
            ]
        )
        rows = rows.transpose(1, 0, 2, 3).reshape(2, HEADS * tok, HEAD_DIM)
        ahead = [(source, source + HEADS) for source in range(seq_count - HEADS)]
        back = [(source + HEADS, source) for source in range(seq_count - HEADS)]
        halves = [
            lax.ppermute(rows[:, -HALF:], "seq", ahead),
            lax.ppermute(rows[:, :HALF], "seq", back),
        ]
    grads = head_grads(place, arrays, key_values, query_grads, halves, groups)
    if groups > 1:
        from_after = lax.ppermute(grads[:HALF].astype(jnp.bfloat16), "seq", back)
        from_before = lax.ppermute(grads[-HALF:].astype(jnp.bfloat16), "seq", ahead)
        inner = grads[HALF:-HALF]
        inner = inner.at[-HALF:].add(from_after.astype(jnp.float32))
        inner = inner.at[:HALF].add(from_before.astype(jnp.float32))
        inner = inner.astype(jnp.bfloat16)
        grads = [
            lax.dynamic_slice_in_dim(inner, ((me // 2) ^ distance) * 2 * tok, 2 * tok, 0)
            for distance in range(HEADS // 2)
        ]

    near = [grads[0]] + [None] * (HEADS // 2 - 1)
    for distance in (3, 2, 1):
        near[distance] = exchange(grads[distance], "seq", 2 * distance)
    near_other = [exchange(piece, "dp", 1) for piece in near]
    far = [exchange(piece, "seq", 1) for piece in near]

    if groups > 1:
        far_other = [exchange(piece, "dp", 1) for piece in far]
        members = [list(range(first, seq_count, 2)) for first in (0, 1)]

        def scattered(own, other):
            parts = weight_parts(place, inputs, own, other, jnp.float32)[:-1]
            return lax.psum_scatter(
                jnp.concatenate(parts), "seq", scatter_dimension=0,
                axis_index_groups=members, tiled=True,
            )

        first = scattered(near, near_other)
        second = scattered(far, far_other)
        share, width = first.shape
        shape = (share, HEADS // 2, HEAD_DIM)
        result = ordered(parity, first.reshape(shape), second.reshape(shape), 2)
        return result.reshape(share, 2 * width)

    def spread(parts, total):
        return [total] + [
            exchange(parts[distance], "seq", 2 * distance) for distance in (3, 2, 1)
        ]

    near_other, far[:2] = after(near_other, far[:2])
    *parts, total = weight_parts(place, inputs, near, near_other, jnp.bfloat16)
    first = spread(parts, total)
    far[2:], first[1] = after(far[2:], first[1])
    far_other = [exchange(piece, "dp", 1) for piece in far]
    *parts, total = weight_parts(place, inputs, far, far_other, jnp.bfloat16)
    return summed(place, first, spread(parts, total))


def solution(mesh):
    spec = P(("parts", "dp"), "seq", None)
    out_specs = P(("parts", "seq", "dp"), None)
    return jax.shard_map(
        local, mesh=mesh, in_specs=(spec,) * 5, out_specs=out_specs, check_vma=False
    )
```

profile of v0, /device:TPU:0, one launch (start us, length us, event | category | flops | bytes accessed | tf_op | source)
XLA Modules:
  0.0 113.4 jit_solution(8728214283004812463)
XLA Ops:
  0.1 1.1 copy-done.2
  3.0 6.1 %collective-permute-start.7 = (bf16[2,256,128]{2,1,0:T(8,128)(2,1)S(1)}, bf16[2,256,128]{2,1,0:T(8,128)(2,1)S(1)}, u32[]{:S(2)}, u32[]{:S(2)}) collective-permute-start(bf16[2,256,128]{2,1,0:T(8,128)(2,1)S(1)} %get-tuple-element.79), channel_id=1, source_target_pairs={{0,14},{2,12},{4,10},{6,8},{8,6},{10,4},{12,2},{14,0},{1,15},{3,13... | collective-permute-start | bytes 393224 | tf_op jit(solution)/shard_map/ppermute | solution.py:21
  9.7 3.1 %collective-permute-start.4 = (bf16[2,256,128]{2,1,0:T(8,128)(2,1)S(1)}, bf16[2,256,128]{2,1,0:T(8,128)(2,1)S(1)}, u32[]{:S(2)}, u32[]{:S(2)}) collective-permute-start(bf16[2,256,128]{2,1,0:T(8,128)(2,1)S(1)} %get-tuple-element.71), channel_id=1, source_target_pairs={{0,6},{2,4},{4,2},{6,0},{8,14},{10,12},{12,10},{14,8},{1,7},{3,5},... | collective-permute-start | bytes 393224 | tf_op jit(solution)/shard_map/ppermute | solution.py:21
  14.6 6.3 %collective-permute-start.8 = (bf16[2,256,128]{2,1,0:T(8,128)(2,1)S(1)}, bf16[2,256,128]{2,1,0:T(8,128)(2,1)S(1)}, u32[]{:S(2)}, u32[]{:S(2)}) collective-permute-start(bf16[2,256,128]{2,1,0:T(8,128)(2,1)S(1)} %get-tuple-element.81), channel_id=1, source_target_pairs={{0,10},{2,8},{4,14},{6,12},{8,2},{10,0},{12,6},{14,4},{1,11},{3,9}... | collective-permute-start | bytes 393224 | tf_op jit(solution)/shard_map/ppermute | solution.py:21
  21.0 2.2 %collective-permute-start.6 = (bf16[2,256,128]{2,1,0:T(8,128)(2,1)S(1)}, bf16[2,256,128]{2,1,0:T(8,128)(2,1)S(1)}, u32[]{:S(2)}, u32[]{:S(2)}) collective-permute-start(bf16[2,256,128]{2,1,0:T(8,128)(2,1)S(1)} %get-tuple-element.76), channel_id=1, source_target_pairs={{0,8},{2,10},{4,12},{6,14},{8,0},{10,2},{12,4},{14,6},{1,9},{3,11}... | collective-permute-start | bytes 393224 | tf_op jit(solution)/shard_map/ppermute | solution.py:21
  23.7 3.0 %collective-permute-start.11 = (bf16[2,256,128]{2,1,0:T(8,128)(2,1)S(1)}, bf16[2,256,128]{2,1,0:T(8,128)(2,1)S(1)}, u32[]{:S(2)}, u32[]{:S(2)}) collective-permute-start(bf16[2,256,128]{2,1,0:T(8,128)(2,1)S(1)} %get-tuple-element.90), channel_id=1, source_target_pairs={{0,6},{2,4},{4,2},{6,0},{8,14},{10,12},{12,10},{14,8},{1,7},{3,5},... | collective-permute-start | bytes 393224 | tf_op jit(solution)/shard_map/ppermute | solution.py:21
  27.4 2.4 %collective-permute-done.8.refs_8_ = bf16[2,256,128]{2,1,0:T(8,128)(2,1)S(1)} collective-permute-done((bf16[2,256,128]{2,1,0:T(8,128)(2,1)S(1)}, bf16[2,256,128]{2,1,0:T(8,128)(2,1)S(1)}, u32[]{:S(2)}, u32[]{:S(2)}) %collective-permute-start.8) | collective-permute-done | bytes 131104 | tf_op jit(solution)/shard_map/ppermute | solution.py:21
  29.8 1.6 %collective-permute-done.6.refs_7_ = bf16[2,256,128]{2,1,0:T(8,128)(2,1)S(1)} collective-permute-done((bf16[2,256,128]{2,1,0:T(8,128)(2,1)S(1)}, bf16[2,256,128]{2,1,0:T(8,128)(2,1)S(1)}, u32[]{:S(2)}, u32[]{:S(2)}) %collective-permute-start.6) | collective-permute-done | bytes 131104 | tf_op jit(solution)/shard_map/ppermute | solution.py:21
  31.4 2.9 %collective-permute-start.13 = (bf16[2,256,128]{2,1,0:T(8,128)(2,1)S(1)}, bf16[2,256,128]{2,1,0:T(8,128)(2,1)S(1)}, u32[]{:S(2)}, u32[]{:S(2)}) collective-permute-start(bf16[2,256,128]{2,1,0:T(8,128)(2,1)S(1)} %get-tuple-element.97), channel_id=1, source_target_pairs={{0,10},{2,8},{4,14},{6,12},{8,2},{10,0},{12,6},{14,4},{1,11},{3,9}... | collective-permute-start | bytes 393224 | tf_op jit(solution)/shard_map/ppermute | solution.py:21
  34.4 2.5 %collective-permute-start.14 = (bf16[2,256,128]{2,1,0:T(8,128)(2,1)S(1)}, bf16[2,256,128]{2,1,0:T(8,128)(2,1)S(1)}, u32[]{:S(2)}, u32[]{:S(2)}) collective-permute-start(bf16[2,256,128]{2,1,0:T(8,128)(2,1)S(1)} %get-tuple-element.98), channel_id=1, source_target_pairs={{0,12},{2,14},{4,8},{6,10},{8,4},{10,6},{12,0},{14,2},{1,13},{3,15... | collective-permute-start | bytes 393224 | tf_op jit(solution)/shard_map/ppermute | solution.py:21
  36.9 9.7 %head_first.1 = (f32[2048,128]{1,0:T(8,128)S(1)}, bf16[2048,128]{1,0:T(8,128)(2,1)S(1)}, bf16[2048,128]{1,0:T(8,128)(2,1)S(1)}) custom-call(s32[3]{0:T(128)S(1)} %pad_add_fusion.place, bf16[256,1024]{1,0:T(8,128)(2,1)S(1)} %bitcast.12, bf16[256,1024]{1,0:T(8,128)(2,1)S(1)} %bitcast.14, bf16[256,1024]{1,0:T(8,128)(2,1)S(1)} %bitcast.16, ...), custom_call_target="tpu_custom_call" | custom-call | flops 13421772800 | bytes 2097152 | tf_op jit(solution)/shard_map/head_first/pallas_call | solution.py:293
  46.5 2.3 %collective-permute-start.15 = (bf16[2,256,128]{2,1,0:T(8,128)(2,1)S(1)}, bf16[2,256,128]{2,1,0:T(8,128)(2,1)S(1)}, u32[]{:S(2)}, u32[]{:S(2)}) collective-permute-start(bf16[2,256,128]{2,1,0:T(8,128)(2,1)S(1)} %get-tuple-element.99), channel_id=1, source_target_pairs={{0,14},{2,12},{4,10},{6,8},{8,6},{10,4},{12,2},{14,0},{1,15},{3,13... | collective-permute-start | bytes 393224 | tf_op jit(solution)/shard_map/ppermute | solution.py:21
  48.9 4.5 %head_later.2.before_ref = f32[2048,128]{1,0:T(8,128)S(1)} custom-call(s32[3]{0:T(128)S(1)} %pad_add_fusion.place, f32[2048,128]{1,0:T(8,128)S(1)} %get-tuple-element.91.before_ref, bf16[2048,128]{1,0:T(8,128)(2,1)S(1)} %get-tuple-element.92.key_ref, bf16[2048,128]{1,0:T(8,128)(2,1)S(1)} %get-tuple-element.93.value_ref, ...), custom_call_target="tpu_custom_call" | custom-call | flops 6710886400 | bytes 2097152 | tf_op jit(solution)/shard_map/head_later/pallas_call | solution.py:307
  54.9 4.6 %head_later.3 = (bf16[512,128]{1,0:T(8,128)(2,1)S(1)}, bf16[512,128]{1,0:T(8,128)(2,1)S(1)}, bf16[512,128]{1,0:T(8,128)(2,1)S(1)}, bf16[512,128]{1,0:T(8,128)(2,1)S(1)}) custom-call(s32[3]{0:T(128)S(1)} %pad_add_fusion.place, f32[2048,128]{1,0:T(8,128)S(1)} %head_later.2.before_ref, bf16[2048,128]{1,0:T(8,128)(2,1)S(1)} %get-tuple-element.92.key_ref, ...), custom_call_target="tpu_custom_call" | custom-call | flops 6710886400 | bytes 2097152 | tf_op jit(solution)/shard_map/head_later/pallas_call | solution.py:307
  59.5 2.7 %collective-permute-start.16 = (bf16[512,128]{1,0:T(8,128)(2,1)S(1)}, bf16[512,128]{1,0:T(8,128)(2,1)S(1)}, u32[]{:S(2)}, u32[]{:S(2)}) collective-permute-start(bf16[512,128]{1,0:T(8,128)(2,1)S(1)} %get-tuple-element.101), channel_id=1, source_target_pairs={{0,4},{2,6},{4,0},{6,2},{8,12},{10,14},{12,8},{14,10},{1,5},{3,7},... | collective-permute-start | bytes 393224 | tf_op jit(solution)/shard_map/ppermute | solution.py:21
  62.4 2.3 %collective-permute-start.18 = (bf16[512,128]{1,0:T(8,128)(2,1)S(1)}, bf16[512,128]{1,0:T(8,128)(2,1)S(1)}, u32[]{:S(2)}, u32[]{:S(2)}) collective-permute-start(bf16[512,128]{1,0:T(8,128)(2,1)S(1)} %get-tuple-element.103), channel_id=1, source_target_pairs={{0,12},{2,14},{4,8},{6,10},{8,4},{10,6},{12,0},{14,2},{1,13},{3,15... | collective-permute-start | bytes 393224 | tf_op jit(solution)/shard_map/ppermute | solution.py:21
  64.6 2.2 %collective-permute-done.16.refs_1_ = bf16[512,128]{1,0:T(8,128)(2,1)S(1)} collective-permute-done((bf16[512,128]{1,0:T(8,128)(2,1)S(1)}, bf16[512,128]{1,0:T(8,128)(2,1)S(1)}, u32[]{:S(2)}, u32[]{:S(2)}) %collective-permute-start.16) | collective-permute-done | bytes 131104 | tf_op jit(solution)/shard_map/ppermute | solution.py:21
  67.6 7.2 %collective-permute-done.17.refs_2_ = bf16[512,128]{1,0:T(8,128)(2,1)S(1)} collective-permute-done((bf16[512,128]{1,0:T(8,128)(2,1)S(1)}, bf16[512,128]{1,0:T(8,128)(2,1)S(1)}, u32[]{:S(2)}, u32[]{:S(2)}) %collective-permute-start.17) | collective-permute-done | bytes 131104 | tf_op jit(solution)/shard_map/ppermute | solution.py:21
  76.2 1.2 %collective-permute-start.25 = (bf16[512,128]{1,0:T(8,128)(2,1)S(1)}, bf16[512,128]{1,0:T(8,128)(2,1)S(1)}, u32[]{:S(2)}, u32[]{:S(2)}) collective-permute-start(bf16[512,128]{1,0:T(8,128)(2,1)S(1)} %collective-permute-done.17.refs_2_), channel_id=1, source_target_pairs={{0,2},{2,0},{4,6},{6,4},{8,10},{10,8},{12,14},{14,12},{1,3},{3,1},... | collective-permute-start | bytes 393224 | tf_op jit(solution)/shard_map/ppermute | solution.py:21
  78.2 3.5 %collective-permute-done.24.refs_1_ = bf16[512,128]{1,0:T(8,128)(2,1)S(1)} collective-permute-done((bf16[512,128]{1,0:T(8,128)(2,1)S(1)}, bf16[512,128]{1,0:T(8,128)(2,1)S(1)}, u32[]{:S(2)}, u32[]{:S(2)}) %collective-permute-start.24) | collective-permute-done | bytes 131104 | tf_op jit(solution)/shard_map/ppermute | solution.py:21
  82.6 1.7 %weight_parts.2 = (bf16[128,512]{1,0:T(8,128)(2,1)}, bf16[128,512]{1,0:T(8,128)(2,1)S(1)}, bf16[128,512]{1,0:T(8,128)(2,1)S(1)}, bf16[128,512]{1,0:T(8,128)(2,1)S(1)}, f32[128,512]{1,0:T(8,128)S(1)}) custom-call(s32[3]{0:T(128)S(1)} %pad_add_fusion.place, bf16[4,128,1024]{2,1,0:T(8,128)(2,1)S(1)} %moved.5.input_ref, ...), custom_call_target="tpu_custom_call" | custom-call | flops 536870912 | bytes 2097152 | tf_op jit(solution)/shard_map/weight_parts/pallas_call | solution.py:350
  84.3 1.7 %collective-permute-start.27 = (bf16[128,512]{1,0:T(8,128)(2,1)S(1)}, bf16[128,512]{1,0:T(8,128)(2,1)S(1)}, u32[]{:S(2)}, u32[]{:S(2)}) collective-permute-start(bf16[128,512]{1,0:T(8,128)(2,1)S(1)} %get-tuple-element.109), channel_id=1, source_target_pairs={{0,12},{2,14},{4,8},{6,10},{8,4},{10,6},{12,0},{14,2},{1,13},{3,15... | collective-permute-start | bytes 393224 | tf_op jit(solution)/shard_map/ppermute | solution.py:21
  86.8 4.3 %collective-permute-done.27.refs_1_ = bf16[128,512]{1,0:T(8,128)(2,1)S(1)} collective-permute-done((bf16[128,512]{1,0:T(8,128)(2,1)S(1)}, bf16[128,512]{1,0:T(8,128)(2,1)S(1)}, u32[]{:S(2)}, u32[]{:S(2)}) %collective-permute-start.27) | collective-permute-done | bytes 131104 | tf_op jit(solution)/shard_map/ppermute | solution.py:21
  91.6 2.1 %collective-permute-start.28 = (bf16[128,512]{1,0:T(8,128)(2,1)S(1)}, bf16[128,512]{1,0:T(8,128)(2,1)S(1)}, u32[]{:S(2)}, u32[]{:S(2)}) collective-permute-start(bf16[128,512]{1,0:T(8,128)(2,1)S(1)} %get-tuple-element.111), channel_id=1, source_target_pairs={{0,8},{2,10},{4,12},{6,14},{8,0},{10,2},{12,4},{14,6},{1,9},{3,11}... | collective-permute-start | bytes 393224 | tf_op jit(solution)/shard_map/ppermute | solution.py:21
  93.9 1.7 %weight_parts.3 = (bf16[128,512]{1,0:T(8,128)(2,1)}, bf16[128,512]{1,0:T(8,128)(2,1)S(1)}, bf16[128,512]{1,0:T(8,128)(2,1)S(1)}, bf16[128,512]{1,0:T(8,128)(2,1)S(1)}, f32[128,512]{1,0:T(8,128)S(1)}) custom-call(s32[3]{0:T(128)S(1)} %pad_add_fusion.place, bf16[4,128,1024]{2,1,0:T(8,128)(2,1)S(1)} %moved.5.input_ref, ...), custom_call_target="tpu_custom_call" | custom-call | flops 536870912 | bytes 2097152 | tf_op jit(solution)/shard_map/weight_parts/pallas_call | solution.py:350
  95.7 2.1 %collective-permute-start.34 = (bf16[128,512]{1,0:T(8,128)(2,1)S(1)}, bf16[128,512]{1,0:T(8,128)(2,1)S(1)}, u32[]{:S(2)}, u32[]{:S(2)}) collective-permute-start(bf16[128,512]{1,0:T(8,128)(2,1)S(1)} %get-tuple-element.118), channel_id=1, source_target_pairs={{0,12},{2,14},{4,8},{6,10},{8,4},{10,6},{12,0},{14,2},{1,13},{3,15... | collective-permute-start | bytes 393224 | tf_op jit(solution)/shard_map/ppermute | solution.py:21
  97.8 1.2 %collective-permute-start.35 = (bf16[128,512]{1,0:T(8,128)(2,1)S(1)}, bf16[128,512]{1,0:T(8,128)(2,1)S(1)}, u32[]{:S(2)}, u32[]{:S(2)}) collective-permute-start(bf16[128,512]{1,0:T(8,128)(2,1)S(1)} %get-tuple-element.119), channel_id=1, source_target_pairs={{0,8},{2,10},{4,12},{6,14},{8,0},{10,2},{12,4},{14,6},{1,9},{3,11}... | collective-permute-start | bytes 393224 | tf_op jit(solution)/shard_map/ppermute | solution.py:21
  99.0 1.1 collective-permute-start.36
  100.1 2.1 %collective-permute-done.28.refs_2_ = bf16[128,512]{1,0:T(8,128)(2,1)S(1)} collective-permute-done((bf16[128,512]{1,0:T(8,128)(2,1)S(1)}, bf16[128,512]{1,0:T(8,128)(2,1)S(1)}, u32[]{:S(2)}, u32[]{:S(2)}) %collective-permute-start.28) | collective-permute-done | bytes 131104 | tf_op jit(solution)/shard_map/ppermute | solution.py:21
  102.2 3.8 %collective-permute-done.34.refs_5_ = bf16[128,512]{1,0:T(8,128)(2,1)S(1)} collective-permute-done((bf16[128,512]{1,0:T(8,128)(2,1)S(1)}, bf16[128,512]{1,0:T(8,128)(2,1)S(1)}, u32[]{:S(2)}, u32[]{:S(2)}) %collective-permute-start.34) | collective-permute-done | bytes 131104 | tf_op jit(solution)/shard_map/ppermute | solution.py:21
  106.0 6.0 %collective-permute-done.35.refs_6_ = bf16[128,512]{1,0:T(8,128)(2,1)S(1)} collective-permute-done((bf16[128,512]{1,0:T(8,128)(2,1)S(1)}, bf16[128,512]{1,0:T(8,128)(2,1)S(1)}, u32[]{:S(2)}, u32[]{:S(2)}) %collective-permute-start.35) | collective-permute-done | bytes 131104 | tf_op jit(solution)/shard_map/ppermute | solution.py:21
  112.0 1.5 %summed.1 = f32[128,1024]{1,0:T(8,128)} custom-call(s32[3]{0:T(128)S(1)} %pad_add_fusion.place, f32[128,512]{1,0:T(8,128)S(1)} %get-tuple-element.108.refs_0_, bf16[128,512]{1,0:T(8,128)(2,1)S(1)} %collective-permute-done.27.refs_1_, bf16[128,512]{1,0:T(8,128)(2,1)S(1)} %collective-permute-done.28.refs_2_, ...), custom_call_target="tpu_custom_call" | custom-call | tf_op jit(solution)/shard_map/summed/pallas_call | solution.py:385
  (70 shorter events, 12.8 us)
Async XLA Ops:
  3.0 11.6 %collective-permute-start.7 = (bf16[2,256,128]{2,1,0:T(8,128)(2,1)S(1)}, bf16[2,256,128]{2,1,0:T(8,128)(2,1)S(1)}, u32[]{:S(2)}, u32[]{:S(2)}) collective-permute-start(bf16[2,256,128]{2,1,0:T(8,128)(2,1)S(1)} %get-tuple-element.79), channel_id=1, source_target_pairs={{0,14},{2,12},{4,10},{6,8},{8,6},{10,4},{12,2},{14,0},{1,15},{3,13... | collective-permute-start | bytes 393224 | tf_op jit(solution)/shard_map/ppermute | solution.py:21
  9.1 11.9 %collective-permute-start.5 = (bf16[2,256,128]{2,1,0:T(8,128)(2,1)S(1)}, bf16[2,256,128]{2,1,0:T(8,128)(2,1)S(1)}, u32[]{:S(2)}, u32[]{:S(2)}) collective-permute-start(bf16[2,256,128]{2,1,0:T(8,128)(2,1)S(1)} %get-tuple-element.74), channel_id=1, source_target_pairs={{0,12},{2,14},{4,8},{6,10},{8,4},{10,6},{12,0},{14,2},{1,13},{3,15... | collective-permute-start | bytes 393224 | tf_op jit(solution)/shard_map/ppermute | solution.py:21
  9.3 13.8 %collective-permute-start = (bf16[2,256,128]{2,1,0:T(8,128)(2,1)S(1)}, bf16[2,256,128]{2,1,0:T(8,128)(2,1)S(1)}, u32[]{:S(2)}, u32[]{:S(2)}) collective-permute-start(bf16[2,256,128]{2,1,0:T(8,128)(2,1)S(1)} %get-tuple-element.63), channel_id=1, source_target_pairs={{0,2},{2,0},{4,6},{6,4},{8,10},{10,8},{12,14},{14,12},{1,3},{3,1},... | collective-permute-start | bytes 393224 | tf_op jit(solution)/shard_map/ppermute | solution.py:21
  9.7 14.0 %collective-permute-start.3 = (bf16[2,256,128]{2,1,0:T(8,128)(2,1)S(1)}, bf16[2,256,128]{2,1,0:T(8,128)(2,1)S(1)}, u32[]{:S(2)}, u32[]{:S(2)}) collective-permute-start(bf16[2,256,128]{2,1,0:T(8,128)(2,1)S(1)} %get-tuple-element.68), channel_id=1, source_target_pairs={{0,4},{2,6},{4,0},{6,2},{8,12},{10,14},{12,8},{14,10},{1,5},{3,7},... | collective-permute-start | bytes 393224 | tf_op jit(solution)/shard_map/ppermute | solution.py:21
  9.7 14.0 %collective-permute-start.4 = (bf16[2,256,128]{2,1,0:T(8,128)(2,1)S(1)}, bf16[2,256,128]{2,1,0:T(8,128)(2,1)S(1)}, u32[]{:S(2)}, u32[]{:S(2)}) collective-permute-start(bf16[2,256,128]{2,1,0:T(8,128)(2,1)S(1)} %get-tuple-element.71), channel_id=1, source_target_pairs={{0,6},{2,4},{4,2},{6,0},{8,14},{10,12},{12,10},{14,8},{1,7},{3,5},... | collective-permute-start | bytes 393224 | tf_op jit(solution)/shard_map/ppermute | solution.py:21
  14.6 15.2 %collective-permute-start.8 = (bf16[2,256,128]{2,1,0:T(8,128)(2,1)S(1)}, bf16[2,256,128]{2,1,0:T(8,128)(2,1)S(1)}, u32[]{:S(2)}, u32[]{:S(2)}) collective-permute-start(bf16[2,256,128]{2,1,0:T(8,128)(2,1)S(1)} %get-tuple-element.81), channel_id=1, source_target_pairs={{0,10},{2,8},{4,14},{6,12},{8,2},{10,0},{12,6},{14,4},{1,11},{3,9}... | collective-permute-start | bytes 393224 | tf_op jit(solution)/shard_map/ppermute | solution.py:21
  21.0 10.5 %collective-permute-start.6 = (bf16[2,256,128]{2,1,0:T(8,128)(2,1)S(1)}, bf16[2,256,128]{2,1,0:T(8,128)(2,1)S(1)}, u32[]{:S(2)}, u32[]{:S(2)}) collective-permute-start(bf16[2,256,128]{2,1,0:T(8,128)(2,1)S(1)} %get-tuple-element.76), channel_id=1, source_target_pairs={{0,8},{2,10},{4,12},{6,14},{8,0},{10,2},{12,4},{14,6},{1,9},{3,11}... | collective-permute-start | bytes 393224 | tf_op jit(solution)/shard_map/ppermute | solution.py:21
  23.1 8.3 %collective-permute-start.9 = (bf16[2,256,128]{2,1,0:T(8,128)(2,1)S(1)}, bf16[2,256,128]{2,1,0:T(8,128)(2,1)S(1)}, u32[]{:S(2)}, u32[]{:S(2)}) collective-permute-start(bf16[2,256,128]{2,1,0:T(8,128)(2,1)S(1)} %get-tuple-element.88), channel_id=1, source_target_pairs={{0,2},{2,0},{4,6},{6,4},{8,10},{10,8},{12,14},{14,12},{1,3},{3,1},... | collective-permute-start | bytes 393224 | tf_op jit(solution)/shard_map/ppermute | solution.py:21
  23.7 10.7 %collective-permute-start.10 = (bf16[2,256,128]{2,1,0:T(8,128)(2,1)S(1)}, bf16[2,256,128]{2,1,0:T(8,128)(2,1)S(1)}, u32[]{:S(2)}, u32[]{:S(2)}) collective-permute-start(bf16[2,256,128]{2,1,0:T(8,128)(2,1)S(1)} %get-tuple-element.89), channel_id=1, source_target_pairs={{0,4},{2,6},{4,0},{6,2},{8,12},{10,14},{12,8},{14,10},{1,5},{3,7},... | collective-permute-start | bytes 393224 | tf_op jit(solution)/shard_map/ppermute | solution.py:21
  23.7 13.1 %collective-permute-start.11 = (bf16[2,256,128]{2,1,0:T(8,128)(2,1)S(1)}, bf16[2,256,128]{2,1,0:T(8,128)(2,1)S(1)}, u32[]{:S(2)}, u32[]{:S(2)}) collective-permute-start(bf16[2,256,128]{2,1,0:T(8,128)(2,1)S(1)} %get-tuple-element.90), channel_id=1, source_target_pairs={{0,6},{2,4},{4,2},{6,0},{8,14},{10,12},{12,10},{14,8},{1,7},{3,5},... | collective-permute-start | bytes 393224 | tf_op jit(solution)/shard_map/ppermute | solution.py:21
  29.8 23.6 %collective-permute-start.1 = (bf16[8,256,128]{2,1,0:T(8,128)(2,1)S(1)}, bf16[8,256,128]{2,1,0:T(8,128)(2,1)S(1)}, u32[]{:S(2)}, u32[]{:S(2)}) collective-permute-start(bf16[8,256,128]{2,1,0:T(8,128)(2,1)S(1)} %moved.3), channel_id=1, source_target_pairs={{0,1},{1,0},{2,3},{3,2},{4,5},{5,4},{6,7},{7,6},{8,9},{9,8},{10,11... | collective-permute-start | bytes 1572872 | tf_op jit(solution)/shard_map/ppermute | solution.py:21
  31.4 15.1 %collective-permute-start.12 = (bf16[2,256,128]{2,1,0:T(8,128)(2,1)S(1)}, bf16[2,256,128]{2,1,0:T(8,128)(2,1)S(1)}, u32[]{:S(2)}, u32[]{:S(2)}) collective-permute-start(bf16[2,256,128]{2,1,0:T(8,128)(2,1)S(1)} %get-tuple-element.94), channel_id=1, source_target_pairs={{0,8},{2,10},{4,12},{6,14},{8,0},{10,2},{12,4},{14,6},{1,9},{3,11}... | collective-permute-start | bytes 393224 | tf_op jit(solution)/shard_map/ppermute | solution.py:21
  31.4 17.4 %collective-permute-start.13 = (bf16[2,256,128]{2,1,0:T(8,128)(2,1)S(1)}, bf16[2,256,128]{2,1,0:T(8,128)(2,1)S(1)}, u32[]{:S(2)}, u32[]{:S(2)}) collective-permute-start(bf16[2,256,128]{2,1,0:T(8,128)(2,1)S(1)} %get-tuple-element.97), channel_id=1, source_target_pairs={{0,10},{2,8},{4,14},{6,12},{8,2},{10,0},{12,6},{14,4},{1,11},{3,9}... | collective-permute-start | bytes 393224 | tf_op jit(solution)/shard_map/ppermute | solution.py:21
  34.4 20.6 %collective-permute-start.14 = (bf16[2,256,128]{2,1,0:T(8,128)(2,1)S(1)}, bf16[2,256,128]{2,1,0:T(8,128)(2,1)S(1)}, u32[]{:S(2)}, u32[]{:S(2)}) collective-permute-start(bf16[2,256,128]{2,1,0:T(8,128)(2,1)S(1)} %get-tuple-element.98), channel_id=1, source_target_pairs={{0,12},{2,14},{4,8},{6,10},{8,4},{10,6},{12,0},{14,2},{1,13},{3,15... | collective-permute-start | bytes 393224 | tf_op jit(solution)/shard_map/ppermute | solution.py:21
  46.5 8.4 %collective-permute-start.15 = (bf16[2,256,128]{2,1,0:T(8,128)(2,1)S(1)}, bf16[2,256,128]{2,1,0:T(8,128)(2,1)S(1)}, u32[]{:S(2)}, u32[]{:S(2)}) collective-permute-start(bf16[2,256,128]{2,1,0:T(8,128)(2,1)S(1)} %get-tuple-element.99), channel_id=1, source_target_pairs={{0,14},{2,12},{4,10},{6,8},{8,6},{10,4},{12,2},{14,0},{1,15},{3,13... | collective-permute-start | bytes 393224 | tf_op jit(solution)/shard_map/ppermute | solution.py:21
  54.1 27.6 %collective-permute-start.2 = (bf16[8,256,128]{2,1,0:T(8,128)(2,1)S(1)}, bf16[8,256,128]{2,1,0:T(8,128)(2,1)S(1)}, u32[]{:S(2)}, u32[]{:S(2)}) collective-permute-start(bf16[8,256,128]{2,1,0:T(8,128)(2,1)S(1)} %moved.4), channel_id=1, source_target_pairs={{0,2},{2,0},{4,6},{6,4},{8,10},{10,8},{12,14},{14,12},{1,3},{3,1},... | collective-permute-start | bytes 1572872 | tf_op jit(solution)/shard_map/ppermute | solution.py:21
  59.5 7.3 %collective-permute-start.16 = (bf16[512,128]{1,0:T(8,128)(2,1)S(1)}, bf16[512,128]{1,0:T(8,128)(2,1)S(1)}, u32[]{:S(2)}, u32[]{:S(2)}) collective-permute-start(bf16[512,128]{1,0:T(8,128)(2,1)S(1)} %get-tuple-element.101), channel_id=1, source_target_pairs={{0,4},{2,6},{4,0},{6,2},{8,12},{10,14},{12,8},{14,10},{1,5},{3,7},... | collective-permute-start | bytes 393224 | tf_op jit(solution)/shard_map/ppermute | solution.py:21
  62.2 12.6 %collective-permute-start.17 = (bf16[512,128]{1,0:T(8,128)(2,1)S(1)}, bf16[512,128]{1,0:T(8,128)(2,1)S(1)}, u32[]{:S(2)}, u32[]{:S(2)}) collective-permute-start(bf16[512,128]{1,0:T(8,128)(2,1)S(1)} %get-tuple-element.102), channel_id=1, source_target_pairs={{0,8},{2,10},{4,12},{6,14},{8,0},{10,2},{12,4},{14,6},{1,9},{3,11}... | collective-permute-start | bytes 393224 | tf_op jit(solution)/shard_map/ppermute | solution.py:21
  62.4 12.4 %collective-permute-start.18 = (bf16[512,128]{1,0:T(8,128)(2,1)S(1)}, bf16[512,128]{1,0:T(8,128)(2,1)S(1)}, u32[]{:S(2)}, u32[]{:S(2)}) collective-permute-start(bf16[512,128]{1,0:T(8,128)(2,1)S(1)} %get-tuple-element.103), channel_id=1, source_target_pairs={{0,12},{2,14},{4,8},{6,10},{8,4},{10,6},{12,0},{14,2},{1,13},{3,15... | collective-permute-start | bytes 393224 | tf_op jit(solution)/shard_map/ppermute | solution.py:21
  64.6 10.7 %collective-permute-start.19 = (bf16[512,128]{1,0:T(8,128)(2,1)S(1)}, bf16[512,128]{1,0:T(8,128)(2,1)S(1)}, u32[]{:S(2)}, u32[]{:S(2)}) collective-permute-start(bf16[512,128]{1,0:T(8,128)(2,1)S(1)} %get-tuple-element.100.refs_0_), channel_id=1, source_target_pairs={{0,1},{1,0},{2,3},{3,2},{4,5},{5,4},{6,7},{7,6},{8,9},{9,8},{10,11... | collective-permute-start | bytes 393224 | tf_op jit(solution)/shard_map/ppermute | solution.py:21
  66.8 8.6 %collective-permute-start.23 = (bf16[512,128]{1,0:T(8,128)(2,1)S(1)}, bf16[512,128]{1,0:T(8,128)(2,1)S(1)}, u32[]{:S(2)}, u32[]{:S(2)}) collective-permute-start(bf16[512,128]{1,0:T(8,128)(2,1)S(1)} %get-tuple-element.100.refs_0_), channel_id=1, source_target_pairs={{0,2},{2,0},{4,6},{6,4},{8,10},{10,8},{12,14},{14,12},{1,3},{3,1},... | collective-permute-start | bytes 393224 | tf_op jit(solution)/shard_map/ppermute | solution.py:21
  75.4 6.3 %collective-permute-start.24 = (bf16[512,128]{1,0:T(8,128)(2,1)S(1)}, bf16[512,128]{1,0:T(8,128)(2,1)S(1)}, u32[]{:S(2)}, u32[]{:S(2)}) collective-permute-start(bf16[512,128]{1,0:T(8,128)(2,1)S(1)} %collective-permute-done.16.refs_1_), channel_id=1, source_target_pairs={{0,2},{2,0},{4,6},{6,4},{8,10},{10,8},{12,14},{14,12},{1,3},{3,1},... | collective-permute-start | bytes 393224 | tf_op jit(solution)/shard_map/ppermute | solution.py:21
  76.2 10.3 %collective-permute-start.25 = (bf16[512,128]{1,0:T(8,128)(2,1)S(1)}, bf16[512,128]{1,0:T(8,128)(2,1)S(1)}, u32[]{:S(2)}, u32[]{:S(2)}) collective-permute-start(bf16[512,128]{1,0:T(8,128)(2,1)S(1)} %collective-permute-done.17.refs_2_), channel_id=1, source_target_pairs={{0,2},{2,0},{4,6},{6,4},{8,10},{10,8},{12,14},{14,12},{1,3},{3,1},... | collective-permute-start | bytes 393224 | tf_op jit(solution)/shard_map/ppermute | solution.py:21
  77.4 9.4 %collective-permute-start.26 = (bf16[512,128]{1,0:T(8,128)(2,1)S(1)}, bf16[512,128]{1,0:T(8,128)(2,1)S(1)}, u32[]{:S(2)}, u32[]{:S(2)}) collective-permute-start(bf16[512,128]{1,0:T(8,128)(2,1)S(1)} %collective-permute-done.18.refs_3_), channel_id=1, source_target_pairs={{0,2},{2,0},{4,6},{6,4},{8,10},{10,8},{12,14},{14,12},{1,3},{3,1},... | collective-permute-start | bytes 393224 | tf_op jit(solution)/shard_map/ppermute | solution.py:21
  84.3 6.8 %collective-permute-start.27 = (bf16[128,512]{1,0:T(8,128)(2,1)S(1)}, bf16[128,512]{1,0:T(8,128)(2,1)S(1)}, u32[]{:S(2)}, u32[]{:S(2)}) collective-permute-start(bf16[128,512]{1,0:T(8,128)(2,1)S(1)} %get-tuple-element.109), channel_id=1, source_target_pairs={{0,12},{2,14},{4,8},{6,10},{8,4},{10,6},{12,0},{14,2},{1,13},{3,15... | collective-permute-start | bytes 393224 | tf_op jit(solution)/shard_map/ppermute | solution.py:21
  86.0 7.7 %collective-permute-start.30 = (bf16[512,128]{1,0:T(8,128)(2,1)S(1)}, bf16[512,128]{1,0:T(8,128)(2,1)S(1)}, u32[]{:S(2)}, u32[]{:S(2)}) collective-permute-start(bf16[512,128]{1,0:T(8,128)(2,1)S(1)} %collective-permute-done.23.refs_0_), channel_id=1, source_target_pairs={{0,1},{1,0},{2,3},{3,2},{4,5},{5,4},{6,7},{7,6},{8,9},{9,8},{10,11... | collective-permute-start | bytes 393224 | tf_op jit(solution)/shard_map/ppermute | solution.py:21
  86.0 7.9 %collective-permute-start.31 = (bf16[512,128]{1,0:T(8,128)(2,1)S(1)}, bf16[512,128]{1,0:T(8,128)(2,1)S(1)}, u32[]{:S(2)}, u32[]{:S(2)}) collective-permute-start(bf16[512,128]{1,0:T(8,128)(2,1)S(1)} %collective-permute-done.24.refs_1_), channel_id=1, source_target_pairs={{0,1},{1,0},{2,3},{3,2},{4,5},{5,4},{6,7},{7,6},{8,9},{9,8},{10,11... | collective-permute-start | bytes 393224 | tf_op jit(solution)/shard_map/ppermute | solution.py:21
  91.6 10.6 %collective-permute-start.28 = (bf16[128,512]{1,0:T(8,128)(2,1)S(1)}, bf16[128,512]{1,0:T(8,128)(2,1)S(1)}, u32[]{:S(2)}, u32[]{:S(2)}) collective-permute-start(bf16[128,512]{1,0:T(8,128)(2,1)S(1)} %get-tuple-element.111), channel_id=1, source_target_pairs={{0,8},{2,10},{4,12},{6,14},{8,0},{10,2},{12,4},{14,6},{1,9},{3,11}... | collective-permute-start | bytes 393224 | tf_op jit(solution)/shard_map/ppermute | solution.py:21
  93.7 8.5 %collective-permute-start.29 = (bf16[128,512]{1,0:T(8,128)(2,1)S(1)}, bf16[128,512]{1,0:T(8,128)(2,1)S(1)}, u32[]{:S(2)}, u32[]{:S(2)}) collective-permute-start(bf16[128,512]{1,0:T(8,128)(2,1)S(1)} %get-tuple-element.112), channel_id=1, source_target_pairs={{0,4},{2,6},{4,0},{6,2},{8,12},{10,14},{12,8},{14,10},{1,5},{3,7},... | collective-permute-start | bytes 393224 | tf_op jit(solution)/shard_map/ppermute | solution.py:21
  95.7 10.4 %collective-permute-start.34 = (bf16[128,512]{1,0:T(8,128)(2,1)S(1)}, bf16[128,512]{1,0:T(8,128)(2,1)S(1)}, u32[]{:S(2)}, u32[]{:S(2)}) collective-permute-start(bf16[128,512]{1,0:T(8,128)(2,1)S(1)} %get-tuple-element.118), channel_id=1, source_target_pairs={{0,12},{2,14},{4,8},{6,10},{8,4},{10,6},{12,0},{14,2},{1,13},{3,15... | collective-permute-start | bytes 393224 | tf_op jit(solution)/shard_map/ppermute | solution.py:21
  97.8 14.2 %collective-permute-start.35 = (bf16[128,512]{1,0:T(8,128)(2,1)S(1)}, bf16[128,512]{1,0:T(8,128)(2,1)S(1)}, u32[]{:S(2)}, u32[]{:S(2)}) collective-permute-start(bf16[128,512]{1,0:T(8,128)(2,1)S(1)} %get-tuple-element.119), channel_id=1, source_target_pairs={{0,8},{2,10},{4,12},{6,14},{8,0},{10,2},{12,4},{14,6},{1,9},{3,11}... | collective-permute-start | bytes 393224 | tf_op jit(solution)/shard_map/ppermute | solution.py:21
  99.0 13.0 %collective-permute-start.36 = (bf16[128,512]{1,0:T(8,128)(2,1)S(1)}, bf16[128,512]{1,0:T(8,128)(2,1)S(1)}, u32[]{:S(2)}, u32[]{:S(2)}) collective-permute-start(bf16[128,512]{1,0:T(8,128)(2,1)S(1)} %get-tuple-element.120), channel_id=1, source_target_pairs={{0,4},{2,6},{4,0},{6,2},{8,12},{10,14},{12,8},{14,10},{1,5},{3,7},... | collective-permute-start | bytes 393224 | tf_op jit(solution)/shard_map/ppermute | solution.py:21
  (13 other events, 92.4 us)
where the time goes:
time: 114 us; the launch traced here: 113 us
  starting transfers between devices  49.1 us (43%)
  waiting for transfers between devices  33.5 us (29%)
  Pallas kernels  27.5 us (24%)
  local copies, waits for them, and re-layouts  3.2 us (3%)
    ppermute x37, starting transfers between devices, exchange(): lax.ppermute(value, axis, [(source, source ^ distance) for source in rang...  49.1 us
    ppermute x37, waiting for transfers between devices, exchange(): lax.ppermute(value, axis, [(source, source ^ distance) for source in rang...  33.5 us
    pallas_call x1, Pallas kernels, head_grads(): pl.pallas_call(functools.partial(first_kernel, dims, (0, 1)), out_shape=[...  9.66 us
    pallas_call x2, Pallas kernels, head_grads(): pl.pallas_call(functools.partial(later_kernel, dims, (distance,), last),...  9.12 us
    pallas_call x2, Pallas kernels, weight_parts(): pl.pallas_call(weight_kernel, out_shape=[jax.ShapeDtypeStruct((share, wid...  3.47 us
    unnamed x16, local copies, waits for them, and re-layouts  3.2 us
  transfers between devices with their start and end apart: 37, of which 10 were waited for; matrix products, arithmetic and copies ran while one was open for 0% of the time, Pallas kernels for 22%

commit v1 on v0

--- a/solution.py
+++ b/solution.py
@@ -29,69 +29,89 @@
     return total
 
 
+def slot_distances(column, core):
+    aside = (column % 2) ^ core
+    return (2 + aside, 3 - aside, 1 - aside, aside)
+
+
+def slot_route(slot):
+    pairs = []
+    for source in range(lax.axis_size("seq")):
+        for core in range(2):
+            column, parity = source // 2, source % 2
+            target = column ^ slot_distances(column, core)[slot]
+            pairs.append((2 * source + core, 2 * (2 * target + parity) + column % 2))
+    return pairs
+
+
 def columns(array, block):
     return array[:, pl.ds(pl.multiple_of(block * HEAD_DIM, HEAD_DIM), HEAD_DIM)]
 
 
-def split_kernel(distances, place, left, right, *outs):
+def split_kernel(distances, place, left, right, *refs):
+    outs, sem = refs[:-1], refs[-1]
+    copies = []
     for distance, out in zip(distances, outs):
+        start = pl.multiple_of((place[0] ^ distance) * HEAD_DIM, HEAD_DIM)
         for index, array in enumerate((left, right)):
-            out[index] = columns(array, place[0] ^ distance)
+            piece = array.at[:, pl.ds(start, HEAD_DIM)]
+            copies.append(pltpu.make_async_copy(piece, out.at[index], sem))
+    for copy in copies:
+        copy.start()
+    for copy in copies:
+        copy.wait()
 
 
 def split_heads(place, left, right, distances):
     vmem = pl.BlockSpec(memory_space=pltpu.VMEM)
+    hbm = pl.BlockSpec(memory_space=pltpu.HBM)
     tok = left.shape[0]
     shape = jax.ShapeDtypeStruct((2, tok, HEAD_DIM), left.dtype)
     pieces = pl.pallas_call(
         functools.partial(split_kernel, distances),
         out_shape=[shape] * len(distances),
-        in_specs=[pl.BlockSpec(memory_space=pltpu.SMEM), vmem, vmem],
+        in_specs=[pl.BlockSpec(memory_space=pltpu.SMEM), hbm, hbm],
         out_specs=[vmem] * len(distances),
+        scratch_shapes=[pltpu.SemaphoreType.DMA],
         compiler_params=pltpu.CompilerParams(vmem_limit_bytes=4 * 2**20),
         name="split_heads",
     )(place, left, right)
     return dict(zip(distances, pieces))
 
 
-def core_kernel(place, inputs, out):
-    for device in range(HEADS):
-        out[device] = columns(inputs, 2 * device + 1 - place[2])
-
-
-def neighbour_kernel(place, inputs, other, out):
-    count = HEADS // 2
-    for column in range(count):
-        device = 2 * column + 1 - place[0] % 2
-        out[column] = columns(inputs, 2 * device + place[2])
-        out[count + column] = other[device]
-
-
-def turned_kernel(place, inputs, other, received, out):
-    count = HEADS // 2
-    tok = inputs.shape[0]
+def sides_kernel(place, inputs, keep, give):
+    for column in range(HEADS // 2):
+        for core in range(2):
+            device = 2 * column + place[0] % 2
+            keep[2 * column + core] = columns(inputs, 2 * device + core)
+            device = 2 * column + 1 - place[0] % 2
+            give[2 * column + core] = columns(inputs, 2 * device + core)
+
+
+def turned_kernel(place, keep, keep_other, received, received_other, out):
+    tok = keep.shape[1]
     parity, core = place[0] % 2, place[2]
-
-    def put(distance, document, side, block):
-        start = pl.multiple_of((2 * document + side) * tok, tok)
-        out[distance, :, pl.ds(start, tok)] = block.T
-
-    for distance in range(count):
-        column = (place[0] // 2) ^ distance
-        device = 2 * column + parity
-        put(distance, core, parity, columns(inputs, 2 * device + core))
-        put(distance, 1 - core, parity, other[device])
-        put(distance, core, 1 - parity, received[column])
-        put(distance, 1 - core, 1 - parity, received[count + column])
-
-
-def moved(kernel, shape, dtype, *operands):
+    for distance in range(HEADS // 2):
+        for target in range(2):
+            index = 2 * ((place[0] // 2) ^ distance) + target
+            rows = slice(target * HEAD_DIM, (target + 1) * HEAD_DIM)
+            for document, side, blocks in (
+                (core, parity, keep),
+                (1 - core, parity, keep_other),
+                (core, 1 - parity, received),
+                (1 - core, 1 - parity, received_other),
+            ):
+                start = pl.multiple_of((2 * document + side) * tok, tok)
+                out[distance, rows, pl.ds(start, tok)] = blocks[index].T
+
+
+def moved(kernel, shapes, *operands):
     vmem = pl.BlockSpec(memory_space=pltpu.VMEM)
     return pl.pallas_call(
         kernel,
-        out_shape=jax.ShapeDtypeStruct(shape, dtype),
+        out_shape=shapes,
         in_specs=[pl.BlockSpec(memory_space=pltpu.SMEM)] + [vmem] * (len(operands) - 1),
-        out_specs=vmem,
+        out_specs=[vmem] * len(shapes),
         compiler_params=pltpu.CompilerParams(vmem_limit_bytes=6 * 2**20),
         name="moved",
     )(*operands)
@@ -253,7 +273,7 @@
     inverse_root = 1.0 / math.sqrt(HEAD_DIM)
     if split:
         pair = 2 * tok
-        for distance, out in enumerate(outs):
+        for distance, out in zip(slot_distances(place[0] // 2, place[2]), outs):
             start = pl.multiple_of(((place[0] // 2) ^ distance) * pair, pair)
             out[...] = (total_ref[pl.ds(start, pair)] * inverse_root).astype(jnp.bfloat16)
     elif last:
@@ -321,19 +341,15 @@
 
 
 def weight_kernel(place, input_ref, *refs):
-    count = HEADS // 2
-    own, other = refs[0:count], refs[count : 2 * count]
+    pieces, out_refs = refs[:4], refs[4:-2]
     near_ref, grad_ref = refs[-2:]
-    out_refs = refs[2 * count : -2]
     column = place[0] // 2
-    core = place[2]
-    tokens = own[0].shape[0]
-    for distance in range(count):
-        start = pl.multiple_of((column ^ distance) * HEAD_DIM, HEAD_DIM)
-        at = pl.multiple_of(core * tokens, tokens)
-        grad_ref[pl.ds(at, tokens), pl.ds(start, HEAD_DIM)] = own[distance][...]
-        at = pl.multiple_of((1 - core) * tokens, tokens)
-        grad_ref[pl.ds(at, tokens), pl.ds(start, HEAD_DIM)] = other[distance][...]
+    tokens = pieces[0].shape[0]
+    for slot, piece in enumerate(pieces):
+        document = (column % 2) ^ int(slot in (1, 2))
+        side = ((column // 2) % 2) ^ int(slot < 2)
+        rows = pl.ds(pl.multiple_of(document * tokens, tokens), tokens)
+        grad_ref[rows, pl.ds(pl.multiple_of(side * HEAD_DIM, HEAD_DIM), HEAD_DIM)] = piece[...]
     for target in range(input_ref.shape[0]):
         product = jnp.dot(
             input_ref[target], grad_ref[...], preferred_element_type=jnp.float32
@@ -343,15 +359,15 @@
             near_ref[...] = product
 
 
-def weight_parts(place, inputs, own, other, dtype):
+def weight_parts(place, inputs, pieces, dtype):
     targets, share, depth = inputs.shape
-    width = len(own) * HEAD_DIM
+    width = 2 * HEAD_DIM
     vmem = pl.BlockSpec(memory_space=pltpu.VMEM)
     return pl.pallas_call(
         weight_kernel,
         out_shape=[jax.ShapeDtypeStruct((share, width), dtype)] * targets
         + [jax.ShapeDtypeStruct((share, width), jnp.float32)],
-        in_specs=[pl.BlockSpec(memory_space=pltpu.SMEM)] + [vmem] * (1 + len(own) + len(other)),
+        in_specs=[pl.BlockSpec(memory_space=pltpu.SMEM)] + [vmem] * (1 + len(pieces)),
         out_specs=[vmem] * (targets + 1),
         scratch_shapes=[pltpu.VMEM((depth, width), jnp.bfloat16)],
         compiler_params=pltpu.CompilerParams(vmem_limit_bytes=8 * 2**20),
@@ -361,35 +377,55 @@
             transcendentals=0,
         ),
         name="weight_parts",
-    )(place, inputs, *own, *other)
+    )(place, inputs, *pieces)
 
 
 def sum_kernel(place, *refs):
-    out_ref = refs[-1]
-    count = HEADS // 2
-    for side in range(2):
-        total = refs[side * count][...]
-        for index in range(1, count):
-            total = total + refs[side * count + index][...].astype(jnp.float32)
-        parity = (place[0] % 2) ^ side
-        for column in range(count):
-            start = pl.multiple_of((2 * column + parity) * HEAD_DIM, HEAD_DIM)
-            out_ref[:, pl.ds(start, HEAD_DIM)] = total[
-                :, column * HEAD_DIM : (column + 1) * HEAD_DIM
-            ]
-
-
-def summed(place, near, far):
-    share, width = near[0].shape
+    keep_ref, give_ref = refs[-2:]
+    share = keep_ref.shape[0]
+    for out_ref, core in ((give_ref, 1 - place[2]), (keep_ref, place[2])):
+        rows = pl.ds(pl.multiple_of(core * share, share), share)
+        total = refs[0][rows]
+        for part in refs[1:-2]:
+            total = total + part[rows].astype(jnp.float32)
+        out_ref[...] = total
+
+
+def summed(place, parts):
+    share, width = parts[0].shape
     vmem = pl.BlockSpec(memory_space=pltpu.VMEM)
     return pl.pallas_call(
         sum_kernel,
-        out_shape=jax.ShapeDtypeStruct((share, 2 * width), jnp.float32),
-        in_specs=[pl.BlockSpec(memory_space=pltpu.SMEM)] + [vmem] * (len(near) + len(far)),
+        out_shape=[jax.ShapeDtypeStruct((share // 2, width), jnp.float32)] * 2,
+        in_specs=[pl.BlockSpec(memory_space=pltpu.SMEM)] + [vmem] * len(parts),
+        out_specs=[vmem] * 2,
+        compiler_params=pltpu.CompilerParams(vmem_limit_bytes=4 * 2**20),
+        name="summed",
+    )(place, *parts)
+
+
+def place_kernel(place, *refs):
+    out_ref = refs[-1]
+    for index, ref in enumerate(refs[:-1]):
+        parity, core = (place[0] % 2) ^ (index // 2), place[2] ^ (index % 2)
+        for column in range(HEADS // 4):
+            start = pl.multiple_of((4 * column + 2 * core + parity) * HEAD_DIM, HEAD_DIM)
+            out_ref[:, pl.ds(start, HEAD_DIM)] = ref[
+                :, column * HEAD_DIM : (column + 1) * HEAD_DIM
+            ]
+
+
+def placed(place, *parts):
+    share, width = parts[0].shape
+    vmem = pl.BlockSpec(memory_space=pltpu.VMEM)
+    return pl.pallas_call(
+        place_kernel,
+        out_shape=jax.ShapeDtypeStruct((share, 4 * width), jnp.float32),
+        in_specs=[pl.BlockSpec(memory_space=pltpu.SMEM)] + [vmem] * len(parts),
         out_specs=vmem,
         compiler_params=pltpu.CompilerParams(vmem_limit_bytes=4 * 2**20),
-        name="summed",
-    )(place, *near, *far)
+        name="placed",
+    )(place, *parts)
 
 
 def ordered(first, own, other, axis):
@@ -404,11 +440,9 @@
     keep = lax.dynamic_index_in_dim(shaped, parity, 2, keepdims=False)
     give = lax.dynamic_index_in_dim(shaped, 1 - parity, 2, keepdims=False)
     both = ordered(parity, keep, exchange(give, "seq", 1), 0)
-    both = both.reshape(2 * tok, columns, 2, share)
-    keep = lax.dynamic_index_in_dim(both, core, 2, keepdims=False)
-    give = lax.dynamic_index_in_dim(both, 1 - core, 2, keepdims=False)
-    full = ordered(core, keep, exchange(give, "dp", 1), 0)
-    full = full.reshape(4 * tok, columns, share).transpose(1, 2, 0)
+    both = both.reshape(2 * tok, columns, 2 * share)
+    full = ordered(core, both, exchange(both, "dp", 1), 0)
+    full = full.reshape(4 * tok, columns, 2 * share).transpose(1, 2, 0)
     if groups == 1:
         here = me // 2
         full = jnp.stack(
@@ -451,21 +485,24 @@
             key_values[first], pieces[second] = after(key_values[first], pieces[second])
         key_values |= sent(pieces, (4, 5))
         key_values[1], source = after(key_values[1], source)
-        block = (HEADS, tok, HEAD_DIM)
-        other = exchange(moved(core_kernel, block, source.dtype, place, source), "dp", 1)
-        near_piece = moved(neighbour_kernel, block, source.dtype, place, source, other)
-        received = exchange(near_piece, "seq", 1)
-        shape = (HEADS // 2, HEAD_DIM, 4 * tok)
-        inputs = moved(turned_kernel, shape, source.dtype, place, source, other, received)
+        block = jax.ShapeDtypeStruct((HEADS, tok, HEAD_DIM), source.dtype)
+        keep, give = moved(sides_kernel, [block] * 2, place, source)
+        received = exchange(give, "seq", 1)
+        sides = [keep, exchange(keep, "dp", 1), received, exchange(received, "dp", 1)]
+        shape = (HEADS // 2, 2 * HEAD_DIM, 4 * tok)
+        turned = jax.ShapeDtypeStruct(shape, source.dtype)
     else:
         key_values = sent(split_heads(place, keys, values, every), every)
         inputs = gathered_inputs(source, me, parity, core, groups)
     pieces = split_heads(place, arrays[0], arrays[3], every)
-    for first, second in ((1, 1), (2, 2), (3, 3), (4, 4), (5, 5), (5, 6)):
+    for first, second in ((1, 1), (2, 2), (3, 3), (4, 4), (5, 5), (5, 6), (5, 7)):
         key_values[first], pieces[second] = after(key_values[first], pieces[second])
-    query_grads = sent(pieces, (1, 2, 3, 4, 5, 6))
-    query_grads[4], pieces[7] = after(query_grads[4], pieces[7])
-    query_grads[7] = exchange(pieces[7], "seq", 7)
+    if direct:
+        sides[1], pieces[7] = after(sides[1], pieces[7])
+    query_grads = sent(pieces, every)
+    if direct:
+        inputs = moved(turned_kernel, [turned], place, *sides)[0]
+        query_grads[7], inputs = after(query_grads[7], inputs)
     key_values = [key_values[d] for d in range(1, HEADS)]
     query_grads = [query_grads[d] for d in range(1, HEADS)]
     halves = []
@@ -495,45 +532,47 @@
         inner = inner.astype(jnp.bfloat16)
         grads = [
             lax.dynamic_slice_in_dim(inner, ((me // 2) ^ distance) * 2 * tok, 2 * tok, 0)
-            for distance in range(HEADS // 2)
+            for distance in slot_distances(me // 2, core)
         ]
 
-    near = [grads[0]] + [None] * (HEADS // 2 - 1)
-    for distance in (3, 2, 1):
-        near[distance] = exchange(grads[distance], "seq", 2 * distance)
-    near_other = [exchange(piece, "dp", 1) for piece in near]
-    far = [exchange(piece, "seq", 1) for piece in near]
+    near = [
+        lax.ppermute(piece, ("seq", "dp"), slot_route(slot)) for slot, piece in enumerate(grads)
+    ]
+    far = [exchange(piece, "seq", 1) for piece in near[2:]]
+    held = after(near[0], near[1], *near[2:], *far)
+    far = list(held[4:])
+    far = [exchange(piece, "seq", 1) for piece in held[:2]] + far
 
     if groups > 1:
-        far_other = [exchange(piece, "dp", 1) for piece in far]
         members = [list(range(first, seq_count, 2)) for first in (0, 1)]
 
-        def scattered(own, other):
-            parts = weight_parts(place, inputs, own, other, jnp.float32)[:-1]
-            return lax.psum_scatter(
+        def scattered(pieces):
+            parts = weight_parts(place, inputs, pieces, jnp.float32)[:-1]
+            rows = lax.psum_scatter(
                 jnp.concatenate(parts), "seq", scatter_dimension=0,
                 axis_index_groups=members, tiled=True,
             )
-
-        first = scattered(near, near_other)
-        second = scattered(far, far_other)
-        share, width = first.shape
-        shape = (share, HEADS // 2, HEAD_DIM)
-        result = ordered(parity, first.reshape(shape), second.reshape(shape), 2)
-        return result.reshape(share, 2 * width)
-
-    def spread(parts, total):
+            rows = rows.reshape(2, -1, HEADS // 4, HEAD_DIM)
+            keep = lax.dynamic_index_in_dim(rows, core, 0, keepdims=False)
+            give = lax.dynamic_index_in_dim(rows, 1 - core, 0, keepdims=False)
+            return ordered(core, keep, exchange(give, "dp", 1), 2)
+
+        result = ordered(parity, scattered(near), scattered(far), 3)
+        return result.reshape(result.shape[0], HEADS * HEAD_DIM)
+
+    def spread(pieces):
+        *parts, total = weight_parts(place, inputs, pieces, jnp.bfloat16)
         return [total] + [
             exchange(parts[distance], "seq", 2 * distance) for distance in (3, 2, 1)
         ]
 
-    near_other, far[:2] = after(near_other, far[:2])
-    *parts, total = weight_parts(place, inputs, near, near_other, jnp.bfloat16)
-    first = spread(parts, total)
-    far[2:], first[1] = after(far[2:], first[1])
-    far_other = [exchange(piece, "dp", 1) for piece in far]
-    *parts, total = weight_parts(place, inputs, far, far_other, jnp.bfloat16)
-    return summed(place, first, spread(parts, total))
+    first = spread(near)
+    far, first[1] = after(far, first[1])
+    second = spread(far)
+    near_keep, near_give = summed(place, first)
+    far_keep, far_give = summed(place, second)
+    near_other, far_other = exchange(near_give, "dp", 1), exchange(far_give, "dp", 1)
+    return placed(place, near_keep, near_other, far_keep, far_other)
 
 
 def solution(mesh):

time: 114 us -> 107 us (0.939)
  waiting for transfers between devices: 33.5 us -> 22.7 us
  starting transfers between devices: 49.1 us -> 50.6 us
    ppermute x37 -> x29, waiting for transfers between devices: 33.5 us -> 16.7 us  [exchange(): lax.ppermute(value, axis, [(source, source ^ distance) for source in rang...]
    ppermute x0 -> x4, starting transfers between devices: none -> 7.74 us  [local(): lax.ppermute(piece, ('seq', 'dp'), slot_route(slot))]
    ppermute x37 -> x29, starting transfers between devices: 49.1 us -> 42.9 us  [exchange(): lax.ppermute(value, axis, [(source, source ^ distance) for source in rang...]
    ppermute x0 -> x4, waiting for transfers between devices: none -> 6.05 us  [local(): lax.ppermute(piece, ('seq', 'dp'), slot_route(slot))]
    unnamed x16 -> x18, local copies, waits for them, and re-layouts: 3.2 us -> 4.26 us
    pallas_call x4 -> x5, Pallas kernels: 3.65 us -> 4.57 us  [the longest x2 1.96 us: moved(): pl.pallas_call(kernel, out_shape=shapes, in_specs=[pl.BlockSpec(memory_sp...]
  transfers between devices with their start and end apart: 37 -> 33, of which waited for: 10 -> 11; matrix products, arithmetic and copies ran while one was open for 0% -> 0% of each run, Pallas kernels for 22% -> 20%
where the time goes in v1:
time: 107 us; the launch traced here: 106 us
  starting transfers between devices  50.6 us (47%)
  Pallas kernels  28.5 us (27%)
  waiting for transfers between devices  22.7 us (21%)
  local copies, waits for them, and re-layouts  4.26 us (4%)
    ppermute x29, starting transfers between devices, exchange(): lax.ppermute(value, axis, [(source, source ^ distance) for source in rang...  42.9 us
    ppermute x29, waiting for transfers between devices, exchange(): lax.ppermute(value, axis, [(source, source ^ distance) for source in rang...  16.7 us
    pallas_call x1, Pallas kernels, head_grads(): pl.pallas_call(functools.partial(first_kernel, dims, (0, 1)), out_shape=[...  9.66 us
    pallas_call x2, Pallas kernels, head_grads(): pl.pallas_call(functools.partial(later_kernel, dims, (distance,), last),...  9.13 us
    ppermute x4, starting transfers between devices, local(): lax.ppermute(piece, ('seq', 'dp'), slot_route(slot))  7.74 us
    ppermute x4, waiting for transfers between devices, local(): lax.ppermute(piece, ('seq', 'dp'), slot_route(slot))  6.05 us
    unnamed x18, local copies, waits for them, and re-layouts  4.26 us
    pallas_call x2, Pallas kernels, weight_parts(): pl.pallas_call(weight_kernel, out_shape=[jax.ShapeDtypeStruct((share, wid...  3.51 us
  transfers between devices with their start and end apart: 33, of which 11 were waited for; matrix products, arithmetic and copies ran while one was open for 0% of the time, Pallas kernels for 20%

profile of v1, /device:TPU:0, one launch (start us, length us, event | category | flops | bytes accessed | tf_op | source)
XLA Modules:
  0.0 106.4 jit_solution(4098129092626496190)
XLA Ops:
  0.1 1.1 %copy-done.3 = bf16[1,256,1024]{2,1,0:T(8,128)(2,1)S(1)} copy-done((bf16[1,256,1024]{2,1,0:T(8,128)(2,1)S(1)}, bf16[1,256,1024]{2,1,0:T(8,128)(2,1)}, u32[]{:S(2)}) %copy-start.3) | copy-done | bytes 524312
  3.1 6.1 %collective-permute-start.2 = (bf16[2,256,128]{2,1,0:T(8,128)(2,1)S(1)}, bf16[2,256,128]{2,1,0:T(8,128)(2,1)S(1)}, u32[]{:S(2)}, u32[]{:S(2)}) collective-permute-start(bf16[2,256,128]{2,1,0:T(8,128)(2,1)S(1)} %get-tuple-element.76), channel_id=1, source_target_pairs={{0,14},{2,12},{4,10},{6,8},{8,6},{10,4},{12,2},{14,0},{1,15},{3,13... | collective-permute-start | bytes 393224 | tf_op jit(solution)/shard_map/ppermute | solution.py:21
  9.8 3.1 %collective-permute-start.8 = (bf16[2,256,128]{2,1,0:T(8,128)(2,1)S(1)}, bf16[2,256,128]{2,1,0:T(8,128)(2,1)S(1)}, u32[]{:S(2)}, u32[]{:S(2)}) collective-permute-start(bf16[2,256,128]{2,1,0:T(8,128)(2,1)S(1)} %get-tuple-element.95), channel_id=1, source_target_pairs={{0,6},{2,4},{4,2},{6,0},{8,14},{10,12},{12,10},{14,8},{1,7},{3,5},... | collective-permute-start | bytes 393224 | tf_op jit(solution)/shard_map/ppermute | solution.py:21
  15.8 5.2 %collective-permute-start.3 = (bf16[2,256,128]{2,1,0:T(8,128)(2,1)S(1)}, bf16[2,256,128]{2,1,0:T(8,128)(2,1)S(1)}, u32[]{:S(2)}, u32[]{:S(2)}) collective-permute-start(bf16[2,256,128]{2,1,0:T(8,128)(2,1)S(1)} %get-tuple-element.78), channel_id=1, source_target_pairs={{0,10},{2,8},{4,14},{6,12},{8,2},{10,0},{12,6},{14,4},{1,11},{3,9}... | collective-permute-start | bytes 393224 | tf_op jit(solution)/shard_map/ppermute | solution.py:21
  21.0 2.2 %collective-permute-start.10 = (bf16[2,256,128]{2,1,0:T(8,128)(2,1)S(1)}, bf16[2,256,128]{2,1,0:T(8,128)(2,1)S(1)}, u32[]{:S(2)}, u32[]{:S(2)}) collective-permute-start(bf16[2,256,128]{2,1,0:T(8,128)(2,1)S(1)} %get-tuple-element.100), channel_id=1, source_target_pairs={{0,8},{2,10},{4,12},{6,14},{8,0},{10,2},{12,4},{14,6},{1,9},{3,11}... | collective-permute-start | bytes 393224 | tf_op jit(solution)/shard_map/ppermute | solution.py:21
  23.2 3.5 %collective-permute-start.13 = (bf16[2,256,128]{2,1,0:T(8,128)(2,1)S(1)}, bf16[2,256,128]{2,1,0:T(8,128)(2,1)S(1)}, u32[]{:S(2)}, u32[]{:S(2)}) collective-permute-start(bf16[2,256,128]{2,1,0:T(8,128)(2,1)S(1)} %get-tuple-element.108), channel_id=1, source_target_pairs={{0,6},{2,4},{4,2},{6,0},{8,14},{10,12},{12,10},{14,8},{1,7},{3,5},... | collective-permute-start | bytes 393224 | tf_op jit(solution)/shard_map/ppermute | solution.py:21
  27.5 2.3 %collective-permute-done.3.refs_8_ = bf16[2,256,128]{2,1,0:T(8,128)(2,1)S(1)} collective-permute-done((bf16[2,256,128]{2,1,0:T(8,128)(2,1)S(1)}, bf16[2,256,128]{2,1,0:T(8,128)(2,1)S(1)}, u32[]{:S(2)}, u32[]{:S(2)}) %collective-permute-start.3) | collective-permute-done | bytes 131104 | tf_op jit(solution)/shard_map/ppermute | solution.py:21
  29.9 1.6 %collective-permute-done.10.refs_7_ = bf16[2,256,128]{2,1,0:T(8,128)(2,1)S(1)} collective-permute-done((bf16[2,256,128]{2,1,0:T(8,128)(2,1)S(1)}, bf16[2,256,128]{2,1,0:T(8,128)(2,1)S(1)}, u32[]{:S(2)}, u32[]{:S(2)}) %collective-permute-start.10) | collective-permute-done | bytes 131104 | tf_op jit(solution)/shard_map/ppermute | solution.py:21
  32.1 3.8 %collective-permute-start.15 = (bf16[2,256,128]{2,1,0:T(8,128)(2,1)S(1)}, bf16[2,256,128]{2,1,0:T(8,128)(2,1)S(1)}, u32[]{:S(2)}, u32[]{:S(2)}) collective-permute-start(bf16[2,256,128]{2,1,0:T(8,128)(2,1)S(1)} %get-tuple-element.113), channel_id=1, source_target_pairs={{0,10},{2,8},{4,14},{6,12},{8,2},{10,0},{12,6},{14,4},{1,11},{3,9}... | collective-permute-start | bytes 393224 | tf_op jit(solution)/shard_map/ppermute | solution.py:21
  35.9 2.6 %collective-permute-start.16 = (bf16[2,256,128]{2,1,0:T(8,128)(2,1)S(1)}, bf16[2,256,128]{2,1,0:T(8,128)(2,1)S(1)}, u32[]{:S(2)}, u32[]{:S(2)}) collective-permute-start(bf16[2,256,128]{2,1,0:T(8,128)(2,1)S(1)} %get-tuple-element.114), channel_id=1, source_target_pairs={{0,12},{2,14},{4,8},{6,10},{8,4},{10,6},{12,0},{14,2},{1,13},{3,15... | collective-permute-start | bytes 393224 | tf_op jit(solution)/shard_map/ppermute | solution.py:21
  38.5 9.7 %head_first.1 = (f32[2048,128]{1,0:T(8,128)S(1)}, bf16[2048,128]{1,0:T(8,128)(2,1)S(1)}, bf16[2048,128]{1,0:T(8,128)(2,1)S(1)}) custom-call(s32[3]{0:T(128)S(1)} %pad_add_fusion.place, bf16[256,1024]{1,0:T(8,128)(2,1)S(1)} %bitcast.10, bf16[256,1024]{1,0:T(8,128)(2,1)S(1)} %bitcast.12, bf16[256,1024]{1,0:T(8,128)(2,1)S(1)} %bitcast.14, ...), custom_call_target="tpu_custom_call" | custom-call | flops 13421772800 | bytes 2097152 | tf_op jit(solution)/shard_map/head_first/pallas_call | solution.py:313
  48.2 1.3 %collective-permute-start.4 = (bf16[2,256,128]{2,1,0:T(8,128)(2,1)S(1)}, bf16[2,256,128]{2,1,0:T(8,128)(2,1)S(1)}, u32[]{:S(2)}, u32[]{:S(2)}) collective-permute-start(bf16[2,256,128]{2,1,0:T(8,128)(2,1)S(1)} %get-tuple-element.85), channel_id=1, source_target_pairs={{0,14},{2,12},{4,10},{6,8},{8,6},{10,4},{12,2},{14,0},{1,15},{3,13... | collective-permute-start | bytes 393224 | tf_op jit(solution)/shard_map/ppermute | solution.py:21
  49.9 4.5 %head_later.2.before_ref = f32[2048,128]{1,0:T(8,128)S(1)} custom-call(s32[3]{0:T(128)S(1)} %pad_add_fusion.place, f32[2048,128]{1,0:T(8,128)S(1)} %get-tuple-element.109.before_ref, bf16[2048,128]{1,0:T(8,128)(2,1)S(1)} %get-tuple-element.110.key_ref, bf16[2048,128]{1,0:T(8,128)(2,1)S(1)} %get-tuple-element.111.value_ref, ...), custom_call_target="tpu_custom_call" | custom-call | flops 6710886400 | bytes 2097152 | tf_op jit(solution)/shard_map/head_later/pallas_call | solution.py:327
  54.4 1.1 %moved.3.input_ref = bf16[4,256,1024]{2,1,0:T(8,128)(2,1)S(1)} custom-call(s32[3]{0:T(128)S(1)} %pad_add_fusion.place, bf16[8,256,128]{2,1,0:T(8,128)(2,1)S(1)} %get-tuple-element.75.keep, bf16[8,256,128]{2,1,0:T(8,128)(2,1)S(1)} %collective-permute-done.1.keep_other, bf16[8,256,128]{2,1,0:T(8,128)(2,1)S(1)} %collective-permute-done.5.received, ...), custom_call_target="tpu_custom_call" | custom-call | tf_op jit(solution)/shard_map/moved/pallas_call | solution.py:110
  56.0 4.6 %head_later.3 = (bf16[512,128]{1,0:T(8,128)(2,1)S(1)}, bf16[512,128]{1,0:T(8,128)(2,1)S(1)}, bf16[512,128]{1,0:T(8,128)(2,1)S(1)}, bf16[512,128]{1,0:T(8,128)(2,1)S(1)}) custom-call(s32[3]{0:T(128)S(1)} %pad_add_fusion.place, f32[2048,128]{1,0:T(8,128)S(1)} %head_later.2.before_ref, bf16[2048,128]{1,0:T(8,128)(2,1)S(1)} %get-tuple-element.110.key_ref, ...), custom_call_target="tpu_custom_call" | custom-call | flops 6710886400 | bytes 2097152 | tf_op jit(solution)/shard_map/head_later/pallas_call | solution.py:327
  60.6 2.2 %collective-permute-start.19 = (bf16[512,128]{1,0:T(8,128)(2,1)S(1)}, bf16[512,128]{1,0:T(8,128)(2,1)S(1)}, u32[]{:S(2)}, u32[]{:S(2)}) collective-permute-start(bf16[512,128]{1,0:T(8,128)(2,1)S(1)} %get-tuple-element.118), channel_id=1, source_target_pairs={{0,4},{1,0},{2,6},{3,2},{4,5},{5,1},{6,7},{7,3},{8,12},{9,8},{10,1... | collective-permute-start | bytes 393224 | tf_op jit(solution)/shard_map/ppermute | solution.py:539
  63.7 4.7 %collective-permute-start.18 = (bf16[512,128]{1,0:T(8,128)(2,1)S(1)}, bf16[512,128]{1,0:T(8,128)(2,1)S(1)}, u32[]{:S(2)}, u32[]{:S(2)}) collective-permute-start(bf16[512,128]{1,0:T(8,128)(2,1)S(1)} %get-tuple-element.117), channel_id=1, source_target_pairs={{0,12},{1,8},{2,14},{3,10},{4,13},{5,9},{6,15},{7,11},{8,4},{9,0},... | collective-permute-start | bytes 393224 | tf_op jit(solution)/shard_map/ppermute | solution.py:539
  68.3 1.1 %collective-permute-start.21 = (bf16[512,128]{1,0:T(8,128)(2,1)S(1)}, bf16[512,128]{1,0:T(8,128)(2,1)S(1)}, u32[]{:S(2)}, u32[]{:S(2)}) collective-permute-start(bf16[512,128]{1,0:T(8,128)(2,1)S(1)} %collective-permute-done.19.refs_2_), channel_id=1, source_target_pairs={{0,2},{2,0},{4,6},{6,4},{8,10},{10,8},{12,14},{14,12},{1,3},{3,1},... | collective-permute-start | bytes 393224 | tf_op jit(solution)/shard_map/ppermute | solution.py:21
  70.4 4.6 %collective-permute-done.17.refs_0_ = bf16[512,128]{1,0:T(8,128)(2,1)S(1)} collective-permute-done((bf16[512,128]{1,0:T(8,128)(2,1)S(1)}, bf16[512,128]{1,0:T(8,128)(2,1)S(1)}, u32[]{:S(2)}, u32[]{:S(2)}) %collective-permute-start.17) | collective-permute-done | bytes 131104 | tf_op jit(solution)/shard_map/ppermute | solution.py:539
  75.0 1.4 %collective-permute-done.18.refs_1_ = bf16[512,128]{1,0:T(8,128)(2,1)S(1)} collective-permute-done((bf16[512,128]{1,0:T(8,128)(2,1)S(1)}, bf16[512,128]{1,0:T(8,128)(2,1)S(1)}, u32[]{:S(2)}, u32[]{:S(2)}) %collective-permute-start.18) | collective-permute-done | bytes 131104 | tf_op jit(solution)/shard_map/ppermute | solution.py:539
  76.4 1.8 %weight_parts.2 = (bf16[256,256]{1,0:T(8,128)(2,1)}, bf16[256,256]{1,0:T(8,128)(2,1)S(1)}, bf16[256,256]{1,0:T(8,128)(2,1)S(1)}, bf16[256,256]{1,0:T(8,128)(2,1)S(1)}, f32[256,256]{1,0:T(8,128)S(1)}) custom-call(s32[3]{0:T(128)S(1)} %pad_add_fusion.place, bf16[4,256,1024]{2,1,0:T(8,128)(2,1)S(1)} %moved.3.input_ref, ...), custom_call_target="tpu_custom_call" | custom-call | flops 536870912 | bytes 2621440 | tf_op jit(solution)/shard_map/weight_parts/pallas_call | solution.py:366
  78.4 1.8 %collective-permute-start.23 = (bf16[512,128]{1,0:T(8,128)(2,1)S(1)}, bf16[512,128]{1,0:T(8,128)(2,1)S(1)}, u32[]{:S(2)}, u32[]{:S(2)}) collective-permute-start(bf16[512,128]{1,0:T(8,128)(2,1)S(1)} %collective-permute-done.17.refs_0_), channel_id=1, source_target_pairs={{0,2},{2,0},{4,6},{6,4},{8,10},{10,8},{12,14},{14,12},{1,3},{3,1},... | collective-permute-start | bytes 393224 | tf_op jit(solution)/shard_map/ppermute | solution.py:21
  80.4 2.5 %collective-permute-start.26 = (bf16[256,256]{1,0:T(8,128)(2,1)S(1)}, bf16[256,256]{1,0:T(8,128)(2,1)S(1)}, u32[]{:S(2)}, u32[]{:S(2)}) collective-permute-start(bf16[256,256]{1,0:T(8,128)(2,1)S(1)} %get-tuple-element.127), channel_id=1, source_target_pairs={{0,8},{2,10},{4,12},{6,14},{8,0},{10,2},{12,4},{14,6},{1,9},{3,11}... | collective-permute-start | bytes 393224 | tf_op jit(solution)/shard_map/ppermute | solution.py:21
  82.9 1.7 %collective-permute-start.27 = (bf16[256,256]{1,0:T(8,128)(2,1)S(1)}, bf16[256,256]{1,0:T(8,128)(2,1)S(1)}, u32[]{:S(2)}, u32[]{:S(2)}) collective-permute-start(bf16[256,256]{1,0:T(8,128)(2,1)S(1)} %get-tuple-element.128), channel_id=1, source_target_pairs={{0,4},{2,6},{4,0},{6,2},{8,12},{10,14},{12,8},{14,10},{1,5},{3,7},... | collective-permute-start | bytes 393224 | tf_op jit(solution)/shard_map/ppermute | solution.py:21
  84.6 1.8 %collective-permute-done.25.refs_1_ = bf16[256,256]{1,0:T(8,128)(2,1)S(1)} collective-permute-done((bf16[256,256]{1,0:T(8,128)(2,1)S(1)}, bf16[256,256]{1,0:T(8,128)(2,1)S(1)}, u32[]{:S(2)}, u32[]{:S(2)}) %collective-permute-start.25) | collective-permute-done | bytes 131104 | tf_op jit(solution)/shard_map/ppermute | solution.py:21
  86.5 1.8 %weight_parts.3 = (bf16[256,256]{1,0:T(8,128)(2,1)}, bf16[256,256]{1,0:T(8,128)(2,1)S(1)}, bf16[256,256]{1,0:T(8,128)(2,1)S(1)}, bf16[256,256]{1,0:T(8,128)(2,1)S(1)}, f32[256,256]{1,0:T(8,128)S(1)}) custom-call(s32[3]{0:T(128)S(1)} %pad_add_fusion.place, bf16[4,256,1024]{2,1,0:T(8,128)(2,1)S(1)} %moved.3.input_ref, ...), custom_call_target="tpu_custom_call" | custom-call | flops 536870912 | bytes 2621440 | tf_op jit(solution)/shard_map/weight_parts/pallas_call | solution.py:366
  88.3 2.8 %collective-permute-start.29 = (bf16[256,256]{1,0:T(8,128)(2,1)S(1)}, bf16[256,256]{1,0:T(8,128)(2,1)S(1)}, u32[]{:S(2)}, u32[]{:S(2)}) collective-permute-start(bf16[256,256]{1,0:T(8,128)(2,1)S(1)} %get-tuple-element.136), channel_id=1, source_target_pairs={{0,12},{2,14},{4,8},{6,10},{8,4},{10,6},{12,0},{14,2},{1,13},{3,15... | collective-permute-start | bytes 393224 | tf_op jit(solution)/shard_map/ppermute | solution.py:21
  91.0 2.6 %collective-permute-start.30 = (bf16[256,256]{1,0:T(8,128)(2,1)S(1)}, bf16[256,256]{1,0:T(8,128)(2,1)S(1)}, u32[]{:S(2)}, u32[]{:S(2)}) collective-permute-start(bf16[256,256]{1,0:T(8,128)(2,1)S(1)} %get-tuple-element.137), channel_id=1, source_target_pairs={{0,8},{2,10},{4,12},{6,14},{8,0},{10,2},{12,4},{14,6},{1,9},{3,11}... | collective-permute-start | bytes 393224 | tf_op jit(solution)/shard_map/ppermute | solution.py:21
  94.3 2.1 %collective-permute-done.29.refs_1_ = bf16[256,256]{1,0:T(8,128)(2,1)S(1)} collective-permute-done((bf16[256,256]{1,0:T(8,128)(2,1)S(1)}, bf16[256,256]{1,0:T(8,128)(2,1)S(1)}, u32[]{:S(2)}, u32[]{:S(2)}) %collective-permute-start.29) | collective-permute-done | bytes 131104 | tf_op jit(solution)/shard_map/ppermute | solution.py:21
  96.4 6.5 %collective-permute-done.30.refs_2_ = bf16[256,256]{1,0:T(8,128)(2,1)S(1)} collective-permute-done((bf16[256,256]{1,0:T(8,128)(2,1)S(1)}, bf16[256,256]{1,0:T(8,128)(2,1)S(1)}, u32[]{:S(2)}, u32[]{:S(2)}) %collective-permute-start.30) | collective-permute-done | bytes 131104 | tf_op jit(solution)/shard_map/ppermute | solution.py:21
  103.6 1.3 %collective-permute-done.32.refs_3_ = f32[128,256]{1,0:T(8,128)S(1)} collective-permute-done((f32[128,256]{1,0:T(8,128)S(1)}, f32[128,256]{1,0:T(8,128)S(1)}, u32[]{:S(2)}, u32[]{:S(2)}) %collective-permute-start.32) | collective-permute-done | bytes 131104 | tf_op jit(solution)/shard_map/ppermute | solution.py:21
  105.0 1.4 %placed.1 = f32[128,1024]{1,0:T(8,128)} custom-call(s32[3]{0:T(128)S(1)} %pad_add_fusion.place, f32[128,256]{1,0:T(8,128)S(1)} %get-tuple-element.129.refs_0_, f32[128,256]{1,0:T(8,128)S(1)} %collective-permute-done.28.refs_1_, f32[128,256]{1,0:T(8,128)S(1)} %get-tuple-element.139.refs_2_, f32[128,256]{1,0:T(8,128)S(1)} %collective-permute-done.32.refs_3_), custom_call_target="tpu_custom_call" | custom-call | tf_op jit(solution)/shard_map/placed/pallas_call | solution.py:421
  (65 shorter events, 11.4 us)
Async XLA Ops:
  3.1 12.7 %collective-permute-start.2 = (bf16[2,256,128]{2,1,0:T(8,128)(2,1)S(1)}, bf16[2,256,128]{2,1,0:T(8,128)(2,1)S(1)}, u32[]{:S(2)}, u32[]{:S(2)}) collective-permute-start(bf16[2,256,128]{2,1,0:T(8,128)(2,1)S(1)} %get-tuple-element.76), channel_id=1, source_target_pairs={{0,14},{2,12},{4,10},{6,8},{8,6},{10,4},{12,2},{14,0},{1,15},{3,13... | collective-permute-start | bytes 393224 | tf_op jit(solution)/shard_map/ppermute | solution.py:21
  9.1 11.9 %collective-permute-start = (bf16[2,256,128]{2,1,0:T(8,128)(2,1)S(1)}, bf16[2,256,128]{2,1,0:T(8,128)(2,1)S(1)}, u32[]{:S(2)}, u32[]{:S(2)}) collective-permute-start(bf16[2,256,128]{2,1,0:T(8,128)(2,1)S(1)} %get-tuple-element.73), channel_id=1, source_target_pairs={{0,2},{2,0},{4,6},{6,4},{8,10},{10,8},{12,14},{14,12},{1,3},{3,1},... | collective-permute-start | bytes 393224 | tf_op jit(solution)/shard_map/ppermute | solution.py:21
  9.6 11.4 %collective-permute-start.9 = (bf16[2,256,128]{2,1,0:T(8,128)(2,1)S(1)}, bf16[2,256,128]{2,1,0:T(8,128)(2,1)S(1)}, u32[]{:S(2)}, u32[]{:S(2)}) collective-permute-start(bf16[2,256,128]{2,1,0:T(8,128)(2,1)S(1)} %get-tuple-element.98), channel_id=1, source_target_pairs={{0,12},{2,14},{4,8},{6,10},{8,4},{10,6},{12,0},{14,2},{1,13},{3,15... | collective-permute-start | bytes 393224 | tf_op jit(solution)/shard_map/ppermute | solution.py:21
  9.8 13.4 %collective-permute-start.7 = (bf16[2,256,128]{2,1,0:T(8,128)(2,1)S(1)}, bf16[2,256,128]{2,1,0:T(8,128)(2,1)S(1)}, u32[]{:S(2)}, u32[]{:S(2)}) collective-permute-start(bf16[2,256,128]{2,1,0:T(8,128)(2,1)S(1)} %get-tuple-element.92), channel_id=1, source_target_pairs={{0,4},{2,6},{4,0},{6,2},{8,12},{10,14},{12,8},{14,10},{1,5},{3,7},... | collective-permute-start | bytes 393224 | tf_op jit(solution)/shard_map/ppermute | solution.py:21
  9.8 13.4 %collective-permute-start.8 = (bf16[2,256,128]{2,1,0:T(8,128)(2,1)S(1)}, bf16[2,256,128]{2,1,0:T(8,128)(2,1)S(1)}, u32[]{:S(2)}, u32[]{:S(2)}) collective-permute-start(bf16[2,256,128]{2,1,0:T(8,128)(2,1)S(1)} %get-tuple-element.95), channel_id=1, source_target_pairs={{0,6},{2,4},{4,2},{6,0},{8,14},{10,12},{12,10},{14,8},{1,7},{3,5},... | collective-permute-start | bytes 393224 | tf_op jit(solution)/shard_map/ppermute | solution.py:21
  15.8 14.1 %collective-permute-start.3 = (bf16[2,256,128]{2,1,0:T(8,128)(2,1)S(1)}, bf16[2,256,128]{2,1,0:T(8,128)(2,1)S(1)}, u32[]{:S(2)}, u32[]{:S(2)}) collective-permute-start(bf16[2,256,128]{2,1,0:T(8,128)(2,1)S(1)} %get-tuple-element.78), channel_id=1, source_target_pairs={{0,10},{2,8},{4,14},{6,12},{8,2},{10,0},{12,6},{14,4},{1,11},{3,9}... | collective-permute-start | bytes 393224 | tf_op jit(solution)/shard_map/ppermute | solution.py:21
  21.0 10.5 %collective-permute-start.10 = (bf16[2,256,128]{2,1,0:T(8,128)(2,1)S(1)}, bf16[2,256,128]{2,1,0:T(8,128)(2,1)S(1)}, u32[]{:S(2)}, u32[]{:S(2)}) collective-permute-start(bf16[2,256,128]{2,1,0:T(8,128)(2,1)S(1)} %get-tuple-element.100), channel_id=1, source_target_pairs={{0,8},{2,10},{4,12},{6,14},{8,0},{10,2},{12,4},{14,6},{1,9},{3,11}... | collective-permute-start | bytes 393224 | tf_op jit(solution)/shard_map/ppermute | solution.py:21
  23.2 8.9 %collective-permute-start.11 = (bf16[2,256,128]{2,1,0:T(8,128)(2,1)S(1)}, bf16[2,256,128]{2,1,0:T(8,128)(2,1)S(1)}, u32[]{:S(2)}, u32[]{:S(2)}) collective-permute-start(bf16[2,256,128]{2,1,0:T(8,128)(2,1)S(1)} %get-tuple-element.106), channel_id=1, source_target_pairs={{0,2},{2,0},{4,6},{6,4},{8,10},{10,8},{12,14},{14,12},{1,3},{3,1},... | collective-permute-start | bytes 393224 | tf_op jit(solution)/shard_map/ppermute | solution.py:21
  23.2 8.9 %collective-permute-start.12 = (bf16[2,256,128]{2,1,0:T(8,128)(2,1)S(1)}, bf16[2,256,128]{2,1,0:T(8,128)(2,1)S(1)}, u32[]{:S(2)}, u32[]{:S(2)}) collective-permute-start(bf16[2,256,128]{2,1,0:T(8,128)(2,1)S(1)} %get-tuple-element.107), channel_id=1, source_target_pairs={{0,4},{2,6},{4,0},{6,2},{8,12},{10,14},{12,8},{14,10},{1,5},{3,7},... | collective-permute-start | bytes 393224 | tf_op jit(solution)/shard_map/ppermute | solution.py:21
  23.2 12.7 %collective-permute-start.13 = (bf16[2,256,128]{2,1,0:T(8,128)(2,1)S(1)}, bf16[2,256,128]{2,1,0:T(8,128)(2,1)S(1)}, u32[]{:S(2)}, u32[]{:S(2)}) collective-permute-start(bf16[2,256,128]{2,1,0:T(8,128)(2,1)S(1)} %get-tuple-element.108), channel_id=1, source_target_pairs={{0,6},{2,4},{4,2},{6,0},{8,14},{10,12},{12,10},{14,8},{1,7},{3,5},... | collective-permute-start | bytes 393224 | tf_op jit(solution)/shard_map/ppermute | solution.py:21
  29.9 18.3 %collective-permute-start.1 = (bf16[8,256,128]{2,1,0:T(8,128)(2,1)S(1)}, bf16[8,256,128]{2,1,0:T(8,128)(2,1)S(1)}, u32[]{:S(2)}, u32[]{:S(2)}) collective-permute-start(bf16[8,256,128]{2,1,0:T(8,128)(2,1)S(1)} %get-tuple-element.75.keep), channel_id=1, source_target_pairs={{0,1},{1,0},{2,3},{3,2},{4,5},{5,4},{6,7},{7,6},{8,9},{9,8},{10,11... | collective-permute-start | bytes 1572872 | tf_op jit(solution)/shard_map/ppermute | solution.py:21
  31.5 18.0 %collective-permute-start.5 = (bf16[8,256,128]{2,1,0:T(8,128)(2,1)S(1)}, bf16[8,256,128]{2,1,0:T(8,128)(2,1)S(1)}, u32[]{:S(2)}, u32[]{:S(2)}) collective-permute-start(bf16[8,256,128]{2,1,0:T(8,128)(2,1)S(1)} %get-tuple-element.87), channel_id=1, source_target_pairs={{0,2},{2,0},{4,6},{6,4},{8,10},{10,8},{12,14},{14,12},{1,3},{3,1},... | collective-permute-start | bytes 1572872 | tf_op jit(solution)/shard_map/ppermute | solution.py:21
  32.1 17.4 %collective-permute-start.14 = (bf16[2,256,128]{2,1,0:T(8,128)(2,1)S(1)}, bf16[2,256,128]{2,1,0:T(8,128)(2,1)S(1)}, u32[]{:S(2)}, u32[]{:S(2)}) collective-permute-start(bf16[2,256,128]{2,1,0:T(8,128)(2,1)S(1)} %get-tuple-element.112), channel_id=1, source_target_pairs={{0,8},{2,10},{4,12},{6,14},{8,0},{10,2},{12,4},{14,6},{1,9},{3,11}... | collective-permute-start | bytes 393224 | tf_op jit(solution)/shard_map/ppermute | solution.py:21
  32.1 17.8 %collective-permute-start.15 = (bf16[2,256,128]{2,1,0:T(8,128)(2,1)S(1)}, bf16[2,256,128]{2,1,0:T(8,128)(2,1)S(1)}, u32[]{:S(2)}, u32[]{:S(2)}) collective-permute-start(bf16[2,256,128]{2,1,0:T(8,128)(2,1)S(1)} %get-tuple-element.113), channel_id=1, source_target_pairs={{0,10},{2,8},{4,14},{6,12},{8,2},{10,0},{12,6},{14,4},{1,11},{3,9}... | collective-permute-start | bytes 393224 | tf_op jit(solution)/shard_map/ppermute | solution.py:21
  35.9 20.1 %collective-permute-start.16 = (bf16[2,256,128]{2,1,0:T(8,128)(2,1)S(1)}, bf16[2,256,128]{2,1,0:T(8,128)(2,1)S(1)}, u32[]{:S(2)}, u32[]{:S(2)}) collective-permute-start(bf16[2,256,128]{2,1,0:T(8,128)(2,1)S(1)} %get-tuple-element.114), channel_id=1, source_target_pairs={{0,12},{2,14},{4,8},{6,10},{8,4},{10,6},{12,0},{14,2},{1,13},{3,15... | collective-permute-start | bytes 393224 | tf_op jit(solution)/shard_map/ppermute | solution.py:21
  48.2 7.8 %collective-permute-start.4 = (bf16[2,256,128]{2,1,0:T(8,128)(2,1)S(1)}, bf16[2,256,128]{2,1,0:T(8,128)(2,1)S(1)}, u32[]{:S(2)}, u32[]{:S(2)}) collective-permute-start(bf16[2,256,128]{2,1,0:T(8,128)(2,1)S(1)} %get-tuple-element.85), channel_id=1, source_target_pairs={{0,14},{2,12},{4,10},{6,8},{8,6},{10,4},{12,2},{14,0},{1,15},{3,13... | collective-permute-start | bytes 393224 | tf_op jit(solution)/shard_map/ppermute | solution.py:21
  49.5 4.9 %collective-permute-start.6 = (bf16[8,256,128]{2,1,0:T(8,128)(2,1)S(1)}, bf16[8,256,128]{2,1,0:T(8,128)(2,1)S(1)}, u32[]{:S(2)}, u32[]{:S(2)}) collective-permute-start(bf16[8,256,128]{2,1,0:T(8,128)(2,1)S(1)} %collective-permute-done.5.received), channel_id=1, source_target_pairs={{0,1},{1,0},{2,3},{3,2},{4,5},{5,4},{6,7},{7,6},{8,9},{9,8},{10,11... | collective-permute-start | bytes 1572872 | tf_op jit(solution)/shard_map/ppermute | solution.py:21
  60.6 7.8 %collective-permute-start.19 = (bf16[512,128]{1,0:T(8,128)(2,1)S(1)}, bf16[512,128]{1,0:T(8,128)(2,1)S(1)}, u32[]{:S(2)}, u32[]{:S(2)}) collective-permute-start(bf16[512,128]{1,0:T(8,128)(2,1)S(1)} %get-tuple-element.118), channel_id=1, source_target_pairs={{0,4},{1,0},{2,6},{3,2},{4,5},{5,1},{6,7},{7,3},{8,12},{9,8},{10,1... | collective-permute-start | bytes 393224 | tf_op jit(solution)/shard_map/ppermute | solution.py:539
  62.8 6.6 %collective-permute-start.20 = (bf16[512,128]{1,0:T(8,128)(2,1)S(1)}, bf16[512,128]{1,0:T(8,128)(2,1)S(1)}, u32[]{:S(2)}, u32[]{:S(2)}) collective-permute-start(bf16[512,128]{1,0:T(8,128)(2,1)S(1)} %get-tuple-element.119), channel_id=1, source_target_pairs={{0,0},{1,4},{2,2},{3,6},{4,1},{5,5},{6,3},{7,7},{8,8},{9,12},{10,1... | collective-permute-start | bytes 393224 | tf_op jit(solution)/shard_map/ppermute | solution.py:539
  63.5 11.5 %collective-permute-start.17 = (bf16[512,128]{1,0:T(8,128)(2,1)S(1)}, bf16[512,128]{1,0:T(8,128)(2,1)S(1)}, u32[]{:S(2)}, u32[]{:S(2)}) collective-permute-start(bf16[512,128]{1,0:T(8,128)(2,1)S(1)} %get-tuple-element.116), channel_id=1, source_target_pairs={{0,8},{1,12},{2,10},{3,14},{4,9},{5,13},{6,11},{7,15},{8,0},{9,4},... | collective-permute-start | bytes 393224 | tf_op jit(solution)/shard_map/ppermute | solution.py:539
  63.7 12.8 %collective-permute-start.18 = (bf16[512,128]{1,0:T(8,128)(2,1)S(1)}, bf16[512,128]{1,0:T(8,128)(2,1)S(1)}, u32[]{:S(2)}, u32[]{:S(2)}) collective-permute-start(bf16[512,128]{1,0:T(8,128)(2,1)S(1)} %get-tuple-element.117), channel_id=1, source_target_pairs={{0,12},{1,8},{2,14},{3,10},{4,13},{5,9},{6,15},{7,11},{8,4},{9,0},... | collective-permute-start | bytes 393224 | tf_op jit(solution)/shard_map/ppermute | solution.py:539
  68.3 10.0 %collective-permute-start.21 = (bf16[512,128]{1,0:T(8,128)(2,1)S(1)}, bf16[512,128]{1,0:T(8,128)(2,1)S(1)}, u32[]{:S(2)}, u32[]{:S(2)}) collective-permute-start(bf16[512,128]{1,0:T(8,128)(2,1)S(1)} %collective-permute-done.19.refs_2_), channel_id=1, source_target_pairs={{0,2},{2,0},{4,6},{6,4},{8,10},{10,8},{12,14},{14,12},{1,3},{3,1},... | collective-permute-start | bytes 393224 | tf_op jit(solution)/shard_map/ppermute | solution.py:21
  69.4 9.0 %collective-permute-start.22 = (bf16[512,128]{1,0:T(8,128)(2,1)S(1)}, bf16[512,128]{1,0:T(8,128)(2,1)S(1)}, u32[]{:S(2)}, u32[]{:S(2)}) collective-permute-start(bf16[512,128]{1,0:T(8,128)(2,1)S(1)} %collective-permute-done.20.refs_3_), channel_id=1, source_target_pairs={{0,2},{2,0},{4,6},{6,4},{8,10},{10,8},{12,14},{14,12},{1,3},{3,1},... | collective-permute-start | bytes 393224 | tf_op jit(solution)/shard_map/ppermute | solution.py:21
  78.2 8.2 %collective-permute-start.25 = (bf16[256,256]{1,0:T(8,128)(2,1)S(1)}, bf16[256,256]{1,0:T(8,128)(2,1)S(1)}, u32[]{:S(2)}, u32[]{:S(2)}) collective-permute-start(bf16[256,256]{1,0:T(8,128)(2,1)S(1)} %get-tuple-element.125), channel_id=1, source_target_pairs={{0,12},{2,14},{4,8},{6,10},{8,4},{10,6},{12,0},{14,2},{1,13},{3,15... | collective-permute-start | bytes 393224 | tf_op jit(solution)/shard_map/ppermute | solution.py:21
  78.4 8.0 %collective-permute-start.23 = (bf16[512,128]{1,0:T(8,128)(2,1)S(1)}, bf16[512,128]{1,0:T(8,128)(2,1)S(1)}, u32[]{:S(2)}, u32[]{:S(2)}) collective-permute-start(bf16[512,128]{1,0:T(8,128)(2,1)S(1)} %collective-permute-done.17.refs_0_), channel_id=1, source_target_pairs={{0,2},{2,0},{4,6},{6,4},{8,10},{10,8},{12,14},{14,12},{1,3},{3,1},... | collective-permute-start | bytes 393224 | tf_op jit(solution)/shard_map/ppermute | solution.py:21
  80.2 6.3 %collective-permute-start.24 = (bf16[512,128]{1,0:T(8,128)(2,1)S(1)}, bf16[512,128]{1,0:T(8,128)(2,1)S(1)}, u32[]{:S(2)}, u32[]{:S(2)}) collective-permute-start(bf16[512,128]{1,0:T(8,128)(2,1)S(1)} %collective-permute-done.18.refs_1_), channel_id=1, source_target_pairs={{0,2},{2,0},{4,6},{6,4},{8,10},{10,8},{12,14},{14,12},{1,3},{3,1},... | collective-permute-start | bytes 393224 | tf_op jit(solution)/shard_map/ppermute | solution.py:21
  80.4 13.2 %collective-permute-start.26 = (bf16[256,256]{1,0:T(8,128)(2,1)S(1)}, bf16[256,256]{1,0:T(8,128)(2,1)S(1)}, u32[]{:S(2)}, u32[]{:S(2)}) collective-permute-start(bf16[256,256]{1,0:T(8,128)(2,1)S(1)} %get-tuple-element.127), channel_id=1, source_target_pairs={{0,8},{2,10},{4,12},{6,14},{8,0},{10,2},{12,4},{14,6},{1,9},{3,11}... | collective-permute-start | bytes 393224 | tf_op jit(solution)/shard_map/ppermute | solution.py:21
  82.9 10.7 %collective-permute-start.27 = (bf16[256,256]{1,0:T(8,128)(2,1)S(1)}, bf16[256,256]{1,0:T(8,128)(2,1)S(1)}, u32[]{:S(2)}, u32[]{:S(2)}) collective-permute-start(bf16[256,256]{1,0:T(8,128)(2,1)S(1)} %get-tuple-element.128), channel_id=1, source_target_pairs={{0,4},{2,6},{4,0},{6,2},{8,12},{10,14},{12,8},{14,10},{1,5},{3,7},... | collective-permute-start | bytes 393224 | tf_op jit(solution)/shard_map/ppermute | solution.py:21
  88.3 8.1 %collective-permute-start.29 = (bf16[256,256]{1,0:T(8,128)(2,1)S(1)}, bf16[256,256]{1,0:T(8,128)(2,1)S(1)}, u32[]{:S(2)}, u32[]{:S(2)}) collective-permute-start(bf16[256,256]{1,0:T(8,128)(2,1)S(1)} %get-tuple-element.136), channel_id=1, source_target_pairs={{0,12},{2,14},{4,8},{6,10},{8,4},{10,6},{12,0},{14,2},{1,13},{3,15... | collective-permute-start | bytes 393224 | tf_op jit(solution)/shard_map/ppermute | solution.py:21
  91.0 11.9 %collective-permute-start.30 = (bf16[256,256]{1,0:T(8,128)(2,1)S(1)}, bf16[256,256]{1,0:T(8,128)(2,1)S(1)}, u32[]{:S(2)}, u32[]{:S(2)}) collective-permute-start(bf16[256,256]{1,0:T(8,128)(2,1)S(1)} %get-tuple-element.137), channel_id=1, source_target_pairs={{0,8},{2,10},{4,12},{6,14},{8,0},{10,2},{12,4},{14,6},{1,9},{3,11}... | collective-permute-start | bytes 393224 | tf_op jit(solution)/shard_map/ppermute | solution.py:21
  93.6 9.3 %collective-permute-start.31 = (bf16[256,256]{1,0:T(8,128)(2,1)S(1)}, bf16[256,256]{1,0:T(8,128)(2,1)S(1)}, u32[]{:S(2)}, u32[]{:S(2)}) collective-permute-start(bf16[256,256]{1,0:T(8,128)(2,1)S(1)} %get-tuple-element.138), channel_id=1, source_target_pairs={{0,4},{2,6},{4,0},{6,2},{8,12},{10,14},{12,8},{14,10},{1,5},{3,7},... | collective-permute-start | bytes 393224 | tf_op jit(solution)/shard_map/ppermute | solution.py:21
  94.2 9.4 %collective-permute-start.28 = (f32[128,256]{1,0:T(8,128)S(1)}, f32[128,256]{1,0:T(8,128)S(1)}, u32[]{:S(2)}, u32[]{:S(2)}) collective-permute-start(f32[128,256]{1,0:T(8,128)S(1)} %get-tuple-element.130), channel_id=1, source_target_pairs={{0,1},{1,0},{2,3},{3,2},{4,5},{5,4},{6,7},{7,6},{8,9},{9,8},{10,11... | collective-permute-start | bytes 393224 | tf_op jit(solution)/shard_map/ppermute | solution.py:21
  (10 other events, 126.5 us)

commit v2 on v1

--- a/solution.py
+++ b/solution.py
@@ -13,6 +13,7 @@
 HALF = 1024
 NEG = -1e30
 CHUNK = 2
+SKIP = 2
 NT = (((1,), (1,)), ((), ()))
 
 
@@ -117,19 +118,26 @@
     )(*operands)
 
 
-def head_block(dims, place, b, query, grad, key_ref, value_ref, score_ref, dprob_ref, total_ref):
+def head_block(dims, place, b, edge, query, grad, key_ref, value_ref, score_ref, dprob_ref, total_ref):
     tok, halo, groups = dims
     shift = halo // tok
     reach = HALF // tok
     scale = math.log2(math.e) / math.sqrt(HEAD_DIM)
     ahead = lax.broadcasted_iota(jnp.int32, (tok, tok), 0)
     ahead = ahead - lax.broadcasted_iota(jnp.int32, (tok, tok), 1)
-    first, count = (b + shift - reach, 2 * reach + 1) if halo else (0, HEADS)
+    if halo:
+        first, count, below, above = b + shift - reach, 2 * reach + 1, 1, 2 * reach
+    elif edge:
+        first, count = jnp.where(b >= reach, SKIP, 0), HEADS - SKIP
+        below, above = HEADS - reach - SKIP, reach
+    else:
+        first, count, below, above = 0, HEADS, SKIP, HEADS - SKIP
     chunks = [range(start, min(start + CHUNK, count)) for start in range(0, count, CHUNK)]
 
     def rows_of(chunk):
         start = (first + chunk[0]) * tok
-        return pl.ds(pl.multiple_of(start, tok) if halo else start, len(chunk) * tok)
+        traced = halo or edge
+        return pl.ds(pl.multiple_of(start, tok) if traced else start, len(chunk) * tok)
 
     def held(at):
         return slice(at * tok, (at + 1) * tok)
@@ -142,9 +150,9 @@
         for at in chunk:
             score = scores[held(at - chunk[0])]
             distance = first + at - shift - b
-            if at == 0 if halo else at < HEADS - reach:
+            if at < below:
                 score = jnp.where(ahead >= -HALF - distance * tok, score, NEG)
-            if at == 2 * reach if halo else at >= reach:
+            if at >= above:
                 score = jnp.where(ahead <= HALF - distance * tok, score, NEG)
             if halo:
                 inside = (first + at >= shift) | (place[1] > 0)
@@ -195,10 +203,21 @@
 
     def block(slot, distance):
         rows = pl.ds(pl.multiple_of(slot * tok, tok), tok)
-        head_block(
-            dims, place, me ^ distance, query_ref[rows], grad_ref[rows], key_ref, value_ref,
-            score_ref, dprob_ref, total_ref,
-        )
+        index = me ^ distance
+
+        def work(edge):
+            head_block(
+                dims, place, index, edge, query_ref[rows], grad_ref[rows], key_ref, value_ref,
+                score_ref, dprob_ref, total_ref,
+            )
+
+        if dims[1]:
+            work(False)
+            return
+        reach = HALF // tok
+        edge = (index < HEADS - SKIP - reach) | (index >= reach + SKIP)
+        pl.when(edge)(lambda: work(True))
+        pl.when(jnp.logical_not(edge))(lambda: work(False))
 
     @pl.loop(0, 2 * len(distances))
     def _(slot):
@@ -340,9 +359,8 @@
     return out if split else out[0]
 
 
-def weight_kernel(place, input_ref, *refs):
-    pieces, out_refs = refs[:4], refs[4:-2]
-    near_ref, grad_ref = refs[-2:]
+def weight_kernel(targets, place, input_ref, *refs):
+    pieces, out_refs, grad_ref = refs[:4], refs[4:-1], refs[-1]
     column = place[0] // 2
     tokens = pieces[0].shape[0]
     for slot, piece in enumerate(pieces):
@@ -350,30 +368,27 @@
         side = ((column // 2) % 2) ^ int(slot < 2)
         rows = pl.ds(pl.multiple_of(document * tokens, tokens), tokens)
         grad_ref[rows, pl.ds(pl.multiple_of(side * HEAD_DIM, HEAD_DIM), HEAD_DIM)] = piece[...]
-    for target in range(input_ref.shape[0]):
+    for target, out_ref in zip(targets, out_refs):
         product = jnp.dot(
             input_ref[target], grad_ref[...], preferred_element_type=jnp.float32
         )
-        out_refs[target][...] = product.astype(out_refs[target].dtype)
-        if target == 0:
-            near_ref[...] = product
-
-
-def weight_parts(place, inputs, pieces, dtype):
-    targets, share, depth = inputs.shape
+        out_ref[...] = product.astype(out_ref.dtype)
+
+
+def weight_parts(place, inputs, pieces, targets, dtypes):
+    _, share, depth = inputs.shape
     width = 2 * HEAD_DIM
     vmem = pl.BlockSpec(memory_space=pltpu.VMEM)
     return pl.pallas_call(
-        weight_kernel,
-        out_shape=[jax.ShapeDtypeStruct((share, width), dtype)] * targets
-        + [jax.ShapeDtypeStruct((share, width), jnp.float32)],
+        functools.partial(weight_kernel, targets),
+        out_shape=[jax.ShapeDtypeStruct((share, width), dtype) for dtype in dtypes],
         in_specs=[pl.BlockSpec(memory_space=pltpu.SMEM)] + [vmem] * (1 + len(pieces)),
-        out_specs=[vmem] * (targets + 1),
+        out_specs=[vmem] * len(targets),
         scratch_shapes=[pltpu.VMEM((depth, width), jnp.bfloat16)],
         compiler_params=pltpu.CompilerParams(vmem_limit_bytes=8 * 2**20),
         cost_estimate=pl.CostEstimate(
-            flops=2 * targets * share * depth * width,
-            bytes_accessed=2 * depth * (width + targets * share),
+            flops=2 * len(targets) * share * depth * width,
+            bytes_accessed=2 * depth * (width + len(targets) * share),
             transcendentals=0,
         ),
         name="weight_parts",
@@ -404,28 +419,38 @@
     )(place, *parts)
 
 
-def place_kernel(place, *refs):
-    out_ref = refs[-1]
-    for index, ref in enumerate(refs[:-1]):
-        parity, core = (place[0] % 2) ^ (index // 2), place[2] ^ (index % 2)
+def place_kernel(side, place, *refs):
+    parts, out_ref, sem = refs[:2], refs[-2], refs[-1]
+    parity = (place[0] % 2) ^ side
+    copies = []
+    for index, ref in enumerate(parts):
         for column in range(HEADS // 4):
-            start = pl.multiple_of((4 * column + 2 * core + parity) * HEAD_DIM, HEAD_DIM)
-            out_ref[:, pl.ds(start, HEAD_DIM)] = ref[
-                :, column * HEAD_DIM : (column + 1) * HEAD_DIM
-            ]
-
-
-def placed(place, *parts):
-    share, width = parts[0].shape
+            block = 4 * column + 2 * (place[2] ^ index) + parity
+            start = pl.multiple_of(block * HEAD_DIM, HEAD_DIM)
+            source = ref.at[:, column * HEAD_DIM : (column + 1) * HEAD_DIM]
+            target = out_ref.at[:, pl.ds(start, HEAD_DIM)]
+            copies.append(pltpu.make_async_copy(source, target, sem))
+    for copy in copies:
+        copy.start()
+    for copy in copies:
+        copy.wait()
+
+
+def placed(place, side, keep, other, before=None):
+    share, width = keep.shape
     vmem = pl.BlockSpec(memory_space=pltpu.VMEM)
+    hbm = pl.BlockSpec(memory_space=pltpu.HBM)
+    rest = [] if before is None else [before]
     return pl.pallas_call(
-        place_kernel,
+        functools.partial(place_kernel, side),
         out_shape=jax.ShapeDtypeStruct((share, 4 * width), jnp.float32),
-        in_specs=[pl.BlockSpec(memory_space=pltpu.SMEM)] + [vmem] * len(parts),
-        out_specs=vmem,
-        compiler_params=pltpu.CompilerParams(vmem_limit_bytes=4 * 2**20),
+        in_specs=[pl.BlockSpec(memory_space=pltpu.SMEM), vmem, vmem] + [hbm] * len(rest),
+        out_specs=hbm,
+        scratch_shapes=[pltpu.SemaphoreType.DMA],
+        input_output_aliases={3: 0} if rest else {},
+        compiler_params=pltpu.CompilerParams(vmem_limit_bytes=2 * 2**20),
         name="placed",
-    )(place, *parts)
+    )(place, keep, other, *rest)
 
 
 def ordered(first, own, other, axis):
@@ -547,7 +572,8 @@
         members = [list(range(first, seq_count, 2)) for first in (0, 1)]
 
         def scattered(pieces):
-            parts = weight_parts(place, inputs, pieces, jnp.float32)[:-1]
+            targets = range(inputs.shape[0])
+            parts = weight_parts(place, inputs, pieces, targets, [jnp.float32] * len(targets))
             rows = lax.psum_scatter(
                 jnp.concatenate(parts), "seq", scatter_dimension=0,
                 axis_index_groups=members, tiled=True,
@@ -561,18 +587,19 @@
         return result.reshape(result.shape[0], HEADS * HEAD_DIM)
 
     def spread(pieces):
-        *parts, total = weight_parts(place, inputs, pieces, jnp.bfloat16)
-        return [total] + [
-            exchange(parts[distance], "seq", 2 * distance) for distance in (3, 2, 1)
-        ]
+        low = jnp.bfloat16
+        across = weight_parts(place, inputs, pieces, (3, 2), (low, low))
+        beside, total = weight_parts(place, inputs, pieces, (1, 0), (low, jnp.float32))
+        parts = zip((3, 2, 1), (*across, beside))
+        return [total] + [exchange(part, "seq", 2 * distance) for distance, part in parts]
 
     first = spread(near)
     far, first[1] = after(far, first[1])
     second = spread(far)
     near_keep, near_give = summed(place, first)
     far_keep, far_give = summed(place, second)
-    near_other, far_other = exchange(near_give, "dp", 1), exchange(far_give, "dp", 1)
-    return placed(place, near_keep, near_other, far_keep, far_other)
+    half = placed(place, 0, near_keep, exchange(near_give, "dp", 1))
+    return placed(place, 1, far_keep, exchange(far_give, "dp", 1), half)
 
 
 def solution(mesh):

time: 107 us -> 106 us (level)
  Pallas kernels: 28.5 us -> 27.4 us
  starting transfers between devices: 50.6 us -> 51.7 us
  waiting for transfers between devices: 22.7 us -> 21.6 us
    pallas_call x3 -> x6, Pallas kernels: 4.91 us -> 6.84 us  [the longest x4 4.34 us: weight_parts(): pl.pallas_call(functools.partial(weight_kernel, targets), out_shape=[jax....]
    pallas_call x2, Pallas kernels: 9.13 us -> 7.58 us  [head_grads(): pl.pallas_call(functools.partial(later_kernel, dims, (distance,), last),...]
    pallas_call x1, Pallas kernels: 9.66 us -> 8.16 us  [head_grads(): pl.pallas_call(functools.partial(first_kernel, dims, (0, 1)), out_shape=[...]
    ppermute x4, starting transfers between devices: 7.74 us -> 9.08 us  [local(): lax.ppermute(piece, ('seq', 'dp'), slot_route(slot))]
    ppermute x29, waiting for transfers between devices: 16.7 us -> 15.5 us  [exchange(): lax.ppermute(value, axis, [(source, source ^ distance) for source in rang...]
  transfers between devices with their start and end apart: 33 -> 33, of which waited for: 11 -> 10; matrix products, arithmetic and copies ran while one was open for 0% -> 0% of each run, Pallas kernels for 20% -> 21%
where the time goes in v2:
time: 106 us; the launch traced here: 105 us
  starting transfers between devices  51.7 us (49%)
  Pallas kernels  27.4 us (26%)
  waiting for transfers between devices  21.6 us (20%)
  local copies, waits for them, and re-layouts  4.26 us (4%)
    ppermute x29, starting transfers between devices, exchange(): lax.ppermute(value, axis, [(source, source ^ distance) for source in rang...  42.6 us
    ppermute x29, waiting for transfers between devices, exchange(): lax.ppermute(value, axis, [(source, source ^ distance) for source in rang...  15.5 us
    ppermute x4, starting transfers between devices, local(): lax.ppermute(piece, ('seq', 'dp'), slot_route(slot))  9.08 us
    pallas_call x1, Pallas kernels, head_grads(): pl.pallas_call(functools.partial(first_kernel, dims, (0, 1)), out_shape=[...  8.16 us
    pallas_call x2, Pallas kernels, head_grads(): pl.pallas_call(functools.partial(later_kernel, dims, (distance,), last),...  7.58 us
    ppermute x4, waiting for transfers between devices, local(): lax.ppermute(piece, ('seq', 'dp'), slot_route(slot))  6.05 us
    pallas_call x4, Pallas kernels, weight_parts(): pl.pallas_call(functools.partial(weight_kernel, targets), out_shape=[jax....  4.34 us
    unnamed x18, local copies, waits for them, and re-layouts  4.26 us
  transfers between devices with their start and end apart: 33, of which 10 were waited for; matrix products, arithmetic and copies ran while one was open for 0% of the time, Pallas kernels for 21%

profile of v2, /device:TPU:0, one launch (start us, length us, event | category | flops | bytes accessed | tf_op | source)
XLA Modules:
  0.0 105.3 jit_solution(10170517792221185883)
XLA Ops:
  0.1 1.1 %copy-done.3 = bf16[1,256,1024]{2,1,0:T(8,128)(2,1)S(1)} copy-done((bf16[1,256,1024]{2,1,0:T(8,128)(2,1)S(1)}, bf16[1,256,1024]{2,1,0:T(8,128)(2,1)}, u32[]{:S(2)}) %copy-start.3) | copy-done | bytes 524312
  3.1 6.1 %collective-permute-start.2 = (bf16[2,256,128]{2,1,0:T(8,128)(2,1)S(1)}, bf16[2,256,128]{2,1,0:T(8,128)(2,1)S(1)}, u32[]{:S(2)}, u32[]{:S(2)}) collective-permute-start(bf16[2,256,128]{2,1,0:T(8,128)(2,1)S(1)} %get-tuple-element.76), channel_id=1, source_target_pairs={{0,14},{2,12},{4,10},{6,8},{8,6},{10,4},{12,2},{14,0},{1,15},{3,13... | collective-permute-start | bytes 393224 | tf_op jit(solution)/shard_map/ppermute | solution.py:22
  9.8 3.1 %collective-permute-start.8 = (bf16[2,256,128]{2,1,0:T(8,128)(2,1)S(1)}, bf16[2,256,128]{2,1,0:T(8,128)(2,1)S(1)}, u32[]{:S(2)}, u32[]{:S(2)}) collective-permute-start(bf16[2,256,128]{2,1,0:T(8,128)(2,1)S(1)} %get-tuple-element.95), channel_id=1, source_target_pairs={{0,6},{2,4},{4,2},{6,0},{8,14},{10,12},{12,10},{14,8},{1,7},{3,5},... | collective-permute-start | bytes 393224 | tf_op jit(solution)/shard_map/ppermute | solution.py:22
  15.8 5.2 %collective-permute-start.3 = (bf16[2,256,128]{2,1,0:T(8,128)(2,1)S(1)}, bf16[2,256,128]{2,1,0:T(8,128)(2,1)S(1)}, u32[]{:S(2)}, u32[]{:S(2)}) collective-permute-start(bf16[2,256,128]{2,1,0:T(8,128)(2,1)S(1)} %get-tuple-element.78), channel_id=1, source_target_pairs={{0,10},{2,8},{4,14},{6,12},{8,2},{10,0},{12,6},{14,4},{1,11},{3,9}... | collective-permute-start | bytes 393224 | tf_op jit(solution)/shard_map/ppermute | solution.py:22
  21.0 2.2 %collective-permute-start.10 = (bf16[2,256,128]{2,1,0:T(8,128)(2,1)S(1)}, bf16[2,256,128]{2,1,0:T(8,128)(2,1)S(1)}, u32[]{:S(2)}, u32[]{:S(2)}) collective-permute-start(bf16[2,256,128]{2,1,0:T(8,128)(2,1)S(1)} %get-tuple-element.100), channel_id=1, source_target_pairs={{0,8},{2,10},{4,12},{6,14},{8,0},{10,2},{12,4},{14,6},{1,9},{3,11}... | collective-permute-start | bytes 393224 | tf_op jit(solution)/shard_map/ppermute | solution.py:22
  23.2 3.5 %collective-permute-start.13 = (bf16[2,256,128]{2,1,0:T(8,128)(2,1)S(1)}, bf16[2,256,128]{2,1,0:T(8,128)(2,1)S(1)}, u32[]{:S(2)}, u32[]{:S(2)}) collective-permute-start(bf16[2,256,128]{2,1,0:T(8,128)(2,1)S(1)} %get-tuple-element.108), channel_id=1, source_target_pairs={{0,6},{2,4},{4,2},{6,0},{8,14},{10,12},{12,10},{14,8},{1,7},{3,5},... | collective-permute-start | bytes 393224 | tf_op jit(solution)/shard_map/ppermute | solution.py:22
  27.5 2.3 %collective-permute-done.3.refs_8_ = bf16[2,256,128]{2,1,0:T(8,128)(2,1)S(1)} collective-permute-done((bf16[2,256,128]{2,1,0:T(8,128)(2,1)S(1)}, bf16[2,256,128]{2,1,0:T(8,128)(2,1)S(1)}, u32[]{:S(2)}, u32[]{:S(2)}) %collective-permute-start.3) | collective-permute-done | bytes 131104 | tf_op jit(solution)/shard_map/ppermute | solution.py:22
  29.9 1.6 %collective-permute-done.10.refs_7_ = bf16[2,256,128]{2,1,0:T(8,128)(2,1)S(1)} collective-permute-done((bf16[2,256,128]{2,1,0:T(8,128)(2,1)S(1)}, bf16[2,256,128]{2,1,0:T(8,128)(2,1)S(1)}, u32[]{:S(2)}, u32[]{:S(2)}) %collective-permute-start.10) | collective-permute-done | bytes 131104 | tf_op jit(solution)/shard_map/ppermute | solution.py:22
  32.1 3.8 %collective-permute-start.15 = (bf16[2,256,128]{2,1,0:T(8,128)(2,1)S(1)}, bf16[2,256,128]{2,1,0:T(8,128)(2,1)S(1)}, u32[]{:S(2)}, u32[]{:S(2)}) collective-permute-start(bf16[2,256,128]{2,1,0:T(8,128)(2,1)S(1)} %get-tuple-element.113), channel_id=1, source_target_pairs={{0,10},{2,8},{4,14},{6,12},{8,2},{10,0},{12,6},{14,4},{1,11},{3,9}... | collective-permute-start | bytes 393224 | tf_op jit(solution)/shard_map/ppermute | solution.py:22
  35.9 2.6 %collective-permute-start.16 = (bf16[2,256,128]{2,1,0:T(8,128)(2,1)S(1)}, bf16[2,256,128]{2,1,0:T(8,128)(2,1)S(1)}, u32[]{:S(2)}, u32[]{:S(2)}) collective-permute-start(bf16[2,256,128]{2,1,0:T(8,128)(2,1)S(1)} %get-tuple-element.114), channel_id=1, source_target_pairs={{0,12},{2,14},{4,8},{6,10},{8,4},{10,6},{12,0},{14,2},{1,13},{3,15... | collective-permute-start | bytes 393224 | tf_op jit(solution)/shard_map/ppermute | solution.py:22
  38.5 8.2 %head_first.1 = (f32[2048,128]{1,0:T(8,128)S(1)}, bf16[2048,128]{1,0:T(8,128)(2,1)S(1)}, bf16[2048,128]{1,0:T(8,128)(2,1)S(1)}) custom-call(s32[3]{0:T(128)S(1)} %pad_add_fusion.place, bf16[256,1024]{1,0:T(8,128)(2,1)S(1)} %bitcast.10, bf16[256,1024]{1,0:T(8,128)(2,1)S(1)} %bitcast.12, bf16[256,1024]{1,0:T(8,128)(2,1)S(1)} %bitcast.14, ...), custom_call_target="tpu_custom_call" | custom-call | flops 13421772800 | bytes 2097152 | tf_op jit(solution)/shard_map/head_first/pallas_call | solution.py:332
  46.7 1.3 %collective-permute-start.4 = (bf16[2,256,128]{2,1,0:T(8,128)(2,1)S(1)}, bf16[2,256,128]{2,1,0:T(8,128)(2,1)S(1)}, u32[]{:S(2)}, u32[]{:S(2)}) collective-permute-start(bf16[2,256,128]{2,1,0:T(8,128)(2,1)S(1)} %get-tuple-element.85), channel_id=1, source_target_pairs={{0,14},{2,12},{4,10},{6,8},{8,6},{10,4},{12,2},{14,0},{1,15},{3,13... | collective-permute-start | bytes 393224 | tf_op jit(solution)/shard_map/ppermute | solution.py:22
  48.0 1.9 %collective-permute-done.15.refs_1_ = bf16[2,256,128]{2,1,0:T(8,128)(2,1)S(1)} collective-permute-done((bf16[2,256,128]{2,1,0:T(8,128)(2,1)S(1)}, bf16[2,256,128]{2,1,0:T(8,128)(2,1)S(1)}, u32[]{:S(2)}, u32[]{:S(2)}) %collective-permute-start.15) | collective-permute-done | bytes 131104 | tf_op jit(solution)/shard_map/ppermute | solution.py:22
  49.9 4.0 %head_later.2.before_ref = f32[2048,128]{1,0:T(8,128)S(1)} custom-call(s32[3]{0:T(128)S(1)} %pad_add_fusion.place, f32[2048,128]{1,0:T(8,128)S(1)} %get-tuple-element.109.before_ref, bf16[2048,128]{1,0:T(8,128)(2,1)S(1)} %get-tuple-element.110.key_ref, bf16[2048,128]{1,0:T(8,128)(2,1)S(1)} %get-tuple-element.111.value_ref, ...), custom_call_target="tpu_custom_call" | custom-call | flops 6710886400 | bytes 2097152 | tf_op jit(solution)/shard_map/head_later/pallas_call | solution.py:346
  53.9 1.1 %moved.3.input_ref = bf16[4,256,1024]{2,1,0:T(8,128)(2,1)S(1)} custom-call(s32[3]{0:T(128)S(1)} %pad_add_fusion.place, bf16[8,256,128]{2,1,0:T(8,128)(2,1)S(1)} %get-tuple-element.75.keep, bf16[8,256,128]{2,1,0:T(8,128)(2,1)S(1)} %collective-permute-done.1.keep_other, bf16[8,256,128]{2,1,0:T(8,128)(2,1)S(1)} %collective-permute-done.5.received, ...), custom_call_target="tpu_custom_call" | custom-call | tf_op jit(solution)/shard_map/moved/pallas_call | solution.py:111
  55.0 3.6 %head_later.3 = (bf16[512,128]{1,0:T(8,128)(2,1)S(1)}, bf16[512,128]{1,0:T(8,128)(2,1)S(1)}, bf16[512,128]{1,0:T(8,128)(2,1)S(1)}, bf16[512,128]{1,0:T(8,128)(2,1)S(1)}) custom-call(s32[3]{0:T(128)S(1)} %pad_add_fusion.place, f32[2048,128]{1,0:T(8,128)S(1)} %head_later.2.before_ref, bf16[2048,128]{1,0:T(8,128)(2,1)S(1)} %get-tuple-element.110.key_ref, ...), custom_call_target="tpu_custom_call" | custom-call | flops 6710886400 | bytes 2097152 | tf_op jit(solution)/shard_map/head_later/pallas_call | solution.py:346
  58.7 3.6 %collective-permute-start.19 = (bf16[512,128]{1,0:T(8,128)(2,1)S(1)}, bf16[512,128]{1,0:T(8,128)(2,1)S(1)}, u32[]{:S(2)}, u32[]{:S(2)}) collective-permute-start(bf16[512,128]{1,0:T(8,128)(2,1)S(1)} %get-tuple-element.118), channel_id=1, source_target_pairs={{0,4},{1,0},{2,6},{3,2},{4,5},{5,1},{6,7},{7,3},{8,12},{9,8},{10,1... | collective-permute-start | bytes 393224 | tf_op jit(solution)/shard_map/ppermute | solution.py:564
  63.0 4.8 %collective-permute-start.18 = (bf16[512,128]{1,0:T(8,128)(2,1)S(1)}, bf16[512,128]{1,0:T(8,128)(2,1)S(1)}, u32[]{:S(2)}, u32[]{:S(2)}) collective-permute-start(bf16[512,128]{1,0:T(8,128)(2,1)S(1)} %get-tuple-element.117), channel_id=1, source_target_pairs={{0,12},{1,8},{2,14},{3,10},{4,13},{5,9},{6,15},{7,11},{8,4},{9,0},... | collective-permute-start | bytes 393224 | tf_op jit(solution)/shard_map/ppermute | solution.py:564
  67.8 1.1 %collective-permute-start.21 = (bf16[512,128]{1,0:T(8,128)(2,1)S(1)}, bf16[512,128]{1,0:T(8,128)(2,1)S(1)}, u32[]{:S(2)}, u32[]{:S(2)}) collective-permute-start(bf16[512,128]{1,0:T(8,128)(2,1)S(1)} %collective-permute-done.19.refs_2_), channel_id=1, source_target_pairs={{0,2},{2,0},{4,6},{6,4},{8,10},{10,8},{12,14},{14,12},{1,3},{3,1},... | collective-permute-start | bytes 393224 | tf_op jit(solution)/shard_map/ppermute | solution.py:22
  69.8 4.6 %collective-permute-done.17.refs_0_ = bf16[512,128]{1,0:T(8,128)(2,1)S(1)} collective-permute-done((bf16[512,128]{1,0:T(8,128)(2,1)S(1)}, bf16[512,128]{1,0:T(8,128)(2,1)S(1)}, u32[]{:S(2)}, u32[]{:S(2)}) %collective-permute-start.17) | collective-permute-done | bytes 131104 | tf_op jit(solution)/shard_map/ppermute | solution.py:564
  74.4 1.4 %collective-permute-done.18.refs_1_ = bf16[512,128]{1,0:T(8,128)(2,1)S(1)} collective-permute-done((bf16[512,128]{1,0:T(8,128)(2,1)S(1)}, bf16[512,128]{1,0:T(8,128)(2,1)S(1)}, u32[]{:S(2)}, u32[]{:S(2)}) %collective-permute-start.18) | collective-permute-done | bytes 131104 | tf_op jit(solution)/shard_map/ppermute | solution.py:564
  77.2 1.8 %collective-permute-start.23 = (bf16[512,128]{1,0:T(8,128)(2,1)S(1)}, bf16[512,128]{1,0:T(8,128)(2,1)S(1)}, u32[]{:S(2)}, u32[]{:S(2)}) collective-permute-start(bf16[512,128]{1,0:T(8,128)(2,1)S(1)} %collective-permute-done.17.refs_0_), channel_id=1, source_target_pairs={{0,2},{2,0},{4,6},{6,4},{8,10},{10,8},{12,14},{14,12},{1,3},{3,1},... | collective-permute-start | bytes 393224 | tf_op jit(solution)/shard_map/ppermute | solution.py:22
  79.2 2.5 %collective-permute-start.30 = (bf16[256,256]{1,0:T(8,128)(2,1)S(1)}, bf16[256,256]{1,0:T(8,128)(2,1)S(1)}, u32[]{:S(2)}, u32[]{:S(2)}) collective-permute-start(bf16[256,256]{1,0:T(8,128)(2,1)S(1)} %get-tuple-element.137), channel_id=1, source_target_pairs={{0,8},{2,10},{4,12},{6,14},{8,0},{10,2},{12,4},{14,6},{1,9},{3,11}... | collective-permute-start | bytes 393224 | tf_op jit(solution)/shard_map/ppermute | solution.py:22
  82.8 1.7 %collective-permute-start.31 = (bf16[256,256]{1,0:T(8,128)(2,1)S(1)}, bf16[256,256]{1,0:T(8,128)(2,1)S(1)}, u32[]{:S(2)}, u32[]{:S(2)}) collective-permute-start(bf16[256,256]{1,0:T(8,128)(2,1)S(1)} %get-tuple-element.138), channel_id=1, source_target_pairs={{0,4},{2,6},{4,0},{6,2},{8,12},{10,14},{12,8},{14,10},{1,5},{3,7},... | collective-permute-start | bytes 393224 | tf_op jit(solution)/shard_map/ppermute | solution.py:22
  85.4 1.1 %weight_parts.5 = (bf16[256,256]{1,0:T(8,128)(2,1)S(1)}, f32[256,256]{1,0:T(8,128)S(1)}) custom-call(s32[3]{0:T(128)S(1)} %pad_add_fusion.place, bf16[4,256,1024]{2,1,0:T(8,128)(2,1)S(1)} %moved.3.input_ref, bf16[512,128]{1,0:T(8,128)(2,1)S(1)} %collective-permute-done.23.refs_0_, bf16[512,128]{1,0:T(8,128)(2,1)S(1)} %collective-permute-done.24.refs_1_, ...), custom_call_target="tpu_custom_call" | custom-call | flops 268435456 | bytes 1572864 | tf_op jit(solution)/shard_map/weight_parts/pallas_call | solution.py:382
  86.5 1.1 %weight_parts.6 = (bf16[256,256]{1,0:T(8,128)(2,1)S(1)}, bf16[256,256]{1,0:T(8,128)(2,1)S(1)}) custom-call(s32[3]{0:T(128)S(1)} %pad_add_fusion.place, bf16[4,256,1024]{2,1,0:T(8,128)(2,1)S(1)} %moved.3.input_ref, bf16[512,128]{1,0:T(8,128)(2,1)S(1)} %collective-permute-done.23.refs_0_, bf16[512,128]{1,0:T(8,128)(2,1)S(1)} %collective-permute-done.24.refs_1_, ...), custom_call_target="tpu_custom_call" | custom-call | flops 268435456 | bytes 1572864 | tf_op jit(solution)/shard_map/weight_parts/pallas_call | solution.py:382
  87.6 2.5 %collective-permute-start.26 = (bf16[256,256]{1,0:T(8,128)(2,1)S(1)}, bf16[256,256]{1,0:T(8,128)(2,1)S(1)}, u32[]{:S(2)}, u32[]{:S(2)}) collective-permute-start(bf16[256,256]{1,0:T(8,128)(2,1)S(1)} %get-tuple-element.130), channel_id=1, source_target_pairs={{0,12},{2,14},{4,8},{6,10},{8,4},{10,6},{12,0},{14,2},{1,13},{3,15... | collective-permute-start | bytes 393224 | tf_op jit(solution)/shard_map/ppermute | solution.py:22
  90.1 2.4 %collective-permute-start.27 = (bf16[256,256]{1,0:T(8,128)(2,1)S(1)}, bf16[256,256]{1,0:T(8,128)(2,1)S(1)}, u32[]{:S(2)}, u32[]{:S(2)}) collective-permute-start(bf16[256,256]{1,0:T(8,128)(2,1)S(1)} %get-tuple-element.131), channel_id=1, source_target_pairs={{0,8},{2,10},{4,12},{6,14},{8,0},{10,2},{12,4},{14,6},{1,9},{3,11}... | collective-permute-start | bytes 393224 | tf_op jit(solution)/shard_map/ppermute | solution.py:22
  93.2 2.8 %collective-permute-done.26.refs_1_ = bf16[256,256]{1,0:T(8,128)(2,1)S(1)} collective-permute-done((bf16[256,256]{1,0:T(8,128)(2,1)S(1)}, bf16[256,256]{1,0:T(8,128)(2,1)S(1)}, u32[]{:S(2)}, u32[]{:S(2)}) %collective-permute-start.26) | collective-permute-done | bytes 131104 | tf_op jit(solution)/shard_map/ppermute | solution.py:22
  96.0 6.0 %collective-permute-done.27.refs_2_ = bf16[256,256]{1,0:T(8,128)(2,1)S(1)} collective-permute-done((bf16[256,256]{1,0:T(8,128)(2,1)S(1)}, bf16[256,256]{1,0:T(8,128)(2,1)S(1)}, u32[]{:S(2)}, u32[]{:S(2)}) %collective-permute-start.27) | collective-permute-done | bytes 131104 | tf_op jit(solution)/shard_map/ppermute | solution.py:22
  102.6 1.2 %placed.2.refs_2_ = f32[128,1024]{1,0:T(8,128)} custom-call(s32[3]{0:T(128)S(1)} %pad_add_fusion.place, f32[128,256]{1,0:T(8,128)S(1)} %get-tuple-element.139.refs_0_, f32[128,256]{1,0:T(8,128)S(1)} %collective-permute-done.32.refs_1_), custom_call_target="tpu_custom_call" | custom-call | tf_op jit(solution)/shard_map/placed/pallas_call | solution.py:444
  103.9 1.2 %placed.3 = f32[128,1024]{1,0:T(8,128)} custom-call(s32[3]{0:T(128)S(1)} %pad_add_fusion.place, f32[128,256]{1,0:T(8,128)S(1)} %get-tuple-element.133.refs_0_, f32[128,256]{1,0:T(8,128)S(1)} %collective-permute-done.29.refs_1_, f32[128,1024]{1,0:T(8,128)} %placed.2.refs_2_), custom_call_target="tpu_custom_call", output_to_operand_aliasing={{}: (3, {})} | custom-call | tf_op jit(solution)/shard_map/placed/pallas_call | solution.py:444
  (68 shorter events, 13.5 us)
Async XLA Ops:
  3.1 12.7 %collective-permute-start.2 = (bf16[2,256,128]{2,1,0:T(8,128)(2,1)S(1)}, bf16[2,256,128]{2,1,0:T(8,128)(2,1)S(1)}, u32[]{:S(2)}, u32[]{:S(2)}) collective-permute-start(bf16[2,256,128]{2,1,0:T(8,128)(2,1)S(1)} %get-tuple-element.76), channel_id=1, source_target_pairs={{0,14},{2,12},{4,10},{6,8},{8,6},{10,4},{12,2},{14,0},{1,15},{3,13... | collective-permute-start | bytes 393224 | tf_op jit(solution)/shard_map/ppermute | solution.py:22
  9.1 11.9 %collective-permute-start = (bf16[2,256,128]{2,1,0:T(8,128)(2,1)S(1)}, bf16[2,256,128]{2,1,0:T(8,128)(2,1)S(1)}, u32[]{:S(2)}, u32[]{:S(2)}) collective-permute-start(bf16[2,256,128]{2,1,0:T(8,128)(2,1)S(1)} %get-tuple-element.73), channel_id=1, source_target_pairs={{0,2},{2,0},{4,6},{6,4},{8,10},{10,8},{12,14},{14,12},{1,3},{3,1},... | collective-permute-start | bytes 393224 | tf_op jit(solution)/shard_map/ppermute | solution.py:22
  9.6 11.4 %collective-permute-start.9 = (bf16[2,256,128]{2,1,0:T(8,128)(2,1)S(1)}, bf16[2,256,128]{2,1,0:T(8,128)(2,1)S(1)}, u32[]{:S(2)}, u32[]{:S(2)}) collective-permute-start(bf16[2,256,128]{2,1,0:T(8,128)(2,1)S(1)} %get-tuple-element.98), channel_id=1, source_target_pairs={{0,12},{2,14},{4,8},{6,10},{8,4},{10,6},{12,0},{14,2},{1,13},{3,15... | collective-permute-start | bytes 393224 | tf_op jit(solution)/shard_map/ppermute | solution.py:22
  9.8 13.4 %collective-permute-start.7 = (bf16[2,256,128]{2,1,0:T(8,128)(2,1)S(1)}, bf16[2,256,128]{2,1,0:T(8,128)(2,1)S(1)}, u32[]{:S(2)}, u32[]{:S(2)}) collective-permute-start(bf16[2,256,128]{2,1,0:T(8,128)(2,1)S(1)} %get-tuple-element.92), channel_id=1, source_target_pairs={{0,4},{2,6},{4,0},{6,2},{8,12},{10,14},{12,8},{14,10},{1,5},{3,7},... | collective-permute-start | bytes 393224 | tf_op jit(solution)/shard_map/ppermute | solution.py:22
  9.8 13.4 %collective-permute-start.8 = (bf16[2,256,128]{2,1,0:T(8,128)(2,1)S(1)}, bf16[2,256,128]{2,1,0:T(8,128)(2,1)S(1)}, u32[]{:S(2)}, u32[]{:S(2)}) collective-permute-start(bf16[2,256,128]{2,1,0:T(8,128)(2,1)S(1)} %get-tuple-element.95), channel_id=1, source_target_pairs={{0,6},{2,4},{4,2},{6,0},{8,14},{10,12},{12,10},{14,8},{1,7},{3,5},... | collective-permute-start | bytes 393224 | tf_op jit(solution)/shard_map/ppermute | solution.py:22
  15.8 14.1 %collective-permute-start.3 = (bf16[2,256,128]{2,1,0:T(8,128)(2,1)S(1)}, bf16[2,256,128]{2,1,0:T(8,128)(2,1)S(1)}, u32[]{:S(2)}, u32[]{:S(2)}) collective-permute-start(bf16[2,256,128]{2,1,0:T(8,128)(2,1)S(1)} %get-tuple-element.78), channel_id=1, source_target_pairs={{0,10},{2,8},{4,14},{6,12},{8,2},{10,0},{12,6},{14,4},{1,11},{3,9}... | collective-permute-start | bytes 393224 | tf_op jit(solution)/shard_map/ppermute | solution.py:22
  21.0 10.5 %collective-permute-start.10 = (bf16[2,256,128]{2,1,0:T(8,128)(2,1)S(1)}, bf16[2,256,128]{2,1,0:T(8,128)(2,1)S(1)}, u32[]{:S(2)}, u32[]{:S(2)}) collective-permute-start(bf16[2,256,128]{2,1,0:T(8,128)(2,1)S(1)} %get-tuple-element.100), channel_id=1, source_target_pairs={{0,8},{2,10},{4,12},{6,14},{8,0},{10,2},{12,4},{14,6},{1,9},{3,11}... | collective-permute-start | bytes 393224 | tf_op jit(solution)/shard_map/ppermute | solution.py:22
  23.2 8.9 %collective-permute-start.11 = (bf16[2,256,128]{2,1,0:T(8,128)(2,1)S(1)}, bf16[2,256,128]{2,1,0:T(8,128)(2,1)S(1)}, u32[]{:S(2)}, u32[]{:S(2)}) collective-permute-start(bf16[2,256,128]{2,1,0:T(8,128)(2,1)S(1)} %get-tuple-element.106), channel_id=1, source_target_pairs={{0,2},{2,0},{4,6},{6,4},{8,10},{10,8},{12,14},{14,12},{1,3},{3,1},... | collective-permute-start | bytes 393224 | tf_op jit(solution)/shard_map/ppermute | solution.py:22
  23.2 8.9 %collective-permute-start.12 = (bf16[2,256,128]{2,1,0:T(8,128)(2,1)S(1)}, bf16[2,256,128]{2,1,0:T(8,128)(2,1)S(1)}, u32[]{:S(2)}, u32[]{:S(2)}) collective-permute-start(bf16[2,256,128]{2,1,0:T(8,128)(2,1)S(1)} %get-tuple-element.107), channel_id=1, source_target_pairs={{0,4},{2,6},{4,0},{6,2},{8,12},{10,14},{12,8},{14,10},{1,5},{3,7},... | collective-permute-start | bytes 393224 | tf_op jit(solution)/shard_map/ppermute | solution.py:22
  23.2 12.7 %collective-permute-start.13 = (bf16[2,256,128]{2,1,0:T(8,128)(2,1)S(1)}, bf16[2,256,128]{2,1,0:T(8,128)(2,1)S(1)}, u32[]{:S(2)}, u32[]{:S(2)}) collective-permute-start(bf16[2,256,128]{2,1,0:T(8,128)(2,1)S(1)} %get-tuple-element.108), channel_id=1, source_target_pairs={{0,6},{2,4},{4,2},{6,0},{8,14},{10,12},{12,10},{14,8},{1,7},{3,5},... | collective-permute-start | bytes 393224 | tf_op jit(solution)/shard_map/ppermute | solution.py:22
  29.9 16.8 %collective-permute-start.1 = (bf16[8,256,128]{2,1,0:T(8,128)(2,1)S(1)}, bf16[8,256,128]{2,1,0:T(8,128)(2,1)S(1)}, u32[]{:S(2)}, u32[]{:S(2)}) collective-permute-start(bf16[8,256,128]{2,1,0:T(8,128)(2,1)S(1)} %get-tuple-element.75.keep), channel_id=1, source_target_pairs={{0,1},{1,0},{2,3},{3,2},{4,5},{5,4},{6,7},{7,6},{8,9},{9,8},{10,11... | collective-permute-start | bytes 1572872 | tf_op jit(solution)/shard_map/ppermute | solution.py:22
  31.5 16.5 %collective-permute-start.5 = (bf16[8,256,128]{2,1,0:T(8,128)(2,1)S(1)}, bf16[8,256,128]{2,1,0:T(8,128)(2,1)S(1)}, u32[]{:S(2)}, u32[]{:S(2)}) collective-permute-start(bf16[8,256,128]{2,1,0:T(8,128)(2,1)S(1)} %get-tuple-element.87), channel_id=1, source_target_pairs={{0,2},{2,0},{4,6},{6,4},{8,10},{10,8},{12,14},{14,12},{1,3},{3,1},... | collective-permute-start | bytes 1572872 | tf_op jit(solution)/shard_map/ppermute | solution.py:22
  32.1 15.9 %collective-permute-start.14 = (bf16[2,256,128]{2,1,0:T(8,128)(2,1)S(1)}, bf16[2,256,128]{2,1,0:T(8,128)(2,1)S(1)}, u32[]{:S(2)}, u32[]{:S(2)}) collective-permute-start(bf16[2,256,128]{2,1,0:T(8,128)(2,1)S(1)} %get-tuple-element.112), channel_id=1, source_target_pairs={{0,8},{2,10},{4,12},{6,14},{8,0},{10,2},{12,4},{14,6},{1,9},{3,11}... | collective-permute-start | bytes 393224 | tf_op jit(solution)/shard_map/ppermute | solution.py:22
  32.1 17.8 %collective-permute-start.15 = (bf16[2,256,128]{2,1,0:T(8,128)(2,1)S(1)}, bf16[2,256,128]{2,1,0:T(8,128)(2,1)S(1)}, u32[]{:S(2)}, u32[]{:S(2)}) collective-permute-start(bf16[2,256,128]{2,1,0:T(8,128)(2,1)S(1)} %get-tuple-element.113), channel_id=1, source_target_pairs={{0,10},{2,8},{4,14},{6,12},{8,2},{10,0},{12,6},{14,4},{1,11},{3,9}... | collective-permute-start | bytes 393224 | tf_op jit(solution)/shard_map/ppermute | solution.py:22
  35.9 19.1 %collective-permute-start.16 = (bf16[2,256,128]{2,1,0:T(8,128)(2,1)S(1)}, bf16[2,256,128]{2,1,0:T(8,128)(2,1)S(1)}, u32[]{:S(2)}, u32[]{:S(2)}) collective-permute-start(bf16[2,256,128]{2,1,0:T(8,128)(2,1)S(1)} %get-tuple-element.114), channel_id=1, source_target_pairs={{0,12},{2,14},{4,8},{6,10},{8,4},{10,6},{12,0},{14,2},{1,13},{3,15... | collective-permute-start | bytes 393224 | tf_op jit(solution)/shard_map/ppermute | solution.py:22
  46.7 8.3 %collective-permute-start.4 = (bf16[2,256,128]{2,1,0:T(8,128)(2,1)S(1)}, bf16[2,256,128]{2,1,0:T(8,128)(2,1)S(1)}, u32[]{:S(2)}, u32[]{:S(2)}) collective-permute-start(bf16[2,256,128]{2,1,0:T(8,128)(2,1)S(1)} %get-tuple-element.85), channel_id=1, source_target_pairs={{0,14},{2,12},{4,10},{6,8},{8,6},{10,4},{12,2},{14,0},{1,15},{3,13... | collective-permute-start | bytes 393224 | tf_op jit(solution)/shard_map/ppermute | solution.py:22
  48.0 5.9 %collective-permute-start.6 = (bf16[8,256,128]{2,1,0:T(8,128)(2,1)S(1)}, bf16[8,256,128]{2,1,0:T(8,128)(2,1)S(1)}, u32[]{:S(2)}, u32[]{:S(2)}) collective-permute-start(bf16[8,256,128]{2,1,0:T(8,128)(2,1)S(1)} %collective-permute-done.5.received), channel_id=1, source_target_pairs={{0,1},{1,0},{2,3},{3,2},{4,5},{5,4},{6,7},{7,6},{8,9},{9,8},{10,11... | collective-permute-start | bytes 1572872 | tf_op jit(solution)/shard_map/ppermute | solution.py:22
  58.7 9.1 %collective-permute-start.19 = (bf16[512,128]{1,0:T(8,128)(2,1)S(1)}, bf16[512,128]{1,0:T(8,128)(2,1)S(1)}, u32[]{:S(2)}, u32[]{:S(2)}) collective-permute-start(bf16[512,128]{1,0:T(8,128)(2,1)S(1)} %get-tuple-element.118), channel_id=1, source_target_pairs={{0,4},{1,0},{2,6},{3,2},{4,5},{5,1},{6,7},{7,3},{8,12},{9,8},{10,1... | collective-permute-start | bytes 393224 | tf_op jit(solution)/shard_map/ppermute | solution.py:564
  62.2 6.6 %collective-permute-start.20 = (bf16[512,128]{1,0:T(8,128)(2,1)S(1)}, bf16[512,128]{1,0:T(8,128)(2,1)S(1)}, u32[]{:S(2)}, u32[]{:S(2)}) collective-permute-start(bf16[512,128]{1,0:T(8,128)(2,1)S(1)} %get-tuple-element.119), channel_id=1, source_target_pairs={{0,0},{1,4},{2,2},{3,6},{4,1},{5,5},{6,3},{7,7},{8,8},{9,12},{10,1... | collective-permute-start | bytes 393224 | tf_op jit(solution)/shard_map/ppermute | solution.py:564
  62.9 11.5 %collective-permute-start.17 = (bf16[512,128]{1,0:T(8,128)(2,1)S(1)}, bf16[512,128]{1,0:T(8,128)(2,1)S(1)}, u32[]{:S(2)}, u32[]{:S(2)}) collective-permute-start(bf16[512,128]{1,0:T(8,128)(2,1)S(1)} %get-tuple-element.116), channel_id=1, source_target_pairs={{0,8},{1,12},{2,10},{3,14},{4,9},{5,13},{6,11},{7,15},{8,0},{9,4},... | collective-permute-start | bytes 393224 | tf_op jit(solution)/shard_map/ppermute | solution.py:564
  63.0 12.9 %collective-permute-start.18 = (bf16[512,128]{1,0:T(8,128)(2,1)S(1)}, bf16[512,128]{1,0:T(8,128)(2,1)S(1)}, u32[]{:S(2)}, u32[]{:S(2)}) collective-permute-start(bf16[512,128]{1,0:T(8,128)(2,1)S(1)} %get-tuple-element.117), channel_id=1, source_target_pairs={{0,12},{1,8},{2,14},{3,10},{4,13},{5,9},{6,15},{7,11},{8,4},{9,0},... | collective-permute-start | bytes 393224 | tf_op jit(solution)/shard_map/ppermute | solution.py:564
  67.8 9.4 %collective-permute-start.21 = (bf16[512,128]{1,0:T(8,128)(2,1)S(1)}, bf16[512,128]{1,0:T(8,128)(2,1)S(1)}, u32[]{:S(2)}, u32[]{:S(2)}) collective-permute-start(bf16[512,128]{1,0:T(8,128)(2,1)S(1)} %collective-permute-done.19.refs_2_), channel_id=1, source_target_pairs={{0,2},{2,0},{4,6},{6,4},{8,10},{10,8},{12,14},{14,12},{1,3},{3,1},... | collective-permute-start | bytes 393224 | tf_op jit(solution)/shard_map/ppermute | solution.py:22
  68.8 8.4 %collective-permute-start.22 = (bf16[512,128]{1,0:T(8,128)(2,1)S(1)}, bf16[512,128]{1,0:T(8,128)(2,1)S(1)}, u32[]{:S(2)}, u32[]{:S(2)}) collective-permute-start(bf16[512,128]{1,0:T(8,128)(2,1)S(1)} %collective-permute-done.20.refs_3_), channel_id=1, source_target_pairs={{0,2},{2,0},{4,6},{6,4},{8,10},{10,8},{12,14},{14,12},{1,3},{3,1},... | collective-permute-start | bytes 393224 | tf_op jit(solution)/shard_map/ppermute | solution.py:22
  76.9 8.3 %collective-permute-start.25 = (bf16[256,256]{1,0:T(8,128)(2,1)S(1)}, bf16[256,256]{1,0:T(8,128)(2,1)S(1)}, u32[]{:S(2)}, u32[]{:S(2)}) collective-permute-start(bf16[256,256]{1,0:T(8,128)(2,1)S(1)} %get-tuple-element.124), channel_id=1, source_target_pairs={{0,12},{2,14},{4,8},{6,10},{8,4},{10,6},{12,0},{14,2},{1,13},{3,15... | collective-permute-start | bytes 393224 | tf_op jit(solution)/shard_map/ppermute | solution.py:22
  77.2 8.0 %collective-permute-start.23 = (bf16[512,128]{1,0:T(8,128)(2,1)S(1)}, bf16[512,128]{1,0:T(8,128)(2,1)S(1)}, u32[]{:S(2)}, u32[]{:S(2)}) collective-permute-start(bf16[512,128]{1,0:T(8,128)(2,1)S(1)} %collective-permute-done.17.refs_0_), channel_id=1, source_target_pairs={{0,2},{2,0},{4,6},{6,4},{8,10},{10,8},{12,14},{14,12},{1,3},{3,1},... | collective-permute-start | bytes 393224 | tf_op jit(solution)/shard_map/ppermute | solution.py:22
  79.0 6.3 %collective-permute-start.24 = (bf16[512,128]{1,0:T(8,128)(2,1)S(1)}, bf16[512,128]{1,0:T(8,128)(2,1)S(1)}, u32[]{:S(2)}, u32[]{:S(2)}) collective-permute-start(bf16[512,128]{1,0:T(8,128)(2,1)S(1)} %collective-permute-done.18.refs_1_), channel_id=1, source_target_pairs={{0,2},{2,0},{4,6},{6,4},{8,10},{10,8},{12,14},{14,12},{1,3},{3,1},... | collective-permute-start | bytes 393224 | tf_op jit(solution)/shard_map/ppermute | solution.py:22
  79.2 13.3 %collective-permute-start.30 = (bf16[256,256]{1,0:T(8,128)(2,1)S(1)}, bf16[256,256]{1,0:T(8,128)(2,1)S(1)}, u32[]{:S(2)}, u32[]{:S(2)}) collective-permute-start(bf16[256,256]{1,0:T(8,128)(2,1)S(1)} %get-tuple-element.137), channel_id=1, source_target_pairs={{0,8},{2,10},{4,12},{6,14},{8,0},{10,2},{12,4},{14,6},{1,9},{3,11}... | collective-permute-start | bytes 393224 | tf_op jit(solution)/shard_map/ppermute | solution.py:22
  82.8 9.7 %collective-permute-start.31 = (bf16[256,256]{1,0:T(8,128)(2,1)S(1)}, bf16[256,256]{1,0:T(8,128)(2,1)S(1)}, u32[]{:S(2)}, u32[]{:S(2)}) collective-permute-start(bf16[256,256]{1,0:T(8,128)(2,1)S(1)} %get-tuple-element.138), channel_id=1, source_target_pairs={{0,4},{2,6},{4,0},{6,2},{8,12},{10,14},{12,8},{14,10},{1,5},{3,7},... | collective-permute-start | bytes 393224 | tf_op jit(solution)/shard_map/ppermute | solution.py:22
  87.6 8.4 %collective-permute-start.26 = (bf16[256,256]{1,0:T(8,128)(2,1)S(1)}, bf16[256,256]{1,0:T(8,128)(2,1)S(1)}, u32[]{:S(2)}, u32[]{:S(2)}) collective-permute-start(bf16[256,256]{1,0:T(8,128)(2,1)S(1)} %get-tuple-element.130), channel_id=1, source_target_pairs={{0,12},{2,14},{4,8},{6,10},{8,4},{10,6},{12,0},{14,2},{1,13},{3,15... | collective-permute-start | bytes 393224 | tf_op jit(solution)/shard_map/ppermute | solution.py:22
  90.1 11.8 %collective-permute-start.27 = (bf16[256,256]{1,0:T(8,128)(2,1)S(1)}, bf16[256,256]{1,0:T(8,128)(2,1)S(1)}, u32[]{:S(2)}, u32[]{:S(2)}) collective-permute-start(bf16[256,256]{1,0:T(8,128)(2,1)S(1)} %get-tuple-element.131), channel_id=1, source_target_pairs={{0,8},{2,10},{4,12},{6,14},{8,0},{10,2},{12,4},{14,6},{1,9},{3,11}... | collective-permute-start | bytes 393224 | tf_op jit(solution)/shard_map/ppermute | solution.py:22
  92.5 9.4 %collective-permute-start.28 = (bf16[256,256]{1,0:T(8,128)(2,1)S(1)}, bf16[256,256]{1,0:T(8,128)(2,1)S(1)}, u32[]{:S(2)}, u32[]{:S(2)}) collective-permute-start(bf16[256,256]{1,0:T(8,128)(2,1)S(1)} %get-tuple-element.132), channel_id=1, source_target_pairs={{0,4},{2,6},{4,0},{6,2},{8,12},{10,14},{12,8},{14,10},{1,5},{3,7},... | collective-permute-start | bytes 393224 | tf_op jit(solution)/shard_map/ppermute | solution.py:22
  93.1 9.5 %collective-permute-start.32 = (f32[128,256]{1,0:T(8,128)S(1)}, f32[128,256]{1,0:T(8,128)S(1)}, u32[]{:S(2)}, u32[]{:S(2)}) collective-permute-start(f32[128,256]{1,0:T(8,128)S(1)} %get-tuple-element.140), channel_id=1, source_target_pairs={{0,1},{1,0},{2,3},{3,2},{4,5},{5,4},{6,7},{7,6},{8,9},{9,8},{10,11... | collective-permute-start | bytes 393224 | tf_op jit(solution)/shard_map/ppermute | solution.py:22
  (10 other events, 126.5 us)

commit v3 on v2

--- a/solution.py
+++ b/solution.py
@@ -589,6 +589,8 @@
     def spread(pieces):
         low = jnp.bfloat16
         across = weight_parts(place, inputs, pieces, (3, 2), (low, low))
+        held = after(*across, *pieces)
+        across, pieces = held[:2], held[2:]
         beside, total = weight_parts(place, inputs, pieces, (1, 0), (low, jnp.float32))
         parts = zip((3, 2, 1), (*across, beside))
         return [total] + [exchange(part, "seq", 2 * distance) for distance, part in parts]

time: 106 us -> 105 us (level)
  no operation moved by 1% of the time
where the time goes in v3:
time: 105 us
  starting transfers between devices  51.7 us (49%)
  Pallas kernels  27.4 us (26%)
  waiting for transfers between devices  21.1 us (20%)
  local copies, waits for them, and re-layouts  4.26 us (4%)
    ppermute x29, starting transfers between devices, exchange(): lax.ppermute(value, axis, [(source, source ^ distance) for source in rang...  42.6 us
    ppermute x29, waiting for transfers between devices, exchange(): lax.ppermute(value, axis, [(source, source ^ distance) for source in rang...  15 us
    ppermute x4, starting transfers between devices, local(): lax.ppermute(piece, ('seq', 'dp'), slot_route(slot))  9.08 us
    pallas_call x1, Pallas kernels, head_grads(): pl.pallas_call(functools.partial(first_kernel, dims, (0, 1)), out_shape=[...  8.16 us
    pallas_call x2, Pallas kernels, head_grads(): pl.pallas_call(functools.partial(later_kernel, dims, (distance,), last),...  7.58 us
    ppermute x4, waiting for transfers between devices, local(): lax.ppermute(piece, ('seq', 'dp'), slot_route(slot))  6.05 us
    pallas_call x4, Pallas kernels, weight_parts(): pl.pallas_call(functools.partial(weight_kernel, targets), out_shape=[jax....  4.34 us
    unnamed x18, local copies, waits for them, and re-layouts  4.26 us
  transfers between devices with their start and end apart: 33, of which 10 were waited for; matrix products, arithmetic and copies ran while one was open for 0% of the time, Pallas kernels for 21%

profile of v3, /device:TPU:0, one launch (start us, length us, event | category | flops | bytes accessed | tf_op | source)
XLA Modules:
  0.0 104.9 jit_solution(18429057418513903426)
XLA Ops:
  0.1 1.1 %copy-done.3 = bf16[1,256,1024]{2,1,0:T(8,128)(2,1)S(1)} copy-done((bf16[1,256,1024]{2,1,0:T(8,128)(2,1)S(1)}, bf16[1,256,1024]{2,1,0:T(8,128)(2,1)}, u32[]{:S(2)}) %copy-start.3) | copy-done | bytes 524312
  3.1 6.1 %collective-permute-start.2 = (bf16[2,256,128]{2,1,0:T(8,128)(2,1)S(1)}, bf16[2,256,128]{2,1,0:T(8,128)(2,1)S(1)}, u32[]{:S(2)}, u32[]{:S(2)}) collective-permute-start(bf16[2,256,128]{2,1,0:T(8,128)(2,1)S(1)} %get-tuple-element.88), channel_id=1, source_target_pairs={{0,14},{2,12},{4,10},{6,8},{8,6},{10,4},{12,2},{14,0},{1,15},{3,13... | collective-permute-start | bytes 393224 | tf_op jit(solution)/shard_map/ppermute | solution.py:22
  9.8 3.1 %collective-permute-start.8 = (bf16[2,256,128]{2,1,0:T(8,128)(2,1)S(1)}, bf16[2,256,128]{2,1,0:T(8,128)(2,1)S(1)}, u32[]{:S(2)}, u32[]{:S(2)}) collective-permute-start(bf16[2,256,128]{2,1,0:T(8,128)(2,1)S(1)} %get-tuple-element.107), channel_id=1, source_target_pairs={{0,6},{2,4},{4,2},{6,0},{8,14},{10,12},{12,10},{14,8},{1,7},{3,5},... | collective-permute-start | bytes 393224 | tf_op jit(solution)/shard_map/ppermute | solution.py:22
  15.8 5.2 %collective-permute-start.3 = (bf16[2,256,128]{2,1,0:T(8,128)(2,1)S(1)}, bf16[2,256,128]{2,1,0:T(8,128)(2,1)S(1)}, u32[]{:S(2)}, u32[]{:S(2)}) collective-permute-start(bf16[2,256,128]{2,1,0:T(8,128)(2,1)S(1)} %get-tuple-element.90), channel_id=1, source_target_pairs={{0,10},{2,8},{4,14},{6,12},{8,2},{10,0},{12,6},{14,4},{1,11},{3,9}... | collective-permute-start | bytes 393224 | tf_op jit(solution)/shard_map/ppermute | solution.py:22
  21.0 2.2 %collective-permute-start.10 = (bf16[2,256,128]{2,1,0:T(8,128)(2,1)S(1)}, bf16[2,256,128]{2,1,0:T(8,128)(2,1)S(1)}, u32[]{:S(2)}, u32[]{:S(2)}) collective-permute-start(bf16[2,256,128]{2,1,0:T(8,128)(2,1)S(1)} %get-tuple-element.112), channel_id=1, source_target_pairs={{0,8},{2,10},{4,12},{6,14},{8,0},{10,2},{12,4},{14,6},{1,9},{3,11}... | collective-permute-start | bytes 393224 | tf_op jit(solution)/shard_map/ppermute | solution.py:22
  23.2 3.5 %collective-permute-start.13 = (bf16[2,256,128]{2,1,0:T(8,128)(2,1)S(1)}, bf16[2,256,128]{2,1,0:T(8,128)(2,1)S(1)}, u32[]{:S(2)}, u32[]{:S(2)}) collective-permute-start(bf16[2,256,128]{2,1,0:T(8,128)(2,1)S(1)} %get-tuple-element.120), channel_id=1, source_target_pairs={{0,6},{2,4},{4,2},{6,0},{8,14},{10,12},{12,10},{14,8},{1,7},{3,5},... | collective-permute-start | bytes 393224 | tf_op jit(solution)/shard_map/ppermute | solution.py:22
  27.5 2.3 %collective-permute-done.3.refs_8_ = bf16[2,256,128]{2,1,0:T(8,128)(2,1)S(1)} collective-permute-done((bf16[2,256,128]{2,1,0:T(8,128)(2,1)S(1)}, bf16[2,256,128]{2,1,0:T(8,128)(2,1)S(1)}, u32[]{:S(2)}, u32[]{:S(2)}) %collective-permute-start.3) | collective-permute-done | bytes 131104 | tf_op jit(solution)/shard_map/ppermute | solution.py:22
  29.9 1.6 %collective-permute-done.10.refs_7_ = bf16[2,256,128]{2,1,0:T(8,128)(2,1)S(1)} collective-permute-done((bf16[2,256,128]{2,1,0:T(8,128)(2,1)S(1)}, bf16[2,256,128]{2,1,0:T(8,128)(2,1)S(1)}, u32[]{:S(2)}, u32[]{:S(2)}) %collective-permute-start.10) | collective-permute-done | bytes 131104 | tf_op jit(solution)/shard_map/ppermute | solution.py:22
  32.1 3.8 %collective-permute-start.15 = (bf16[2,256,128]{2,1,0:T(8,128)(2,1)S(1)}, bf16[2,256,128]{2,1,0:T(8,128)(2,1)S(1)}, u32[]{:S(2)}, u32[]{:S(2)}) collective-permute-start(bf16[2,256,128]{2,1,0:T(8,128)(2,1)S(1)} %get-tuple-element.125), channel_id=1, source_target_pairs={{0,10},{2,8},{4,14},{6,12},{8,2},{10,0},{12,6},{14,4},{1,11},{3,9}... | collective-permute-start | bytes 393224 | tf_op jit(solution)/shard_map/ppermute | solution.py:22
  35.9 2.6 %collective-permute-start.16 = (bf16[2,256,128]{2,1,0:T(8,128)(2,1)S(1)}, bf16[2,256,128]{2,1,0:T(8,128)(2,1)S(1)}, u32[]{:S(2)}, u32[]{:S(2)}) collective-permute-start(bf16[2,256,128]{2,1,0:T(8,128)(2,1)S(1)} %get-tuple-element.126), channel_id=1, source_target_pairs={{0,12},{2,14},{4,8},{6,10},{8,4},{10,6},{12,0},{14,2},{1,13},{3,15... | collective-permute-start | bytes 393224 | tf_op jit(solution)/shard_map/ppermute | solution.py:22
  38.5 8.2 %head_first.1 = (f32[2048,128]{1,0:T(8,128)S(1)}, bf16[2048,128]{1,0:T(8,128)(2,1)S(1)}, bf16[2048,128]{1,0:T(8,128)(2,1)S(1)}) custom-call(s32[3]{0:T(128)S(1)} %pad_add_fusion.place, bf16[256,1024]{1,0:T(8,128)(2,1)S(1)} %bitcast.10, bf16[256,1024]{1,0:T(8,128)(2,1)S(1)} %bitcast.12, bf16[256,1024]{1,0:T(8,128)(2,1)S(1)} %bitcast.14, ...), custom_call_target="tpu_custom_call" | custom-call | flops 13421772800 | bytes 2097152 | tf_op jit(solution)/shard_map/head_first/pallas_call | solution.py:332
  46.7 1.3 %collective-permute-start.4 = (bf16[2,256,128]{2,1,0:T(8,128)(2,1)S(1)}, bf16[2,256,128]{2,1,0:T(8,128)(2,1)S(1)}, u32[]{:S(2)}, u32[]{:S(2)}) collective-permute-start(bf16[2,256,128]{2,1,0:T(8,128)(2,1)S(1)} %get-tuple-element.97), channel_id=1, source_target_pairs={{0,14},{2,12},{4,10},{6,8},{8,6},{10,4},{12,2},{14,0},{1,15},{3,13... | collective-permute-start | bytes 393224 | tf_op jit(solution)/shard_map/ppermute | solution.py:22
  48.0 1.9 %collective-permute-done.15.refs_1_ = bf16[2,256,128]{2,1,0:T(8,128)(2,1)S(1)} collective-permute-done((bf16[2,256,128]{2,1,0:T(8,128)(2,1)S(1)}, bf16[2,256,128]{2,1,0:T(8,128)(2,1)S(1)}, u32[]{:S(2)}, u32[]{:S(2)}) %collective-permute-start.15) | collective-permute-done | bytes 131104 | tf_op jit(solution)/shard_map/ppermute | solution.py:22
  49.9 4.0 %head_later.2.before_ref = f32[2048,128]{1,0:T(8,128)S(1)} custom-call(s32[3]{0:T(128)S(1)} %pad_add_fusion.place, f32[2048,128]{1,0:T(8,128)S(1)} %get-tuple-element.121.before_ref, bf16[2048,128]{1,0:T(8,128)(2,1)S(1)} %get-tuple-element.122.key_ref, bf16[2048,128]{1,0:T(8,128)(2,1)S(1)} %get-tuple-element.123.value_ref, ...), custom_call_target="tpu_custom_call" | custom-call | flops 6710886400 | bytes 2097152 | tf_op jit(solution)/shard_map/head_later/pallas_call | solution.py:346
  53.9 1.1 %moved.3.input_ref = bf16[4,256,1024]{2,1,0:T(8,128)(2,1)S(1)} custom-call(s32[3]{0:T(128)S(1)} %pad_add_fusion.place, bf16[8,256,128]{2,1,0:T(8,128)(2,1)S(1)} %get-tuple-element.87.keep, bf16[8,256,128]{2,1,0:T(8,128)(2,1)S(1)} %collective-permute-done.1.keep_other, bf16[8,256,128]{2,1,0:T(8,128)(2,1)S(1)} %collective-permute-done.5.received, ...), custom_call_target="tpu_custom_call" | custom-call | tf_op jit(solution)/shard_map/moved/pallas_call | solution.py:111
  55.0 3.6 %head_later.3 = (bf16[512,128]{1,0:T(8,128)(2,1)S(1)}, bf16[512,128]{1,0:T(8,128)(2,1)S(1)}, bf16[512,128]{1,0:T(8,128)(2,1)S(1)}, bf16[512,128]{1,0:T(8,128)(2,1)S(1)}) custom-call(s32[3]{0:T(128)S(1)} %pad_add_fusion.place, f32[2048,128]{1,0:T(8,128)S(1)} %head_later.2.before_ref, bf16[2048,128]{1,0:T(8,128)(2,1)S(1)} %get-tuple-element.122.key_ref, ...), custom_call_target="tpu_custom_call" | custom-call | flops 6710886400 | bytes 2097152 | tf_op jit(solution)/shard_map/head_later/pallas_call | solution.py:346
  58.7 3.6 %collective-permute-start.19 = (bf16[512,128]{1,0:T(8,128)(2,1)S(1)}, bf16[512,128]{1,0:T(8,128)(2,1)S(1)}, u32[]{:S(2)}, u32[]{:S(2)}) collective-permute-start(bf16[512,128]{1,0:T(8,128)(2,1)S(1)} %get-tuple-element.130), channel_id=1, source_target_pairs={{0,4},{1,0},{2,6},{3,2},{4,5},{5,1},{6,7},{7,3},{8,12},{9,8},{10,1... | collective-permute-start | bytes 393224 | tf_op jit(solution)/shard_map/ppermute | solution.py:564
  63.0 4.8 %collective-permute-start.18 = (bf16[512,128]{1,0:T(8,128)(2,1)S(1)}, bf16[512,128]{1,0:T(8,128)(2,1)S(1)}, u32[]{:S(2)}, u32[]{:S(2)}) collective-permute-start(bf16[512,128]{1,0:T(8,128)(2,1)S(1)} %get-tuple-element.129), channel_id=1, source_target_pairs={{0,12},{1,8},{2,14},{3,10},{4,13},{5,9},{6,15},{7,11},{8,4},{9,0},... | collective-permute-start | bytes 393224 | tf_op jit(solution)/shard_map/ppermute | solution.py:564
  67.8 1.1 %collective-permute-start.21 = (bf16[512,128]{1,0:T(8,128)(2,1)S(1)}, bf16[512,128]{1,0:T(8,128)(2,1)S(1)}, u32[]{:S(2)}, u32[]{:S(2)}) collective-permute-start(bf16[512,128]{1,0:T(8,128)(2,1)S(1)} %collective-permute-done.19.refs_2_), channel_id=1, source_target_pairs={{0,2},{2,0},{4,6},{6,4},{8,10},{10,8},{12,14},{14,12},{1,3},{3,1},... | collective-permute-start | bytes 393224 | tf_op jit(solution)/shard_map/ppermute | solution.py:22
  69.8 4.6 %collective-permute-done.17.refs_0_ = bf16[512,128]{1,0:T(8,128)(2,1)S(1)} collective-permute-done((bf16[512,128]{1,0:T(8,128)(2,1)S(1)}, bf16[512,128]{1,0:T(8,128)(2,1)S(1)}, u32[]{:S(2)}, u32[]{:S(2)}) %collective-permute-start.17) | collective-permute-done | bytes 131104 | tf_op jit(solution)/shard_map/ppermute | solution.py:564
  74.4 1.4 %collective-permute-done.18.refs_1_ = bf16[512,128]{1,0:T(8,128)(2,1)S(1)} collective-permute-done((bf16[512,128]{1,0:T(8,128)(2,1)S(1)}, bf16[512,128]{1,0:T(8,128)(2,1)S(1)}, u32[]{:S(2)}, u32[]{:S(2)}) %collective-permute-start.18) | collective-permute-done | bytes 131104 | tf_op jit(solution)/shard_map/ppermute | solution.py:564
  75.8 1.1 %weight_parts.4 = (bf16[256,256]{1,0:T(8,128)(2,1)S(1)}, bf16[256,256]{1,0:T(8,128)(2,1)S(1)}) custom-call(s32[3]{0:T(128)S(1)} %pad_add_fusion.place, bf16[4,256,1024]{2,1,0:T(8,128)(2,1)S(1)} %moved.3.input_ref, bf16[512,128]{1,0:T(8,128)(2,1)S(1)} %collective-permute-done.17.refs_0_, bf16[512,128]{1,0:T(8,128)(2,1)S(1)} %collective-permute-done.18.refs_1_, ...), custom_call_target="tpu_custom_call" | custom-call | flops 268435456 | bytes 1572864 | tf_op jit(solution)/shard_map/weight_parts/pallas_call | solution.py:382
  77.2 1.8 %collective-permute-start.23 = (bf16[512,128]{1,0:T(8,128)(2,1)S(1)}, bf16[512,128]{1,0:T(8,128)(2,1)S(1)}, u32[]{:S(2)}, u32[]{:S(2)}) collective-permute-start(bf16[512,128]{1,0:T(8,128)(2,1)S(1)} %collective-permute-done.17.refs_0_), channel_id=1, source_target_pairs={{0,2},{2,0},{4,6},{6,4},{8,10},{10,8},{12,14},{14,12},{1,3},{3,1},... | collective-permute-start | bytes 393224 | tf_op jit(solution)/shard_map/ppermute | solution.py:22
  79.2 2.5 %collective-permute-start.30 = (bf16[256,256]{1,0:T(8,128)(2,1)S(1)}, bf16[256,256]{1,0:T(8,128)(2,1)S(1)}, u32[]{:S(2)}, u32[]{:S(2)}) collective-permute-start(bf16[256,256]{1,0:T(8,128)(2,1)S(1)} %get-tuple-element.161), channel_id=1, source_target_pairs={{0,8},{2,10},{4,12},{6,14},{8,0},{10,2},{12,4},{14,6},{1,9},{3,11}... | collective-permute-start | bytes 393224 | tf_op jit(solution)/shard_map/ppermute | solution.py:22
  82.8 1.7 %collective-permute-start.31 = (bf16[256,256]{1,0:T(8,128)(2,1)S(1)}, bf16[256,256]{1,0:T(8,128)(2,1)S(1)}, u32[]{:S(2)}, u32[]{:S(2)}) collective-permute-start(bf16[256,256]{1,0:T(8,128)(2,1)S(1)} %get-tuple-element.162), channel_id=1, source_target_pairs={{0,4},{2,6},{4,0},{6,2},{8,12},{10,14},{12,8},{14,10},{1,5},{3,7},... | collective-permute-start | bytes 393224 | tf_op jit(solution)/shard_map/ppermute | solution.py:22
  85.4 1.1 %weight_parts.5 = (bf16[256,256]{1,0:T(8,128)(2,1)S(1)}, bf16[256,256]{1,0:T(8,128)(2,1)S(1)}) custom-call(s32[3]{0:T(128)S(1)} %pad_add_fusion.place, bf16[4,256,1024]{2,1,0:T(8,128)(2,1)S(1)} %moved.3.input_ref, bf16[512,128]{1,0:T(8,128)(2,1)S(1)} %collective-permute-done.23.refs_0_, bf16[512,128]{1,0:T(8,128)(2,1)S(1)} %collective-permute-done.24.refs_1_, ...), custom_call_target="tpu_custom_call" | custom-call | flops 268435456 | bytes 1572864 | tf_op jit(solution)/shard_map/weight_parts/pallas_call | solution.py:382
  86.5 2.5 %collective-permute-start.26 = (bf16[256,256]{1,0:T(8,128)(2,1)S(1)}, bf16[256,256]{1,0:T(8,128)(2,1)S(1)}, u32[]{:S(2)}, u32[]{:S(2)}) collective-permute-start(bf16[256,256]{1,0:T(8,128)(2,1)S(1)} %get-tuple-element.150), channel_id=1, source_target_pairs={{0,12},{2,14},{4,8},{6,10},{8,4},{10,6},{12,0},{14,2},{1,13},{3,15... | collective-permute-start | bytes 393224 | tf_op jit(solution)/shard_map/ppermute | solution.py:22
  89.0 2.4 %collective-permute-start.27 = (bf16[256,256]{1,0:T(8,128)(2,1)S(1)}, bf16[256,256]{1,0:T(8,128)(2,1)S(1)}, u32[]{:S(2)}, u32[]{:S(2)}) collective-permute-start(bf16[256,256]{1,0:T(8,128)(2,1)S(1)} %get-tuple-element.151), channel_id=1, source_target_pairs={{0,8},{2,10},{4,12},{6,14},{8,0},{10,2},{12,4},{14,6},{1,9},{3,11}... | collective-permute-start | bytes 393224 | tf_op jit(solution)/shard_map/ppermute | solution.py:22
  93.3 1.5 %collective-permute-done.26.refs_1_ = bf16[256,256]{1,0:T(8,128)(2,1)S(1)} collective-permute-done((bf16[256,256]{1,0:T(8,128)(2,1)S(1)}, bf16[256,256]{1,0:T(8,128)(2,1)S(1)}, u32[]{:S(2)}, u32[]{:S(2)}) %collective-permute-start.26) | collective-permute-done | bytes 131104 | tf_op jit(solution)/shard_map/ppermute | solution.py:22
  94.8 6.7 %collective-permute-done.27.refs_2_ = bf16[256,256]{1,0:T(8,128)(2,1)S(1)} collective-permute-done((bf16[256,256]{1,0:T(8,128)(2,1)S(1)}, bf16[256,256]{1,0:T(8,128)(2,1)S(1)}, u32[]{:S(2)}, u32[]{:S(2)}) %collective-permute-start.27) | collective-permute-done | bytes 131104 | tf_op jit(solution)/shard_map/ppermute | solution.py:22
  102.2 1.2 %placed.2.refs_2_ = f32[128,1024]{1,0:T(8,128)} custom-call(s32[3]{0:T(128)S(1)} %pad_add_fusion.place, f32[128,256]{1,0:T(8,128)S(1)} %get-tuple-element.163.refs_0_, f32[128,256]{1,0:T(8,128)S(1)} %collective-permute-done.32.refs_1_), custom_call_target="tpu_custom_call" | custom-call | tf_op jit(solution)/shard_map/placed/pallas_call | solution.py:444
  103.5 1.2 %placed.3 = f32[128,1024]{1,0:T(8,128)} custom-call(s32[3]{0:T(128)S(1)} %pad_add_fusion.place, f32[128,256]{1,0:T(8,128)S(1)} %get-tuple-element.153.refs_0_, f32[128,256]{1,0:T(8,128)S(1)} %collective-permute-done.29.refs_1_, f32[128,1024]{1,0:T(8,128)} %placed.2.refs_2_), custom_call_target="tpu_custom_call", output_to_operand_aliasing={{}: (3, {})} | custom-call | tf_op jit(solution)/shard_map/placed/pallas_call | solution.py:444
  (68 shorter events, 13.5 us)
Async XLA Ops:
  3.1 12.7 %collective-permute-start.2 = (bf16[2,256,128]{2,1,0:T(8,128)(2,1)S(1)}, bf16[2,256,128]{2,1,0:T(8,128)(2,1)S(1)}, u32[]{:S(2)}, u32[]{:S(2)}) collective-permute-start(bf16[2,256,128]{2,1,0:T(8,128)(2,1)S(1)} %get-tuple-element.88), channel_id=1, source_target_pairs={{0,14},{2,12},{4,10},{6,8},{8,6},{10,4},{12,2},{14,0},{1,15},{3,13... | collective-permute-start | bytes 393224 | tf_op jit(solution)/shard_map/ppermute | solution.py:22
  9.1 11.9 %collective-permute-start = (bf16[2,256,128]{2,1,0:T(8,128)(2,1)S(1)}, bf16[2,256,128]{2,1,0:T(8,128)(2,1)S(1)}, u32[]{:S(2)}, u32[]{:S(2)}) collective-permute-start(bf16[2,256,128]{2,1,0:T(8,128)(2,1)S(1)} %get-tuple-element.85), channel_id=1, source_target_pairs={{0,2},{2,0},{4,6},{6,4},{8,10},{10,8},{12,14},{14,12},{1,3},{3,1},... | collective-permute-start | bytes 393224 | tf_op jit(solution)/shard_map/ppermute | solution.py:22
  9.6 11.4 %collective-permute-start.9 = (bf16[2,256,128]{2,1,0:T(8,128)(2,1)S(1)}, bf16[2,256,128]{2,1,0:T(8,128)(2,1)S(1)}, u32[]{:S(2)}, u32[]{:S(2)}) collective-permute-start(bf16[2,256,128]{2,1,0:T(8,128)(2,1)S(1)} %get-tuple-element.110), channel_id=1, source_target_pairs={{0,12},{2,14},{4,8},{6,10},{8,4},{10,6},{12,0},{14,2},{1,13},{3,15... | collective-permute-start | bytes 393224 | tf_op jit(solution)/shard_map/ppermute | solution.py:22
  9.8 13.4 %collective-permute-start.7 = (bf16[2,256,128]{2,1,0:T(8,128)(2,1)S(1)}, bf16[2,256,128]{2,1,0:T(8,128)(2,1)S(1)}, u32[]{:S(2)}, u32[]{:S(2)}) collective-permute-start(bf16[2,256,128]{2,1,0:T(8,128)(2,1)S(1)} %get-tuple-element.104), channel_id=1, source_target_pairs={{0,4},{2,6},{4,0},{6,2},{8,12},{10,14},{12,8},{14,10},{1,5},{3,7},... | collective-permute-start | bytes 393224 | tf_op jit(solution)/shard_map/ppermute | solution.py:22
  9.8 13.4 %collective-permute-start.8 = (bf16[2,256,128]{2,1,0:T(8,128)(2,1)S(1)}, bf16[2,256,128]{2,1,0:T(8,128)(2,1)S(1)}, u32[]{:S(2)}, u32[]{:S(2)}) collective-permute-start(bf16[2,256,128]{2,1,0:T(8,128)(2,1)S(1)} %get-tuple-element.107), channel_id=1, source_target_pairs={{0,6},{2,4},{4,2},{6,0},{8,14},{10,12},{12,10},{14,8},{1,7},{3,5},... | collective-permute-start | bytes 393224 | tf_op jit(solution)/shard_map/ppermute | solution.py:22
  15.8 14.1 %collective-permute-start.3 = (bf16[2,256,128]{2,1,0:T(8,128)(2,1)S(1)}, bf16[2,256,128]{2,1,0:T(8,128)(2,1)S(1)}, u32[]{:S(2)}, u32[]{:S(2)}) collective-permute-start(bf16[2,256,128]{2,1,0:T(8,128)(2,1)S(1)} %get-tuple-element.90), channel_id=1, source_target_pairs={{0,10},{2,8},{4,14},{6,12},{8,2},{10,0},{12,6},{14,4},{1,11},{3,9}... | collective-permute-start | bytes 393224 | tf_op jit(solution)/shard_map/ppermute | solution.py:22
  21.0 10.5 %collective-permute-start.10 = (bf16[2,256,128]{2,1,0:T(8,128)(2,1)S(1)}, bf16[2,256,128]{2,1,0:T(8,128)(2,1)S(1)}, u32[]{:S(2)}, u32[]{:S(2)}) collective-permute-start(bf16[2,256,128]{2,1,0:T(8,128)(2,1)S(1)} %get-tuple-element.112), channel_id=1, source_target_pairs={{0,8},{2,10},{4,12},{6,14},{8,0},{10,2},{12,4},{14,6},{1,9},{3,11}... | collective-permute-start | bytes 393224 | tf_op jit(solution)/shard_map/ppermute | solution.py:22
  23.2 8.9 %collective-permute-start.11 = (bf16[2,256,128]{2,1,0:T(8,128)(2,1)S(1)}, bf16[2,256,128]{2,1,0:T(8,128)(2,1)S(1)}, u32[]{:S(2)}, u32[]{:S(2)}) collective-permute-start(bf16[2,256,128]{2,1,0:T(8,128)(2,1)S(1)} %get-tuple-element.118), channel_id=1, source_target_pairs={{0,2},{2,0},{4,6},{6,4},{8,10},{10,8},{12,14},{14,12},{1,3},{3,1},... | collective-permute-start | bytes 393224 | tf_op jit(solution)/shard_map/ppermute | solution.py:22
  23.2 8.9 %collective-permute-start.12 = (bf16[2,256,128]{2,1,0:T(8,128)(2,1)S(1)}, bf16[2,256,128]{2,1,0:T(8,128)(2,1)S(1)}, u32[]{:S(2)}, u32[]{:S(2)}) collective-permute-start(bf16[2,256,128]{2,1,0:T(8,128)(2,1)S(1)} %get-tuple-element.119), channel_id=1, source_target_pairs={{0,4},{2,6},{4,0},{6,2},{8,12},{10,14},{12,8},{14,10},{1,5},{3,7},... | collective-permute-start | bytes 393224 | tf_op jit(solution)/shard_map/ppermute | solution.py:22
  23.2 12.7 %collective-permute-start.13 = (bf16[2,256,128]{2,1,0:T(8,128)(2,1)S(1)}, bf16[2,256,128]{2,1,0:T(8,128)(2,1)S(1)}, u32[]{:S(2)}, u32[]{:S(2)}) collective-permute-start(bf16[2,256,128]{2,1,0:T(8,128)(2,1)S(1)} %get-tuple-element.120), channel_id=1, source_target_pairs={{0,6},{2,4},{4,2},{6,0},{8,14},{10,12},{12,10},{14,8},{1,7},{3,5},... | collective-permute-start | bytes 393224 | tf_op jit(solution)/shard_map/ppermute | solution.py:22
  29.9 16.8 %collective-permute-start.1 = (bf16[8,256,128]{2,1,0:T(8,128)(2,1)S(1)}, bf16[8,256,128]{2,1,0:T(8,128)(2,1)S(1)}, u32[]{:S(2)}, u32[]{:S(2)}) collective-permute-start(bf16[8,256,128]{2,1,0:T(8,128)(2,1)S(1)} %get-tuple-element.87.keep), channel_id=1, source_target_pairs={{0,1},{1,0},{2,3},{3,2},{4,5},{5,4},{6,7},{7,6},{8,9},{9,8},{10,11... | collective-permute-start | bytes 1572872 | tf_op jit(solution)/shard_map/ppermute | solution.py:22
  31.5 16.5 %collective-permute-start.5 = (bf16[8,256,128]{2,1,0:T(8,128)(2,1)S(1)}, bf16[8,256,128]{2,1,0:T(8,128)(2,1)S(1)}, u32[]{:S(2)}, u32[]{:S(2)}) collective-permute-start(bf16[8,256,128]{2,1,0:T(8,128)(2,1)S(1)} %get-tuple-element.99), channel_id=1, source_target_pairs={{0,2},{2,0},{4,6},{6,4},{8,10},{10,8},{12,14},{14,12},{1,3},{3,1},... | collective-permute-start | bytes 1572872 | tf_op jit(solution)/shard_map/ppermute | solution.py:22
  32.1 15.9 %collective-permute-start.14 = (bf16[2,256,128]{2,1,0:T(8,128)(2,1)S(1)}, bf16[2,256,128]{2,1,0:T(8,128)(2,1)S(1)}, u32[]{:S(2)}, u32[]{:S(2)}) collective-permute-start(bf16[2,256,128]{2,1,0:T(8,128)(2,1)S(1)} %get-tuple-element.124), channel_id=1, source_target_pairs={{0,8},{2,10},{4,12},{6,14},{8,0},{10,2},{12,4},{14,6},{1,9},{3,11}... | collective-permute-start | bytes 393224 | tf_op jit(solution)/shard_map/ppermute | solution.py:22
  32.1 17.8 %collective-permute-start.15 = (bf16[2,256,128]{2,1,0:T(8,128)(2,1)S(1)}, bf16[2,256,128]{2,1,0:T(8,128)(2,1)S(1)}, u32[]{:S(2)}, u32[]{:S(2)}) collective-permute-start(bf16[2,256,128]{2,1,0:T(8,128)(2,1)S(1)} %get-tuple-element.125), channel_id=1, source_target_pairs={{0,10},{2,8},{4,14},{6,12},{8,2},{10,0},{12,6},{14,4},{1,11},{3,9}... | collective-permute-start | bytes 393224 | tf_op jit(solution)/shard_map/ppermute | solution.py:22
  35.9 19.1 %collective-permute-start.16 = (bf16[2,256,128]{2,1,0:T(8,128)(2,1)S(1)}, bf16[2,256,128]{2,1,0:T(8,128)(2,1)S(1)}, u32[]{:S(2)}, u32[]{:S(2)}) collective-permute-start(bf16[2,256,128]{2,1,0:T(8,128)(2,1)S(1)} %get-tuple-element.126), channel_id=1, source_target_pairs={{0,12},{2,14},{4,8},{6,10},{8,4},{10,6},{12,0},{14,2},{1,13},{3,15... | collective-permute-start | bytes 393224 | tf_op jit(solution)/shard_map/ppermute | solution.py:22
  46.7 8.3 %collective-permute-start.4 = (bf16[2,256,128]{2,1,0:T(8,128)(2,1)S(1)}, bf16[2,256,128]{2,1,0:T(8,128)(2,1)S(1)}, u32[]{:S(2)}, u32[]{:S(2)}) collective-permute-start(bf16[2,256,128]{2,1,0:T(8,128)(2,1)S(1)} %get-tuple-element.97), channel_id=1, source_target_pairs={{0,14},{2,12},{4,10},{6,8},{8,6},{10,4},{12,2},{14,0},{1,15},{3,13... | collective-permute-start | bytes 393224 | tf_op jit(solution)/shard_map/ppermute | solution.py:22
  48.0 5.9 %collective-permute-start.6 = (bf16[8,256,128]{2,1,0:T(8,128)(2,1)S(1)}, bf16[8,256,128]{2,1,0:T(8,128)(2,1)S(1)}, u32[]{:S(2)}, u32[]{:S(2)}) collective-permute-start(bf16[8,256,128]{2,1,0:T(8,128)(2,1)S(1)} %collective-permute-done.5.received), channel_id=1, source_target_pairs={{0,1},{1,0},{2,3},{3,2},{4,5},{5,4},{6,7},{7,6},{8,9},{9,8},{10,11... | collective-permute-start | bytes 1572872 | tf_op jit(solution)/shard_map/ppermute | solution.py:22
  58.7 9.1 %collective-permute-start.19 = (bf16[512,128]{1,0:T(8,128)(2,1)S(1)}, bf16[512,128]{1,0:T(8,128)(2,1)S(1)}, u32[]{:S(2)}, u32[]{:S(2)}) collective-permute-start(bf16[512,128]{1,0:T(8,128)(2,1)S(1)} %get-tuple-element.130), channel_id=1, source_target_pairs={{0,4},{1,0},{2,6},{3,2},{4,5},{5,1},{6,7},{7,3},{8,12},{9,8},{10,1... | collective-permute-start | bytes 393224 | tf_op jit(solution)/shard_map/ppermute | solution.py:564
  62.2 6.6 %collective-permute-start.20 = (bf16[512,128]{1,0:T(8,128)(2,1)S(1)}, bf16[512,128]{1,0:T(8,128)(2,1)S(1)}, u32[]{:S(2)}, u32[]{:S(2)}) collective-permute-start(bf16[512,128]{1,0:T(8,128)(2,1)S(1)} %get-tuple-element.131), channel_id=1, source_target_pairs={{0,0},{1,4},{2,2},{3,6},{4,1},{5,5},{6,3},{7,7},{8,8},{9,12},{10,1... | collective-permute-start | bytes 393224 | tf_op jit(solution)/shard_map/ppermute | solution.py:564
  62.9 11.5 %collective-permute-start.17 = (bf16[512,128]{1,0:T(8,128)(2,1)S(1)}, bf16[512,128]{1,0:T(8,128)(2,1)S(1)}, u32[]{:S(2)}, u32[]{:S(2)}) collective-permute-start(bf16[512,128]{1,0:T(8,128)(2,1)S(1)} %get-tuple-element.128), channel_id=1, source_target_pairs={{0,8},{1,12},{2,10},{3,14},{4,9},{5,13},{6,11},{7,15},{8,0},{9,4},... | collective-permute-start | bytes 393224 | tf_op jit(solution)/shard_map/ppermute | solution.py:564
  63.0 12.9 %collective-permute-start.18 = (bf16[512,128]{1,0:T(8,128)(2,1)S(1)}, bf16[512,128]{1,0:T(8,128)(2,1)S(1)}, u32[]{:S(2)}, u32[]{:S(2)}) collective-permute-start(bf16[512,128]{1,0:T(8,128)(2,1)S(1)} %get-tuple-element.129), channel_id=1, source_target_pairs={{0,12},{1,8},{2,14},{3,10},{4,13},{5,9},{6,15},{7,11},{8,4},{9,0},... | collective-permute-start | bytes 393224 | tf_op jit(solution)/shard_map/ppermute | solution.py:564
  67.8 9.4 %collective-permute-start.21 = (bf16[512,128]{1,0:T(8,128)(2,1)S(1)}, bf16[512,128]{1,0:T(8,128)(2,1)S(1)}, u32[]{:S(2)}, u32[]{:S(2)}) collective-permute-start(bf16[512,128]{1,0:T(8,128)(2,1)S(1)} %collective-permute-done.19.refs_2_), channel_id=1, source_target_pairs={{0,2},{2,0},{4,6},{6,4},{8,10},{10,8},{12,14},{14,12},{1,3},{3,1},... | collective-permute-start | bytes 393224 | tf_op jit(solution)/shard_map/ppermute | solution.py:22
  68.8 8.4 %collective-permute-start.22 = (bf16[512,128]{1,0:T(8,128)(2,1)S(1)}, bf16[512,128]{1,0:T(8,128)(2,1)S(1)}, u32[]{:S(2)}, u32[]{:S(2)}) collective-permute-start(bf16[512,128]{1,0:T(8,128)(2,1)S(1)} %collective-permute-done.20.refs_3_), channel_id=1, source_target_pairs={{0,2},{2,0},{4,6},{6,4},{8,10},{10,8},{12,14},{14,12},{1,3},{3,1},... | collective-permute-start | bytes 393224 | tf_op jit(solution)/shard_map/ppermute | solution.py:22
  76.9 8.3 %collective-permute-start.25 = (bf16[256,256]{1,0:T(8,128)(2,1)S(1)}, bf16[256,256]{1,0:T(8,128)(2,1)S(1)}, u32[]{:S(2)}, u32[]{:S(2)}) collective-permute-start(bf16[256,256]{1,0:T(8,128)(2,1)S(1)} %get-tuple-element.138), channel_id=1, source_target_pairs={{0,12},{2,14},{4,8},{6,10},{8,4},{10,6},{12,0},{14,2},{1,13},{3,15... | collective-permute-start | bytes 393224 | tf_op jit(solution)/shard_map/ppermute | solution.py:22
  77.2 8.0 %collective-permute-start.23 = (bf16[512,128]{1,0:T(8,128)(2,1)S(1)}, bf16[512,128]{1,0:T(8,128)(2,1)S(1)}, u32[]{:S(2)}, u32[]{:S(2)}) collective-permute-start(bf16[512,128]{1,0:T(8,128)(2,1)S(1)} %collective-permute-done.17.refs_0_), channel_id=1, source_target_pairs={{0,2},{2,0},{4,6},{6,4},{8,10},{10,8},{12,14},{14,12},{1,3},{3,1},... | collective-permute-start | bytes 393224 | tf_op jit(solution)/shard_map/ppermute | solution.py:22
  79.0 6.3 %collective-permute-start.24 = (bf16[512,128]{1,0:T(8,128)(2,1)S(1)}, bf16[512,128]{1,0:T(8,128)(2,1)S(1)}, u32[]{:S(2)}, u32[]{:S(2)}) collective-permute-start(bf16[512,128]{1,0:T(8,128)(2,1)S(1)} %collective-permute-done.18.refs_1_), channel_id=1, source_target_pairs={{0,2},{2,0},{4,6},{6,4},{8,10},{10,8},{12,14},{14,12},{1,3},{3,1},... | collective-permute-start | bytes 393224 | tf_op jit(solution)/shard_map/ppermute | solution.py:22
  79.2 13.3 %collective-permute-start.30 = (bf16[256,256]{1,0:T(8,128)(2,1)S(1)}, bf16[256,256]{1,0:T(8,128)(2,1)S(1)}, u32[]{:S(2)}, u32[]{:S(2)}) collective-permute-start(bf16[256,256]{1,0:T(8,128)(2,1)S(1)} %get-tuple-element.161), channel_id=1, source_target_pairs={{0,8},{2,10},{4,12},{6,14},{8,0},{10,2},{12,4},{14,6},{1,9},{3,11}... | collective-permute-start | bytes 393224 | tf_op jit(solution)/shard_map/ppermute | solution.py:22
  82.8 9.7 %collective-permute-start.31 = (bf16[256,256]{1,0:T(8,128)(2,1)S(1)}, bf16[256,256]{1,0:T(8,128)(2,1)S(1)}, u32[]{:S(2)}, u32[]{:S(2)}) collective-permute-start(bf16[256,256]{1,0:T(8,128)(2,1)S(1)} %get-tuple-element.162), channel_id=1, source_target_pairs={{0,4},{2,6},{4,0},{6,2},{8,12},{10,14},{12,8},{14,10},{1,5},{3,7},... | collective-permute-start | bytes 393224 | tf_op jit(solution)/shard_map/ppermute | solution.py:22
  86.5 8.3 %collective-permute-start.26 = (bf16[256,256]{1,0:T(8,128)(2,1)S(1)}, bf16[256,256]{1,0:T(8,128)(2,1)S(1)}, u32[]{:S(2)}, u32[]{:S(2)}) collective-permute-start(bf16[256,256]{1,0:T(8,128)(2,1)S(1)} %get-tuple-element.150), channel_id=1, source_target_pairs={{0,12},{2,14},{4,8},{6,10},{8,4},{10,6},{12,0},{14,2},{1,13},{3,15... | collective-permute-start | bytes 393224 | tf_op jit(solution)/shard_map/ppermute | solution.py:22
  89.0 12.5 %collective-permute-start.27 = (bf16[256,256]{1,0:T(8,128)(2,1)S(1)}, bf16[256,256]{1,0:T(8,128)(2,1)S(1)}, u32[]{:S(2)}, u32[]{:S(2)}) collective-permute-start(bf16[256,256]{1,0:T(8,128)(2,1)S(1)} %get-tuple-element.151), channel_id=1, source_target_pairs={{0,8},{2,10},{4,12},{6,14},{8,0},{10,2},{12,4},{14,6},{1,9},{3,11}... | collective-permute-start | bytes 393224 | tf_op jit(solution)/shard_map/ppermute | solution.py:22
  92.5 9.0 %collective-permute-start.28 = (bf16[256,256]{1,0:T(8,128)(2,1)S(1)}, bf16[256,256]{1,0:T(8,128)(2,1)S(1)}, u32[]{:S(2)}, u32[]{:S(2)}) collective-permute-start(bf16[256,256]{1,0:T(8,128)(2,1)S(1)} %get-tuple-element.152), channel_id=1, source_target_pairs={{0,4},{2,6},{4,0},{6,2},{8,12},{10,14},{12,8},{14,10},{1,5},{3,7},... | collective-permute-start | bytes 393224 | tf_op jit(solution)/shard_map/ppermute | solution.py:22
  93.2 9.0 %collective-permute-start.32 = (f32[128,256]{1,0:T(8,128)S(1)}, f32[128,256]{1,0:T(8,128)S(1)}, u32[]{:S(2)}, u32[]{:S(2)}) collective-permute-start(f32[128,256]{1,0:T(8,128)S(1)} %get-tuple-element.164), channel_id=1, source_target_pairs={{0,1},{1,0},{2,3},{3,2},{4,5},{5,4},{6,7},{7,6},{8,9},{9,8},{10,11... | collective-permute-start | bytes 393224 | tf_op jit(solution)/shard_map/ppermute | solution.py:22
  (10 other events, 126.5 us)
